TPU v7x, 32 devices: a whole 2x2x4 slice. The times are simulated.
32 devices in a mesh: groups: 2 (over x), space: 16 (over z, y, core).
Axes of the slice: x: 2, y: 2, z: 4, core: 2. Of those that a mesh axis runs over, the one named last changes fastest.
Arguments:
- grid_inputs: bfloat16 [227, 65536], P(None, ('groups', 'space')), parts along dimension 1, may hold values from -6 to 6
- grid_count: int32 [16], P('space'), may hold values from 1024 to 2048, as said below
- embed_in: bfloat16 [227, 512], replicated, may hold values from -0.375 to 0.375
- embed_out: bfloat16 [512, 512], replicated, may hold values from -0.25 to 0.25
- grid_gain: float32 [512], replicated, may hold values from 0.25 to 1.75
- g2m_values: bfloat16 [1024, 128, 128], P('space'), may hold values from -0.125 to 0.125
- g2m_src: int32 [1024], P('space'), may hold values from 0 to 15, as said below
- g2m_dst: int32 [1024], P('space'), may hold values from 0 to 63, as said below
- mesh_place: int32 [64], replicated, may hold values from 0 to 63, as said below
- node_in: bfloat16 [512, 512], replicated, may hold values from -0.25 to 0.25
- node_out: bfloat16 [512, 512], replicated, may hold values from -0.25 to 0.25
- node_gain: float32 [512], replicated, may hold values from 0.25 to 1.75
- recv_blocks: int32 [16, 4], P('space'), may hold values from 0 to 3, as said below
- mesh_values: bfloat16 [192, 128, 128], P('space'), may hold values from -0.3125 to 0.3125
- mesh_dst: int32 [192], P('space'), may hold values from 0 to 3, as said below
- mesh_src: int32 [192], P('space'), may hold values from 0 to 9, as said below
- proc_in: bfloat16 [512, 512], replicated, may hold values from -0.25 to 0.25
- proc_out: bfloat16 [512, 512], replicated, may hold values from -0.25 to 0.25
- proc_gain: float32 [512], replicated, may hold values from 0.25 to 1.75
Outputs:
- encoded: bfloat16 [16384, 512], P(('groups', 'space')), parts along dimension 0
- processed: bfloat16 [16384, 512], P(('groups', 'space')), parts along dimension 0
There are 2 independent parts, one for each index of `groups`. A program takes and returns all parts, laid end to end along the dimension named above; an argument that names none is the same for every part. Nothing has to cross between parts.
Inputs may be any that keep to these rules, and one draw needn't show every extreme that they name: `grid_count`: live grid nodes of each latitude slab; a slab's rows from this count on are padding; some slab is full and some holds exactly 1024. `g2m_src`: each of a slab's 16 grid blocks is the source of exactly 4 of the slab's edge blocks. `g2m_dst`: of one slab's edge blocks at most 4 have targets held by any one partition (as mesh_place assigns them), and in every slab some partition holds exactly 4 of them. A permutation: mesh block g is block mesh_place[g] % 4 of partition mesh_place[g] // 4. `recv_blocks`: row p: the first 2 entries are distinct blocks of partition p - 1, the last 2 distinct blocks of partition p + 1 (partitions counted cyclically). `mesh_dst`: every block of a partition is the target of some of its edge blocks. `mesh_src`: code side * 4 + index: side 0 reads slot index of the lower list of recv_blocks, side 1 the partition's own block index, side 2 slot index of the upper list; slots lie below 2 and every slot of both lists is read by some edge block of the partition.
All inputs are finite; a program needn't handle non-finite values.
Results may differ from a plain program's by a relative error of at most 0.013.
Values may be sent and summed in bfloat16 or wider, within the bound.
No kernel may reach another device: no remote copies, remote signals or barrier semaphores. Data moves between devices by JAX's collectives and lax.ppermute only.
A program may use at most 128 MiB of HBM per device.

v0:
```python
import jax
import jax.numpy as jnp
from jax import lax
from jax.sharding import PartitionSpec as P

EPSILON = 1e-05


def extended(cells, sides, width):
    for axis, dim in sides:
        count = lax.axis_size(axis)
        head = lax.slice_in_dim(cells, 0, width, axis=dim)
        tail = lax.slice_in_dim(cells, cells.shape[dim] - width, cells.shape[dim], axis=dim)
        cells = jnp.concatenate(
            [
                lax.ppermute(tail, axis, [(i, (i + 1) % count) for i in range(count)]),
                cells,
                lax.ppermute(head, axis, [((i + 1) % count, i) for i in range(count)]),
            ],
            axis=dim,
        )
    return cells


def normalize(values):
    average = jnp.mean(values, axis=-1, keepdims=True)
    centred = values - average
    variance = jnp.mean(centred * centred, axis=-1, keepdims=True)
    return centred * lax.rsqrt(variance + EPSILON)


def node_update(summed, weight_in, weight_out, gain):
    hidden = jax.nn.silu(
        jnp.dot(summed.astype(jnp.bfloat16), weight_in, preferred_element_type=jnp.float32)
    ).astype(jnp.bfloat16)
    return (
        summed + gain * normalize(jnp.dot(hidden, weight_out, preferred_element_type=jnp.float32))
    ).astype(jnp.bfloat16)


def lookup(table, wanted):
    matches = wanted[:, None] == jnp.arange(table.shape[0], dtype=jnp.int32)[None, :]
    return jnp.sum(jnp.where(matches, table[None, :], 0), axis=1)


def block_sums(labels, blocks, count):
    selector = (labels[None, :] == jnp.arange(count, dtype=jnp.int32)[:, None]).astype(jnp.bfloat16)
    flattened = blocks.reshape(blocks.shape[0], blocks.shape[1] * blocks.shape[2])
    summed = jnp.dot(selector, flattened, preferred_element_type=jnp.float32)
    return summed.reshape(count * blocks.shape[1], blocks.shape[2])


def block_product(values, sources):
    return jnp.einsum("eij,ejd->eid", values, sources, preferred_element_type=jnp.float32).astype(
        jnp.bfloat16
    )


def shards(
    grid_inputs,
    grid_count,
    embed_in,
    embed_out,
    grid_gain,
    g2m_values,
    g2m_src,
    g2m_dst,
    mesh_place,
    node_in,
    node_out,
    node_gain,
    recv_blocks,
    mesh_values,
    mesh_dst,
    mesh_src,
    proc_in,
    proc_out,
    proc_gain,
):
    partitions = lax.axis_size("space")
    slab_rows = grid_inputs.shape[1]
    block_rows = g2m_values.shape[1]
    channels = embed_out.shape[1]
    edge_count = g2m_src.shape[0]
    held_blocks = mesh_place.shape[0] // partitions
    read_blocks = recv_blocks.shape[1] // 2
    capacity = max(1, (edge_count + partitions - 1) // partitions)
    slot_count = partitions * capacity
    embed_pre = lax.dot_general(
        grid_inputs, embed_in, (((0,), (0,)), ((), ())), preferred_element_type=jnp.float32
    )
    embed_hidden = jax.nn.silu(embed_pre).astype(jnp.bfloat16)
    embed_mixed = jnp.dot(embed_hidden, embed_out, preferred_element_type=jnp.float32)
    alive = lax.iota(jnp.int32, slab_rows) < grid_count[0]
    grid_latent = jnp.where(alive[:, None], normalize(embed_mixed) * grid_gain, 0.0).astype(
        jnp.bfloat16
    )
    grid_blocks = grid_latent.reshape(slab_rows // block_rows, block_rows, channels)
    positions = lookup(mesh_place, g2m_dst)
    targets = positions // held_blocks
    local_index = positions % held_blocks
    earlier = jnp.tril(targets[:, None] == targets[None, :], -1)
    ranking = jnp.sum(earlier, axis=1)
    slot_index = targets * capacity + ranking
    labels = jnp.full((slot_count,), -1, jnp.int32).at[slot_index].set(local_index)
    sources = grid_blocks[g2m_src]
    edge_terms = block_product(g2m_values, sources)
    outgoing = (
        jnp.zeros((slot_count, block_rows, channels), jnp.bfloat16).at[slot_index].set(edge_terms)
    )
    arrived, arrived_labels = (
        lax.all_to_all(outgoing, "space", split_axis=0, concat_axis=0, tiled=True),
        lax.all_to_all(labels, "space", split_axis=0, concat_axis=0, tiled=True),
    )
    mesh_sum = block_sums(arrived_labels, arrived, held_blocks)
    encoded = node_update(mesh_sum, node_in, node_out, node_gain)
    side_code = mesh_src // held_blocks
    block_index = mesh_src % held_blocks
    window = extended(encoded, (("space", 0),), held_blocks * block_rows)
    source_frame = window.reshape(3 * held_blocks, block_rows, channels)
    list_entry = lookup(
        recv_blocks[0], jnp.where(side_code == 2, read_blocks + block_index, block_index)
    )
    frame_index = jnp.where(
        side_code == 1, held_blocks + block_index, side_code * held_blocks + list_entry
    )
    mesh_terms = block_product(mesh_values, source_frame[frame_index])
    message = block_sums(mesh_dst, mesh_terms, held_blocks)
    proc_hidden = jax.nn.silu(
        jnp.dot(message.astype(jnp.bfloat16), proc_in, preferred_element_type=jnp.float32)
    ).astype(jnp.bfloat16)
    processed = (
        encoded.astype(jnp.float32)
        + proc_gain * normalize(jnp.dot(proc_hidden, proc_out, preferred_element_type=jnp.float32))
    ).astype(jnp.bfloat16)
    return (encoded, processed)


def solution(mesh):
    return jax.shard_map(
        shards,
        mesh=mesh,
        in_specs=(
            P(None, ("groups", "space")),
            P("space"),
            P(),
            P(),
            P(),
            P("space", None, None),
            P("space"),
            P("space"),
            P(),
            P(),
            P(),
            P(),
            P("space", None),
            P("space", None, None),
            P("space"),
            P("space"),
            P(),
            P(),
            P(),
        ),
        out_specs=(P(("groups", "space"), None), P(("groups", "space"), None)),
        check_vma=False,
    )
```

profile of v0, /device:TPU:0, one launch (start us, length us, event | category | flops | bytes accessed | tf_op | source)
XLA Modules:
  0.0 314.0 jit_solution(4554114928031833762)
XLA Ops:
  0.6 0.0 copy-start
  0.6 1.0 select_reduce_fusion
  1.7 0.2 convert_reduce_fusion
  1.9 0.8 scatter_custom_fusion
  2.7 0.7 all_to_all.9
  3.3 7.4 %all-to-all-start = ((s32[16,4,1]{1,2,0:T(1,128)}), s32[16,4,1]{1,2,0:T(1,128)S(1)}, u32[]{:S(2)}, u32[]{:S(2)}) async-start(s32[16,4,1]{1,2,0:T(1,128)} %bitcast.3), calls=%async_computation | async-start | bytes 16384 | tf_op jit(solution)/shard_map/all_to_all | solution.py:113
  10.7 5.7 %fusion.20 = (f32[2048]{0:T(1024)S(1)}, f32[2048,512]{1,0:T(8,128)}) fusion(bf16[512,512]{1,0:T(8,128)(2,1)} %param.22, bf16[227,2048]{1,0:T(8,128)(2,1)} %param.19, bf16[227,512]{1,0:T(8,128)(2,1)} %param.21), kind=kOutput, calls=%fused_computation.72 | convolution fusion | flops 1556084736 | bytes 5889024 | tf_op jit(solution)/shard_map/dot_general | solution.py:93
  16.4 0.0 copy-start.9
  16.4 0.0 copy-start.2
  16.4 0.0 copy-start.4
  16.4 3.0 multiply_reduce_fusion
  20.1 0.0 copy-done.9
  20.2 0.0 copy-done.2
  20.2 0.0 copy-done.4
  20.2 2.9 select_convert_fusion
  23.1 7.1 %gather_fusion = bf16[64,128,512]{2,1,0:T(8,128)(2,1)} fusion(bf16[16,128,512]{2,1,0:T(8,128)(2,1)} %bitcast.46, s32[1024]{0:T(1024)S(1)} %pad_clamp_fusion.1), kind=kCustom, calls=%fused_computation | custom fusion | bytes 16777472 | tf_op jit(solution)/shard_map/gather | solution.py:106
  30.2 0.0 copy-done
  30.2 6.8 %convert_bitcast_fusion = bf16[64,128,512]{1,2,0:T(8,128)(2,1)} fusion(bf16[64,128,512]{2,1,0:T(8,128)(2,1)} %gather_fusion, bf16[64,128,128]{2,1,0:T(8,128)(2,1)S(1)} %copy-done), kind=kOutput, calls=%fused_computation.5 | convolution fusion | flops 1077936128 | bytes 18874368 | tf_op jit(solution)/shard_map/eij,ejd->eid/dot_general | solution.py:54
  37.0 11.9 %copy.44 = bf16[64,128,512]{2,1,0:T(8,128)(2,1)} copy(bf16[64,128,512]{1,2,0:T(8,128)(2,1)} %convert_bitcast_fusion) | data formatting | bytes 16777216 | tf_op jit(solution)/shard_map/convert_element_type | solution.py:54
  48.9 4.2 %broadcast_in_dim.81 = bf16[64,128,512]{2,1,0:T(8,128)(2,1)} broadcast(bf16[]{:T(256)} %constant.79.clone.1), dimensions={} | broadcast | bytes 8388610 | tf_op jit(solution)/shard_map/broadcast_in_dim | solution.py:109
  53.1 22.1 %scatter_fusion = bf16[64,128,512]{2,1,0:T(8,128)(2,1)} fusion(bf16[64,128,512]{2,1,0:T(8,128)(2,1)} %broadcast_in_dim.81, s32[64]{0:T(128)S(1)} %fusion.14, bf16[64,128,512]{2,1,0:T(8,128)(2,1)} %copy.44), kind=kCustom, calls=%fused_computation.3 | custom fusion | bytes 25166080 | tf_op jit(solution)/shard_map/scatter | solution.py:109
  75.3 0.0 all-to-all-done
  75.3 6.1 %all-to-all-start.1 = ((bf16[64,128,512]{2,1,0:T(8,128)(2,1)}), bf16[64,128,512]{2,1,0:T(8,128)(2,1)}, u32[]{:S(2)}, u32[]{:S(2)}) async-start(bf16[64,128,512]{2,1,0:T(8,128)(2,1)} %scatter_fusion), calls=%async_computation.1 | async-start | bytes 16777216 | tf_op jit(solution)/shard_map/all_to_all | solution.py:112
  81.4 0.5 broadcast.289
  81.9 0.7 reduce.3
  82.6 0.1 eq.83
  82.6 149.4 %all-to-all-done.1 = bf16[64,128,512]{2,1,0:T(8,128)(2,1)} async-done(((bf16[64,128,512]{2,1,0:T(8,128)(2,1)}), bf16[64,128,512]{2,1,0:T(8,128)(2,1)}, u32[]{:S(2)}, u32[]{:S(2)}) %all-to-all-start.1) | async-done | bytes 8388640 | tf_op jit(solution)/shard_map/all_to_all | solution.py:112
  232.1 11.7 %copy.53 = bf16[8,8,128,512]{3,1,2,0:T(8,128)(2,1)} copy(bf16[8,8,128,512]{3,2,1,0:T(8,128)(2,1)} %bitcast.10) | data formatting | bytes 16777216
  243.8 4.6 %fusion.11 = f32[4,65536]{1,0:T(4,128)S(1)} fusion(bf16[64,65536]{1,0:T(8,128)(2,1)} %bitcast.47, s32[64]{0:T(128)S(1)} %eq.83), kind=kOutput, calls=%fused_computation.42 | convolution fusion | flops 33554688 | bytes 9437440 | tf_op jit(solution)/shard_map/dot_general | solution.py:49
  248.4 0.7 reshape.161
  249.1 0.3 copy.45
  249.5 0.0 copy-start.6
  249.5 0.0 copy-start.7
  249.5 0.0 copy-start.10
  249.5 2.2 fusion.21
  251.7 0.2 multiply_reduce_fusion.2
  251.9 0.0 copy-done.6
  251.9 0.2 add_convert_fusion.1
  252.1 0.8 collective-permute-start
  252.9 34.5 %collective-permute-start.1 = (bf16[512,512]{0,1:T(8,128)(2,1)S(1)}, bf16[512,512]{0,1:T(8,128)(2,1)S(1)}, u32[]{:S(2)}, u32[]{:S(2)}) collective-permute-start(bf16[512,512]{0,1:T(8,128)(2,1)S(1)} %add_convert_fusion.1), channel_id=1, source_target_pairs={{1,0},{2,1},{3,2},{4,3},{5,4},{6,5},{7,6},{8,7},{9,8},{10,9},{11,1... | collective-permute-start | bytes 1572872 | tf_op jit(solution)/shard_map/ppermute | solution.py:18
  287.4 0.0 copy-done.7
  287.5 0.0 copy-done.10
  287.5 0.1 select_reduce_fusion.1
  287.6 1.0 copy.49
  288.6 5.4 %collective-permute-done = bf16[512,512]{0,1:T(8,128)(2,1)S(1)} collective-permute-done((bf16[512,512]{0,1:T(8,128)(2,1)S(1)}, bf16[512,512]{0,1:T(8,128)(2,1)S(1)}, u32[]{:S(2)}, u32[]{:S(2)}) %collective-permute-start) | collective-permute-done | bytes 524320 | tf_op jit(solution)/shard_map/ppermute | solution.py:16
  294.0 0.1 collective-permute-done.1
  294.1 0.1 pad_maximum_fusion
  294.3 1.6 copy.46
  295.9 2.1 gather_fusion.1
  297.9 0.0 copy-done.3
  297.9 1.8 fusion.1
  299.7 2.6 copy.48
  302.3 1.6 pad.5
  303.9 1.2 copy.54
  305.1 0.0 copy-done.8
  305.1 0.4 convolution_convert_fusion
  305.6 0.0 copy-start.1
  305.6 1.2 convert_element_type.59
  306.8 3.3 %fusion.24 = (f32[512]{0:T(512)S(1)}, f32[512,512]{0,1:T(8,128)}) fusion(bf16[512,512]{1,0:T(8,128)(2,1)} %param.36, bf16[512,512]{1,0:T(8,128)(2,1)} %convert_element_type.59, bf16[512,512]{1,0:T(8,128)(2,1)} %param.35), kind=kOutput, calls=%fused_computation.74 | convolution fusion | flops 538443264 | bytes 2623488 | tf_op jit(solution)/shard_map/dot_general | solution.py:134
  310.1 1.4 multiply_reduce_fusion.1
  311.5 0.0 copy-done.5
  311.5 1.4 add_convert_fusion
  313.0 1.0 copy.50
  314.0 0.0 copy-done.1
  (17 shorter events, 0.1 us)
Async XLA Ops:
  0.6 29.5 %copy-start = (bf16[64,128,128]{2,1,0:T(8,128)(2,1)S(1)}, bf16[64,128,128]{2,1,0:T(8,128)(2,1)}, u32[]{:S(2)}) copy-start(bf16[64,128,128]{2,1,0:T(8,128)(2,1)} %param.24) | copy-start | bytes 6291460
  3.3 71.9 %all-to-all-start = ((s32[16,4,1]{1,2,0:T(1,128)}), s32[16,4,1]{1,2,0:T(1,128)S(1)}, u32[]{:S(2)}, u32[]{:S(2)}) async-start(s32[16,4,1]{1,2,0:T(1,128)} %bitcast.3), calls=%async_computation | async-start | bytes 16384 | tf_op jit(solution)/shard_map/all_to_all | solution.py:113
  16.4 3.7 %copy-start.9 = (s32[64]{0:T(128)S(1)}, s32[64]{0:T(128)}, u32[]{:S(2)}) copy-start(s32[64]{0:T(128)} %param.25) | copy-start | bytes 772
  16.4 3.8 %copy-start.2 = (f32[2048,512]{1,0:T(8,128)S(1)}, f32[2048,512]{1,0:T(8,128)}, u32[]{:S(2)}) copy-start(f32[2048,512]{1,0:T(8,128)} %get-tuple-element.16) | copy-start | bytes 12582916
  16.4 3.8 %copy-start.4 = (f32[512]{0:T(512)S(1)}, f32[512]{0:T(512)}, u32[]{:S(2)}) copy-start(f32[512]{0:T(512)} %param.23) | copy-start | bytes 6148
  75.3 156.8 %all-to-all-start.1 = ((bf16[64,128,512]{2,1,0:T(8,128)(2,1)}), bf16[64,128,512]{2,1,0:T(8,128)(2,1)}, u32[]{:S(2)}, u32[]{:S(2)}) async-start(bf16[64,128,512]{2,1,0:T(8,128)(2,1)} %scatter_fusion), calls=%async_computation.1 | async-start | bytes 16777216 | tf_op jit(solution)/shard_map/all_to_all | solution.py:112
  249.5 2.5 copy-start.6
  249.5 38.0 %copy-start.7 = (s32[12]{0:T(128)S(1)}, s32[12]{0:T(128)}, u32[]{:S(2)}) copy-start(s32[12]{0:T(128)} %param.34) | copy-start | bytes 148
  249.5 38.0 %copy-start.10 = (s32[1,4]{1,0:T(1,128)S(1)}, s32[1,4]{1,0:T(1,128)}, u32[]{:S(2)}) copy-start(s32[1,4]{1,0:T(1,128)} %param.31) | copy-start | bytes 52
  252.1 41.9 %collective-permute-start = (bf16[512,512]{0,1:T(8,128)(2,1)S(1)}, bf16[512,512]{0,1:T(8,128)(2,1)S(1)}, u32[]{:S(2)}, u32[]{:S(2)}) collective-permute-start(bf16[512,512]{0,1:T(8,128)(2,1)S(1)} %add_convert_fusion.1), channel_id=1, source_target_pairs={{0,1},{1,2},{2,3},{3,4},{4,5},{5,6},{6,7},{7,8},{8,9},{9,10},{10,1... | collective-permute-start | bytes 1572872 | tf_op jit(solution)/shard_map/ppermute | solution.py:16
  252.9 41.2 %collective-permute-start.1 = (bf16[512,512]{0,1:T(8,128)(2,1)S(1)}, bf16[512,512]{0,1:T(8,128)(2,1)S(1)}, u32[]{:S(2)}, u32[]{:S(2)}) collective-permute-start(bf16[512,512]{0,1:T(8,128)(2,1)S(1)} %add_convert_fusion.1), channel_id=1, source_target_pairs={{1,0},{2,1},{3,2},{4,3},{5,4},{6,5},{7,6},{8,7},{9,8},{10,9},{11,1... | collective-permute-start | bytes 1572872 | tf_op jit(solution)/shard_map/ppermute | solution.py:18
  288.6 9.3 %copy-start.3 = (bf16[12,128,128]{2,1,0:T(8,128)(2,1)S(1)}, bf16[12,128,128]{2,1,0:T(8,128)(2,1)}, u32[]{:S(2)}) copy-start(bf16[12,128,128]{2,1,0:T(8,128)(2,1)} %param.32) | copy-start | bytes 1179652
  302.3 2.8 copy-start.8
  305.6 8.4 %copy-start.1 = (bf16[64,128,128]{2,1,0:T(8,128)(2,1)S(1)}, bf16[64,128,128]{2,1,0:T(8,128)(2,1)}, u32[]{:S(2)}) copy-start(bf16[64,128,128]{2,1,0:T(8,128)(2,1)} %param.24) | copy-start | bytes 6291460
  306.8 4.7 %copy-start.5 = (f32[512]{0:T(512)S(1)}, f32[512]{0:T(512)}, u32[]{:S(2)}) copy-start(f32[512]{0:T(512)} %param.37) | copy-start | bytes 6148
where the time goes:
time: 318 us; the launch traced here: 314 us
  waiting for transfers between devices  155 us (49%)
  local copies, waits for them, and re-layouts  72.5 us (23%)
  starting transfers between devices  48.8 us (15%)
  matrix products  24.8 us (8%)
  other arithmetic  11.3 us (4%)
    all_to_all x1, waiting for transfers between devices, shards(): lax.all_to_all(outgoing, 'space', split_axis=0, concat_axis=0, tiled=True)  149 us
    ppermute x1, starting transfers between devices, extended(): lax.ppermute(head, axis, [((i + 1) % count, i) for i in range(count)])  34.5 us
    scatter x1, local copies, waits for them, and re-layouts, shards(): jnp.zeros((slot_count, block_rows, channels), jnp.bfloat16).at[slot_index]  22.1 us
    unnamed x27, local copies, waits for them, and re-layouts  16.6 us
    convert_element_type x2, local copies, waits for them, and re-layouts, block_product(): jnp.einsum('eij,ejd->eid', values, sources, preferred_element_type=jnp.fl...  14.5 us
    dot_general x2, matrix products, block_product(): jnp.einsum('eij,ejd->eid', values, sources, preferred_element_type=jnp.fl...  8.6 us
    all_to_all x1, starting transfers between devices, shards(): lax.all_to_all(labels, 'space', split_axis=0, concat_axis=0, tiled=True)  7.39 us
    gather x1, local copies, waits for them, and re-layouts, shards(): sources = grid_blocks[g2m_src]  7.1 us
  transfers between devices with their start and end apart: 4, of which 3 were waited for; matrix products, arithmetic and copies ran while one was open for 21% of the time, Pallas kernels for 0%

commit v1 on v0

v1 whole, which is shorter than its diff:
```python
import functools

import jax
import jax.numpy as jnp
from jax import lax
from jax.experimental import pallas as pl
from jax.experimental.pallas import tpu as pltpu
from jax.sharding import PartitionSpec as P

EPSILON = 1e-05
LANES = 128
VMEM_BYTES = 56 * 1024 * 1024
VMEM = pl.BlockSpec(memory_space=pltpu.VMEM)
SMEM = pl.BlockSpec(memory_space=pltpu.SMEM)


def silu(values):
    half = 0.5 * values
    return half + half * jnp.tanh(half)


def normalize(values):
    average = jnp.mean(values, axis=-1, keepdims=True)
    centred = values - average
    variance = jnp.mean(centred * centred, axis=-1, keepdims=True)
    return centred * lax.rsqrt(variance + EPSILON)


def matmul(left, right):
    return jnp.dot(left, right, preferred_element_type=jnp.float32)


def transposed_matmul(left, right):
    return lax.dot_general(left, right, (((0,), (0,)), ((), ())), preferred_element_type=jnp.float32)


def add(left, right):
    return left.astype(jnp.float32) + right.astype(jnp.float32)


def place_of(step, order):
    place = 0
    for bit in order:
        place = place * 2 + ((step >> (bit - 1)) & 1)
    return place


def grid_kernel(
    tiles,
    held,
    capacity,
    src_ref,
    dst_ref,
    place_ref,
    count_ref,
    inputs_ref,
    embed_in_ref,
    embed_out_ref,
    gain_ref,
    values_ref,
    *refs,
):
    chunks = (len(refs) - 5) // 2
    mates, owns = refs[:chunks], refs[chunks : 2 * chunks]
    latent, edge_of, local_of, source_of, filled = refs[2 * chunks :]
    step = pl.program_id(0)
    tile_rows = inputs_ref.shape[1]
    rows = values_ref.shape[1]
    edges = src_ref.shape[0]

    @pl.when(step == 0)
    def _():
        me = lax.axis_index("space")

        def clear(slot, carry):
            filled[slot] = 0
            return carry

        lax.fori_loop(0, edges // capacity, clear, 0)

        def sort(edge, carry):
            position = place_ref[dst_ref[edge]]
            slot = lax.div(position, held) ^ me
            at = slot * capacity + filled[slot]
            edge_of[at] = edge
            local_of[at] = lax.rem(position, held)
            source_of[at] = src_ref[edge]
            filled[slot] = filled[slot] + 1
            return carry

        lax.fori_loop(0, edges, sort, 0)

    @pl.when(step < tiles)
    def _():
        hidden = silu(transposed_matmul(inputs_ref[...], embed_in_ref[...])).astype(jnp.bfloat16)
        scaled = normalize(matmul(hidden, embed_out_ref[...])) * gain_ref[...]
        first = pl.multiple_of(step * tile_rows, tile_rows)
        row = first + lax.broadcasted_iota(jnp.int32, (tile_rows, 1), 0)
        latent[pl.ds(first, tile_rows), :] = jnp.where(row < count_ref[0], scaled, 0.0).astype(jnp.bfloat16)

    @pl.when(step >= tiles)
    def _():
        for side, outs in ((0, owns), (1, mates)):
            first = (2 * (step - tiles) + side) * capacity
            operator = []
            sources = []
            for index in range(capacity):
                values = values_ref[edge_of[first + index]]
                local = local_of[first + index]
                zeros = jnp.zeros_like(values)
                operator.append(
                    jnp.concatenate([jnp.where(local == block, values, zeros) for block in range(held)], axis=0)
                )
                start = pl.multiple_of(source_of[first + index] * rows, rows)
                sources.append(latent[pl.ds(start, rows), :])
            summed = matmul(jnp.concatenate(operator, axis=1), jnp.concatenate(sources, axis=0))
            width = summed.shape[1] // chunks
            for chunk, out in enumerate(outs):
                out[...] = summed[:, chunk * width : (chunk + 1) * width].astype(jnp.bfloat16)


def slab_sums(
    grid_inputs, grid_count, embed_in, embed_out, grid_gain, g2m_values, g2m_src, g2m_dst, mesh_place, partitions, orders
):
    tile_rows = 256
    channels_in, slab_rows = grid_inputs.shape
    channels = embed_out.shape[1]
    edges, rows, _ = g2m_values.shape
    held = mesh_place.shape[0] // partitions
    capacity = edges // partitions
    tiles = slab_rows // tile_rows
    pairs = partitions // 2
    width = channels // len(orders)

    def out_spec(order):
        return pl.BlockSpec(
            (held * rows, width), lambda step: (place_of(jnp.maximum(step - tiles, 0), order), 0)
        )

    whole = lambda shape: pl.BlockSpec(shape, lambda step: (0,) * len(shape))
    out_specs = [out_spec(order) for order in orders] * 2
    return pl.pallas_call(
        functools.partial(grid_kernel, tiles, held, capacity),
        grid=(tiles + pairs,),
        in_specs=[
            SMEM,
            SMEM,
            SMEM,
            SMEM,
            pl.BlockSpec((channels_in, tile_rows), lambda step: (0, jnp.minimum(step, tiles - 1))),
            whole(embed_in.shape),
            whole(embed_out.shape),
            whole((1, channels)),
            whole(g2m_values.shape),
        ],
        out_specs=out_specs,
        out_shape=[jax.ShapeDtypeStruct((pairs * held * rows, width), jnp.bfloat16)] * len(out_specs),
        scratch_shapes=[
            pltpu.VMEM((slab_rows, channels), jnp.bfloat16),
            pltpu.SMEM((edges,), jnp.int32),
            pltpu.SMEM((edges,), jnp.int32),
            pltpu.SMEM((edges,), jnp.int32),
            pltpu.SMEM((partitions,), jnp.int32),
        ],
        compiler_params=pltpu.CompilerParams(vmem_limit_bytes=VMEM_BYTES),
        name="grid_to_mesh",
    )(g2m_src, g2m_dst, mesh_place, grid_count, grid_inputs, embed_in, embed_out, grid_gain.reshape(1, -1), g2m_values)


def exchange(cells, bit):
    count = lax.axis_size("space")
    return lax.ppermute(cells, "space", [(i, i ^ (1 << bit)) for i in range(count)])


def reduce_chunks(mates, owns, orders):
    arrived = [exchange(mate, 0) for mate in mates]
    kept = list(owns)
    for stage in range(len(orders[0])):
        for chunk, order in enumerate(orders):
            half = kept[chunk].shape[0] // 2
            send = add(arrived[chunk][half:], kept[chunk][half:]).astype(jnp.bfloat16)
            kept[chunk] = add(arrived[chunk][:half], kept[chunk][:half]).astype(jnp.bfloat16)
            arrived[chunk] = exchange(send, order[stage])
    return arrived, kept


def node_kernel(parts, reads, rows, wanted_ref, *refs):
    summands = refs[:parts]
    node_in_ref, node_out_ref, gain_ref, encoded_ref, upward_ref, downward_ref = refs[parts:]
    if parts == 1:
        summed = summands[0][...]
    else:
        chunks = parts // 2
        summed = jnp.concatenate(
            [add(summands[chunk][...], summands[chunks + chunk][...]) for chunk in range(chunks)], axis=1
        )
    hidden = silu(matmul(summed.astype(jnp.bfloat16), node_in_ref[...])).astype(jnp.bfloat16)
    encoded_ref[...] = (summed + gain_ref[...] * normalize(matmul(hidden, node_out_ref[...]))).astype(jnp.bfloat16)
    for index in range(reads):
        for first, out in ((0, upward_ref), (reads, downward_ref)):
            start = pl.multiple_of(wanted_ref[first + index] * rows, rows)
            out[index * rows : (index + 1) * rows, :] = encoded_ref[pl.ds(start, rows), :]


def encode(summands, node_in, node_out, node_gain, wanted, held, rows):
    channels = node_in.shape[0]
    reads = wanted.shape[0] // 2
    return pl.pallas_call(
        functools.partial(node_kernel, len(summands), reads, rows),
        in_specs=[SMEM] + [VMEM] * (len(summands) + 3),
        out_specs=[VMEM] * 3,
        out_shape=[
            jax.ShapeDtypeStruct((held * rows, channels), jnp.bfloat16),
            jax.ShapeDtypeStruct((reads * rows, channels), jnp.bfloat16),
            jax.ShapeDtypeStruct((reads * rows, channels), jnp.bfloat16),
        ],
        compiler_params=pltpu.CompilerParams(vmem_limit_bytes=VMEM_BYTES),
        name="node_update",
    )(wanted, *summands, node_in, node_out, node_gain.reshape(1, -1))


def process_kernel(
    held,
    reads,
    dst_ref,
    src_ref,
    encoded_ref,
    lower_ref,
    upper_ref,
    values_ref,
    proc_in_ref,
    proc_out_ref,
    gain_ref,
    processed_ref,
    frame,
):
    edges, rows, _ = values_ref.shape
    frame[: reads * rows, :] = lower_ref[...]
    frame[held * rows : 2 * held * rows, :] = encoded_ref[...]
    frame[2 * held * rows : (2 * held + reads) * rows, :] = upper_ref[...]
    operator = []
    sources = []
    for edge in range(edges):
        values = values_ref[edge]
        zeros = jnp.zeros_like(values)
        local = dst_ref[edge]
        operator.append(
            jnp.concatenate([jnp.where(local == block, values, zeros) for block in range(held)], axis=0)
        )
        start = pl.multiple_of(src_ref[edge] * rows, rows)
        sources.append(frame[pl.ds(start, rows), :])
    message = matmul(jnp.concatenate(operator, axis=1), jnp.concatenate(sources, axis=0))
    hidden = silu(matmul(message.astype(jnp.bfloat16), proc_in_ref[...])).astype(jnp.bfloat16)
    update = gain_ref[...] * normalize(matmul(hidden, proc_out_ref[...]))
    processed_ref[...] = (encoded_ref[...].astype(jnp.float32) + update).astype(jnp.bfloat16)


def process(encoded, lower, upper, mesh_values, mesh_dst, mesh_src, proc_in, proc_out, proc_gain, held, reads):
    rows = mesh_values.shape[1]
    return pl.pallas_call(
        functools.partial(process_kernel, held, reads),
        in_specs=[SMEM] * 2 + [VMEM] * 7,
        out_specs=VMEM,
        out_shape=jax.ShapeDtypeStruct(encoded.shape, jnp.bfloat16),
        scratch_shapes=[pltpu.VMEM(((2 * held + reads) * rows, encoded.shape[1]), jnp.bfloat16)],
        compiler_params=pltpu.CompilerParams(vmem_limit_bytes=VMEM_BYTES),
        name="process",
    )(mesh_dst, mesh_src, encoded, lower, upper, mesh_values, proc_in, proc_out, proc_gain.reshape(1, -1))


def lookup(table, wanted):
    matches = wanted[:, None] == jnp.arange(table.shape[0], dtype=jnp.int32)[None, :]
    return jnp.sum(jnp.where(matches, table[None, :], 0), axis=1)


def routed_sum(
    grid_inputs, grid_count, embed_in, embed_out, grid_gain, g2m_values, g2m_src, g2m_dst, mesh_place, partitions
):
    slab_rows = grid_inputs.shape[1]
    edge_count, block_rows, _ = g2m_values.shape
    channels = embed_out.shape[1]
    held = mesh_place.shape[0] // partitions
    capacity = max(1, (edge_count + partitions - 1) // partitions)
    slot_count = partitions * capacity
    hidden = jax.nn.silu(transposed_matmul(grid_inputs, embed_in)).astype(jnp.bfloat16)
    alive = lax.iota(jnp.int32, slab_rows) < grid_count[0]
    latent = jnp.where(alive[:, None], normalize(matmul(hidden, embed_out)) * grid_gain, 0.0).astype(jnp.bfloat16)
    positions = lookup(mesh_place, g2m_dst)
    targets = positions // held
    ranking = jnp.sum(jnp.tril(targets[:, None] == targets[None, :], -1), axis=1)
    slot_index = targets * capacity + ranking
    labels = jnp.full((slot_count,), -1, jnp.int32).at[slot_index].set(positions % held)
    sources = latent.reshape(slab_rows // block_rows, block_rows, channels)[g2m_src]
    terms = jnp.einsum("eij,ejd->eid", g2m_values, sources, preferred_element_type=jnp.float32).astype(jnp.bfloat16)
    outgoing = jnp.zeros((slot_count, block_rows, channels), jnp.bfloat16).at[slot_index].set(terms)
    arrived = lax.all_to_all(outgoing, "space", split_axis=0, concat_axis=0, tiled=True)
    arrived_labels = lax.all_to_all(labels, "space", split_axis=0, concat_axis=0, tiled=True)
    selector = (arrived_labels[None, :] == jnp.arange(held, dtype=jnp.int32)[:, None]).astype(jnp.bfloat16)
    return matmul(selector, arrived.reshape(slot_count, -1)).reshape(held * block_rows, channels)


def shards(
    grid_inputs,
    grid_count,
    embed_in,
    embed_out,
    grid_gain,
    g2m_values,
    g2m_src,
    g2m_dst,
    mesh_place,
    node_in,
    node_out,
    node_gain,
    recv_blocks,
    mesh_values,
    mesh_dst,
    mesh_src,
    proc_in,
    proc_out,
    proc_gain,
):
    partitions = lax.axis_size("space")
    edges, rows, _ = g2m_values.shape
    mesh_blocks = mesh_place.shape[0]
    held = mesh_blocks // partitions
    reads = recv_blocks.shape[1] // 2
    bits = partitions.bit_length() - 1
    upward = [(i, (i + 1) % partitions) for i in range(partitions)]
    downward = [((i + 1) % partitions, i) for i in range(partitions)]
    grid_args = (grid_inputs, grid_count, embed_in, embed_out, grid_gain, g2m_values, g2m_src, g2m_dst, mesh_place)
    if partitions == 1 << bits and bits >= 3 and edges % partitions == 0 and edges >= mesh_blocks:
        near_first = tuple(range(1, bits))
        far_first = (2, 1) + tuple(range(3, bits))
        orders = [far_first, near_first, far_first, near_first]
        sums = slab_sums(*grid_args, partitions, orders)
        arrived, kept = reduce_chunks(sums[: len(orders)], sums[len(orders) :], orders)
        summands = arrived + kept
    else:
        summands = [routed_sum(*grid_args, partitions)]
    wanted = jnp.concatenate(
        [
            lax.ppermute(recv_blocks[0, :reads], "space", downward),
            lax.ppermute(recv_blocks[0, reads:], "space", upward),
        ]
    )
    encoded, to_upper, to_lower = encode(summands, node_in, node_out, node_gain, wanted, held, rows)
    lower = lax.ppermute(to_upper, "space", upward)
    upper = lax.ppermute(to_lower, "space", downward)
    processed = process(
        encoded, lower, upper, mesh_values, mesh_dst, mesh_src, proc_in, proc_out, proc_gain, held, reads
    )
    return (encoded, processed)


def solution(mesh):
    return jax.shard_map(
        shards,
        mesh=mesh,
        in_specs=(
            P(None, ("groups", "space")),
            P("space"),
            P(),
            P(),
            P(),
            P("space", None, None),
            P("space"),
            P("space"),
            P(),
            P(),
            P(),
            P(),
            P("space", None),
            P("space", None, None),
            P("space"),
            P("space"),
            P(),
            P(),
            P(),
        ),
        out_specs=(P(("groups", "space"), None), P(("groups", "space"), None)),
        check_vma=False,
    )
```

time: 318 us -> 103 us (0.32); the launches traced: 314 us -> 103 us
  waiting for transfers between devices: 155 us -> 42.3 us
  local copies, waits for them, and re-layouts: 72.5 us -> 1.54 us
  Pallas kernels: 0 us -> 25.7 us
  matrix products: 24.8 us -> 0 us
  starting transfers between devices: 48.8 us -> 25.7 us
  other arithmetic: 11.3 us -> 6.29 us
    all_to_all x2 -> x0, waiting for transfers between devices: 149 us -> none  [the longest x1 149 us: shards(): lax.all_to_all(outgoing, 'space', split_axis=0, concat_axis=0, tiled=True)]
    ppermute x2 -> x20, waiting for transfers between devices: 5.56 us -> 42.3 us  [the longest x16 29.9 us: exchange(): lax.ppermute(cells, 'space', [(i, i ^ 1 << bit) for i in range(count)])]
    pallas_call x0 -> x3, Pallas kernels: none -> 25.7 us  [the longest x1 17.8 us: slab_sums(): pl.pallas_call(functools.partial(grid_kernel, tiles, held, capacity), gri...]
    dot_general x7 -> x0, matrix products: 24.8 us -> none  [the longest x2 8.6 us: block_product(): jnp.einsum('eij,ejd->eid', values, sources, preferred_element_type=jnp.fl...]
    scatter x2 -> x0, local copies, waits for them, and re-layouts: 22.9 us -> none  [the longest x1 22.1 us: shards(): jnp.zeros((slot_count, block_rows, channels), jnp.bfloat16).at[slot_index]]
    convert_element_type x3 -> x0, local copies, waits for them, and re-layouts: 15.7 us -> none  [the longest x2 14.5 us: block_product(): jnp.einsum('eij,ejd->eid', values, sources, preferred_element_type=jnp.fl...]
    unnamed x27 -> x20, local copies, waits for them, and re-layouts: 16.6 us -> 1.47 us
    all_to_all x2 -> x0, starting transfers between devices: 13.5 us -> none  [the longest x1 7.39 us: shards(): lax.all_to_all(labels, 'space', split_axis=0, concat_axis=0, tiled=True)]
  transfers between devices with their start and end apart: 4 -> 20, of which waited for: 3 -> 13; matrix products, arithmetic and copies ran while one was open for 21% -> 6% of each run, Pallas kernels for 0% -> 0%
where the time goes in v1:
time: 103 us
  waiting for transfers between devices  42.3 us (41%)
  Pallas kernels  25.7 us (25%)
  starting transfers between devices  25.7 us (25%)
  other arithmetic  6.29 us (6%)
  local copies, waits for them, and re-layouts  1.54 us (1%)
  between operations  1.37 us (1%)
    ppermute x16, waiting for transfers between devices, exchange(): lax.ppermute(cells, 'space', [(i, i ^ 1 << bit) for i in range(count)])  29.9 us
    ppermute x16, starting transfers between devices, exchange(): lax.ppermute(cells, 'space', [(i, i ^ 1 << bit) for i in range(count)])  20 us
    pallas_call x1, Pallas kernels, slab_sums(): pl.pallas_call(functools.partial(grid_kernel, tiles, held, capacity), gri...  17.8 us
    ppermute x1, waiting for transfers between devices, shards(): lax.ppermute(recv_blocks[0, reads:], 'space', upward)  5.82 us
    ppermute x1, starting transfers between devices, shards(): upper = lax.ppermute(to_lower, 'space', downward)  4.44 us
    ppermute x1, waiting for transfers between devices, shards(): lower = lax.ppermute(to_upper, 'space', upward)  4.37 us
    pallas_call x1, Pallas kernels, process(): pl.pallas_call(functools.partial(process_kernel, held, reads), in_specs=[...  4.36 us
    pallas_call x1, Pallas kernels, encode(): pl.pallas_call(functools.partial(node_kernel, len(summands), reads, rows)...  3.58 us
  transfers between devices with their start and end apart: 20, of which 13 were waited for; matrix products, arithmetic and copies ran while one was open for 6% of the time, Pallas kernels for 0%

profile of v1, /device:TPU:0, one launch (start us, length us, event | category | flops | bytes accessed | tf_op | source)
XLA Modules:
  0.0 102.9 jit_solution(6463271743388706015)
XLA Ops:
  1.3 17.8 %grid_to_mesh.1 = (bf16[4096,128]{1,0:T(8,128)(2,1)}, bf16[4096,128]{1,0:T(8,128)(2,1)}, bf16[4096,128]{1,0:T(8,128)(2,1)}, bf16[4096,128]{1,0:T(8,128)(2,1)}, b...) custom-call(s32[64]{0:T(128)} %src_ref.2, ...), custom_call_target="tpu_custom_call" | custom-call | tf_op jit(solution)/shard_map/grid_to_mesh/pallas_call | solution.py:142
  19.0 0.0 copy-start.2
  19.1 0.5 collective-permute-start.14
  19.6 0.1 collective-permute-start.10
  19.6 0.4 collective-permute-start.6
  20.1 0.1 collective-permute-start.2
  20.2 1.9 %collective-permute-done.14 = bf16[4096,128]{1,0:T(8,128)(2,1)S(1)} collective-permute-done((bf16[4096,128]{1,0:T(8,128)(2,1)}, bf16[4096,128]{1,0:T(8,128)(2,1)S(1)}, u32[]{:S(2)}, u32[]{:S(2)}) %collective-permute-start.14) | collective-permute-done | bytes 1048608 | tf_op jit(solution)/shard_map/ppermute | solution.py:172
  22.1 1.5 %add_convert_fusion.1 = (bf16[2048,128]{1,0:T(8,128)(2,1)S(1)}, bf16[2048,128]{1,0:T(8,128)(2,1)S(1)}) fusion(bf16[4096,128]{1,0:T(8,128)(2,1)S(1)} %collective-permute-done.14, bf16[4096,128]{1,0:T(8,128)(2,1)} %get-tuple-element.20), kind=kLoop, calls=%fused_computation.1 | loop fusion | flops 2097152 | bytes 3145728 | tf_op jit(solution)/shard_map/convert_element_type | solution.py:181
  23.5 3.0 %collective-permute-start.15 = (bf16[2048,128]{1,0:T(8,128)(2,1)S(1)}, bf16[2048,128]{1,0:T(8,128)(2,1)S(1)}, u32[]{:S(2)}, u32[]{:S(2)}) collective-permute-start(bf16[2048,128]{1,0:T(8,128)(2,1)S(1)} %get-tuple-element.24), channel_id=1, source_target_pairs={{0,2},{1,3},{2,0},{3,1},{4,6},{5,7},{6,4},{7,5},{8,10},{9,11},{10,... | collective-permute-start | bytes 1572872 | tf_op jit(solution)/shard_map/ppermute | solution.py:172
  26.5 0.0 collective-permute-done.10
  26.5 0.0 copy-done.2
  26.5 0.3 add_convert_fusion.3
  26.8 1.6 %collective-permute-start.11 = (bf16[2048,128]{1,0:T(8,128)(2,1)S(1)}, bf16[2048,128]{1,0:T(8,128)(2,1)S(1)}, u32[]{:S(2)}, u32[]{:S(2)}) collective-permute-start(bf16[2048,128]{1,0:T(8,128)(2,1)S(1)} %get-tuple-element.26), channel_id=1, source_target_pairs={{0,4},{1,5},{2,6},{3,7},{4,0},{5,1},{6,2},{7,3},{8,12},{9,13},{10,... | collective-permute-start | bytes 1572872 | tf_op jit(solution)/shard_map/ppermute | solution.py:172
  28.4 0.0 collective-permute-done.6
  28.4 0.3 add_convert_fusion.5
  28.7 0.6 collective-permute-start.7
  29.3 0.0 collective-permute-done.2
  29.3 0.3 add_convert_fusion.7
  29.6 0.7 collective-permute-start.3
  30.2 9.0 %collective-permute-done.15 = bf16[2048,128]{1,0:T(8,128)(2,1)S(1)} collective-permute-done((bf16[2048,128]{1,0:T(8,128)(2,1)S(1)}, bf16[2048,128]{1,0:T(8,128)(2,1)S(1)}, u32[]{:S(2)}, u32[]{:S(2)}) %collective-permute-start.15) | collective-permute-done | bytes 524320 | tf_op jit(solution)/shard_map/ppermute | solution.py:172
  39.2 0.1 add_convert_fusion.9
  39.4 2.2 %collective-permute-start.16 = (bf16[1024,128]{1,0:T(8,128)(2,1)S(1)}, bf16[1024,128]{1,0:T(8,128)(2,1)S(1)}, u32[]{:S(2)}, u32[]{:S(2)}) collective-permute-start(bf16[1024,128]{1,0:T(8,128)(2,1)S(1)} %get-tuple-element.32), channel_id=1, source_target_pairs={{0,4},{1,5},{2,6},{3,7},{4,0},{5,1},{6,2},{7,3},{8,12},{9,13},{10,... | collective-permute-start | bytes 786440 | tf_op jit(solution)/shard_map/ppermute | solution.py:172
  41.5 0.2 collective-permute-done.11
  41.7 0.1 add_convert_fusion.11
  41.8 1.4 %collective-permute-start.12 = (bf16[1024,128]{1,0:T(8,128)(2,1)S(1)}, bf16[1024,128]{1,0:T(8,128)(2,1)S(1)}, u32[]{:S(2)}, u32[]{:S(2)}) collective-permute-start(bf16[1024,128]{1,0:T(8,128)(2,1)S(1)} %get-tuple-element.34), channel_id=1, source_target_pairs={{0,2},{1,3},{2,0},{3,1},{4,6},{5,7},{6,4},{7,5},{8,10},{9,11},{10,... | collective-permute-start | bytes 786440 | tf_op jit(solution)/shard_map/ppermute | solution.py:172
  43.3 7.2 %collective-permute-done.7 = bf16[2048,128]{1,0:T(8,128)(2,1)S(1)} collective-permute-done((bf16[2048,128]{1,0:T(8,128)(2,1)S(1)}, bf16[2048,128]{1,0:T(8,128)(2,1)S(1)}, u32[]{:S(2)}, u32[]{:S(2)}) %collective-permute-start.7) | collective-permute-done | bytes 524320 | tf_op jit(solution)/shard_map/ppermute | solution.py:172
  50.5 0.1 add_convert_fusion.13
  50.6 2.2 %collective-permute-start.8 = (bf16[1024,128]{1,0:T(8,128)(2,1)S(1)}, bf16[1024,128]{1,0:T(8,128)(2,1)S(1)}, u32[]{:S(2)}, u32[]{:S(2)}) collective-permute-start(bf16[1024,128]{1,0:T(8,128)(2,1)S(1)} %get-tuple-element.36), channel_id=1, source_target_pairs={{0,4},{1,5},{2,6},{3,7},{4,0},{5,1},{6,2},{7,3},{8,12},{9,13},{10,... | collective-permute-start | bytes 786440 | tf_op jit(solution)/shard_map/ppermute | solution.py:172
  52.8 0.2 collective-permute-done.3
  52.9 0.1 add_convert_fusion.15
  53.1 1.4 %collective-permute-start.4 = (bf16[1024,128]{1,0:T(8,128)(2,1)S(1)}, bf16[1024,128]{1,0:T(8,128)(2,1)S(1)}, u32[]{:S(2)}, u32[]{:S(2)}) collective-permute-start(bf16[1024,128]{1,0:T(8,128)(2,1)S(1)} %get-tuple-element.38), channel_id=1, source_target_pairs={{0,2},{1,3},{2,0},{3,1},{4,6},{5,7},{6,4},{7,5},{8,10},{9,11},{10,... | collective-permute-start | bytes 786440 | tf_op jit(solution)/shard_map/ppermute | solution.py:172
  54.5 4.0 %collective-permute-done.16 = bf16[1024,128]{1,0:T(8,128)(2,1)S(1)} collective-permute-done((bf16[1024,128]{1,0:T(8,128)(2,1)S(1)}, bf16[1024,128]{1,0:T(8,128)(2,1)S(1)}, u32[]{:S(2)}, u32[]{:S(2)}) %collective-permute-start.16) | collective-permute-done | bytes 262176 | tf_op jit(solution)/shard_map/ppermute | solution.py:172
  58.5 0.7 add_convert_fusion.16
  59.2 2.6 %collective-permute-start.17 = (bf16[512,128]{1,0:T(8,128)(2,1)S(1)}, bf16[512,128]{1,0:T(8,128)(2,1)S(1)}, u32[]{:S(2)}, u32[]{:S(2)}) collective-permute-start(bf16[512,128]{1,0:T(8,128)(2,1)S(1)} %get-tuple-element.41), channel_id=1, source_target_pairs={{0,8},{1,9},{2,10},{3,11},{4,12},{5,13},{6,14},{7,15},{8,0},{9,1},... | collective-permute-start | bytes 393224 | tf_op jit(solution)/shard_map/ppermute | solution.py:172
  61.8 0.0 collective-permute-done.12
  61.8 0.7 add_convert_fusion.17
  62.5 0.4 collective-permute-start.13
  62.9 2.6 %collective-permute-done.8 = bf16[1024,128]{1,0:T(8,128)(2,1)S(1)} collective-permute-done((bf16[1024,128]{1,0:T(8,128)(2,1)S(1)}, bf16[1024,128]{1,0:T(8,128)(2,1)S(1)}, u32[]{:S(2)}, u32[]{:S(2)}) %collective-permute-start.8) | collective-permute-done | bytes 262176 | tf_op jit(solution)/shard_map/ppermute | solution.py:172
  65.5 0.7 add_convert_fusion.18
  66.2 1.4 %collective-permute-start.9 = (bf16[512,128]{1,0:T(8,128)(2,1)S(1)}, bf16[512,128]{1,0:T(8,128)(2,1)S(1)}, u32[]{:S(2)}, u32[]{:S(2)}) collective-permute-start(bf16[512,128]{1,0:T(8,128)(2,1)S(1)} %get-tuple-element.45), channel_id=1, source_target_pairs={{0,8},{1,9},{2,10},{3,11},{4,12},{5,13},{6,14},{7,15},{8,0},{9,1},... | collective-permute-start | bytes 393224 | tf_op jit(solution)/shard_map/ppermute | solution.py:172
  67.7 0.0 collective-permute-done.4
  67.7 0.7 add_convert_fusion.19
  68.4 1.5 %collective-permute-start.5 = (bf16[512,128]{1,0:T(8,128)(2,1)S(1)}, bf16[512,128]{1,0:T(8,128)(2,1)S(1)}, u32[]{:S(2)}, u32[]{:S(2)}) collective-permute-start(bf16[512,128]{1,0:T(8,128)(2,1)S(1)} %get-tuple-element.47), channel_id=1, source_target_pairs={{0,8},{1,9},{2,10},{3,11},{4,12},{5,13},{6,14},{7,15},{8,0},{9,1},... | collective-permute-start | bytes 393224 | tf_op jit(solution)/shard_map/ppermute | solution.py:172
  69.9 0.1 slice_bitcast_fusion.1
  70.0 1.3 %collective-permute-start = (s32[2]{0:T(128)S(1)}, s32[2]{0:T(128)S(1)}, u32[]{:S(2)}, u32[]{:S(2)}) collective-permute-start(s32[2]{0:T(128)S(1)} %get-tuple-element.48), channel_id=1, source_target_pairs={{1,0},{2,1},{3,2},{4,3},{5,4},{6,5},{7,6},{8,7},{9,8},{10,9},{11,1... | collective-permute-start | bytes 32 | tf_op jit(solution)/shard_map/ppermute | solution.py:343
  71.3 2.1 %collective-permute-done = s32[2]{0:T(128)S(1)} collective-permute-done((s32[2]{0:T(128)S(1)}, s32[2]{0:T(128)S(1)}, u32[]{:S(2)}, u32[]{:S(2)}) %collective-permute-start) | collective-permute-done | bytes 40 | tf_op jit(solution)/shard_map/ppermute | solution.py:343
  73.4 0.0 collective-permute-start.1
  73.4 5.8 %collective-permute-done.1 = s32[2]{0:T(128)S(1)} collective-permute-done((s32[2]{0:T(128)S(1)}, s32[2]{0:T(128)S(1)}, u32[]{:S(2)}, u32[]{:S(2)}) %collective-permute-start.1) | collective-permute-done | bytes 40 | tf_op jit(solution)/shard_map/ppermute | solution.py:344
  79.3 0.6 pad_add_fusion.wanted_ref
  79.8 0.0 collective-permute-done.17.refs_3_
  79.8 0.7 collective-permute-done.13.refs_2_
  80.6 2.7 %collective-permute-done.9.refs_1_ = bf16[512,128]{1,0:T(8,128)(2,1)S(1)} collective-permute-done((bf16[512,128]{1,0:T(8,128)(2,1)S(1)}, bf16[512,128]{1,0:T(8,128)(2,1)S(1)}, u32[]{:S(2)}, u32[]{:S(2)}) %collective-permute-start.9) | collective-permute-done | bytes 131104 | tf_op jit(solution)/shard_map/ppermute | solution.py:172
  83.3 1.4 %collective-permute-done.5.refs_0_ = bf16[512,128]{1,0:T(8,128)(2,1)S(1)} collective-permute-done((bf16[512,128]{1,0:T(8,128)(2,1)S(1)}, bf16[512,128]{1,0:T(8,128)(2,1)S(1)}, u32[]{:S(2)}, u32[]{:S(2)}) %collective-permute-start.5) | collective-permute-done | bytes 131104 | tf_op jit(solution)/shard_map/ppermute | solution.py:172
  84.7 0.0 copy-done.5
  84.7 0.0 copy-done.7
  84.7 0.6 copy-done.8
  85.3 3.6 %node_update.1 = (bf16[512,512]{1,0:T(8,128)(2,1)}, bf16[256,512]{1,0:T(8,128)(2,1)}, bf16[256,512]{1,0:T(8,128)(2,1)}) custom-call(s32[4]{0:T(128)} %pad_add_fusion.wanted_ref, bf16[512,128]{1,0:T(8,128)(2,1)} %copy-done.8, bf16[512,128]{1,0:T(8,128)(2,1)} %copy-done.7, bf16[512,128]{1,0:T(8,128)(2,1)} %copy-done.6, bf16[512,128]{1,0:T(8,128)(2,1)} %copy-done.5, ...), custom_call_target="tpu_custom_call" | custom-call | tf_op jit(solution)/shard_map/node_update/pallas_call | solution.py:208
  88.9 0.0 collective-permute-start.18
  88.9 4.4 %collective-permute-start.19 = (bf16[256,512]{1,0:T(8,128)(2,1)}, bf16[256,512]{1,0:T(8,128)(2,1)S(1)}, u32[]{:S(2)}, u32[]{:S(2)}) collective-permute-start(bf16[256,512]{1,0:T(8,128)(2,1)} %get-tuple-element.23), channel_id=1, source_target_pairs={{1,0},{2,1},{3,2},{4,3},{5,4},{6,5},{7,6},{8,7},{9,8},{10,9},{11,1... | collective-permute-start | bytes 786440 | tf_op jit(solution)/shard_map/ppermute | solution.py:349
  93.4 4.4 %collective-permute-done.18.lower_ref = bf16[256,512]{1,0:T(8,128)(2,1)S(1)} collective-permute-done((bf16[256,512]{1,0:T(8,128)(2,1)}, bf16[256,512]{1,0:T(8,128)(2,1)S(1)}, u32[]{:S(2)}, u32[]{:S(2)}) %collective-permute-start.18) | collective-permute-done | bytes 262176 | tf_op jit(solution)/shard_map/ppermute | solution.py:348
  97.7 0.0 collective-permute-done.19.upper_ref
  97.7 0.7 copy-done.3
  98.4 0.1 copy-done.4
  98.5 4.4 %process.1 = bf16[512,512]{1,0:T(8,128)(2,1)} custom-call(s32[12]{0:T(128)} %dst_ref.3, s32[12]{0:T(128)} %src_ref.3, bf16[512,512]{1,0:T(8,128)(2,1)} %get-tuple-element.11.encoded_ref, bf16[256,512]{1,0:T(8,128)(2,1)} %copy-done.3, bf16[256,512]{1,0:T(8,128)(2,1)} %copy-done.4, bf16[12,128,128]{2,1,0:T(8,128)(2,1)} %values_ref.3, ...), custom_call_target="tpu_custom_call" | custom-call | tf_op jit(solution)/shard_map/process/pallas_call | solution.py:260
  (13 shorter events, 0.0 us)
Async XLA Ops:
  19.0 7.5 %copy-start.2 = (bf16[4096,128]{1,0:T(8,128)(2,1)S(1)}, bf16[4096,128]{1,0:T(8,128)(2,1)}, u32[]{:S(2)}) copy-start(bf16[4096,128]{1,0:T(8,128)(2,1)} %get-tuple-element.18) | copy-start | bytes 3145732
  19.1 3.0 %collective-permute-start.14 = (bf16[4096,128]{1,0:T(8,128)(2,1)}, bf16[4096,128]{1,0:T(8,128)(2,1)S(1)}, u32[]{:S(2)}, u32[]{:S(2)}) collective-permute-start(bf16[4096,128]{1,0:T(8,128)(2,1)} %get-tuple-element.19), channel_id=1, source_target_pairs={{0,1},{1,0},{2,3},{3,2},{4,5},{5,4},{6,7},{7,6},{8,9},{9,8},{10,11... | collective-permute-start | bytes 3145736 | tf_op jit(solution)/shard_map/ppermute | solution.py:172
  19.6 6.9 %collective-permute-start.10 = (bf16[4096,128]{1,0:T(8,128)(2,1)}, bf16[4096,128]{1,0:T(8,128)(2,1)S(1)}, u32[]{:S(2)}, u32[]{:S(2)}) collective-permute-start(bf16[4096,128]{1,0:T(8,128)(2,1)} %get-tuple-element.17), channel_id=1, source_target_pairs={{0,1},{1,0},{2,3},{3,2},{4,5},{5,4},{6,7},{7,6},{8,9},{9,8},{10,11... | collective-permute-start | bytes 3145736 | tf_op jit(solution)/shard_map/ppermute | solution.py:172
  19.6 8.8 %collective-permute-start.6 = (bf16[4096,128]{1,0:T(8,128)(2,1)}, bf16[4096,128]{1,0:T(8,128)(2,1)S(1)}, u32[]{:S(2)}, u32[]{:S(2)}) collective-permute-start(bf16[4096,128]{1,0:T(8,128)(2,1)} %get-tuple-element.15), channel_id=1, source_target_pairs={{0,1},{1,0},{2,3},{3,2},{4,5},{5,4},{6,7},{7,6},{8,9},{9,8},{10,11... | collective-permute-start | bytes 3145736 | tf_op jit(solution)/shard_map/ppermute | solution.py:172
  20.1 9.2 %collective-permute-start.2 = (bf16[4096,128]{1,0:T(8,128)(2,1)}, bf16[4096,128]{1,0:T(8,128)(2,1)S(1)}, u32[]{:S(2)}, u32[]{:S(2)}) collective-permute-start(bf16[4096,128]{1,0:T(8,128)(2,1)} %get-tuple-element.13), channel_id=1, source_target_pairs={{0,1},{1,0},{2,3},{3,2},{4,5},{5,4},{6,7},{7,6},{8,9},{9,8},{10,11... | collective-permute-start | bytes 3145736 | tf_op jit(solution)/shard_map/ppermute | solution.py:172
  23.5 4.9 %copy-start.1 = (bf16[4096,128]{1,0:T(8,128)(2,1)S(1)}, bf16[4096,128]{1,0:T(8,128)(2,1)}, u32[]{:S(2)}) copy-start(bf16[4096,128]{1,0:T(8,128)(2,1)} %get-tuple-element.16) | copy-start | bytes 3145732
  23.5 15.7 %collective-permute-start.15 = (bf16[2048,128]{1,0:T(8,128)(2,1)S(1)}, bf16[2048,128]{1,0:T(8,128)(2,1)S(1)}, u32[]{:S(2)}, u32[]{:S(2)}) collective-permute-start(bf16[2048,128]{1,0:T(8,128)(2,1)S(1)} %get-tuple-element.24), channel_id=1, source_target_pairs={{0,2},{1,3},{2,0},{3,1},{4,6},{5,7},{6,4},{7,5},{8,10},{9,11},{10,... | collective-permute-start | bytes 1572872 | tf_op jit(solution)/shard_map/ppermute | solution.py:172
  26.8 2.5 %copy-start = (bf16[4096,128]{1,0:T(8,128)(2,1)S(1)}, bf16[4096,128]{1,0:T(8,128)(2,1)}, u32[]{:S(2)}) copy-start(bf16[4096,128]{1,0:T(8,128)(2,1)} %get-tuple-element.14) | copy-start | bytes 3145732
  26.8 14.9 %collective-permute-start.11 = (bf16[2048,128]{1,0:T(8,128)(2,1)S(1)}, bf16[2048,128]{1,0:T(8,128)(2,1)S(1)}, u32[]{:S(2)}, u32[]{:S(2)}) collective-permute-start(bf16[2048,128]{1,0:T(8,128)(2,1)S(1)} %get-tuple-element.26), channel_id=1, source_target_pairs={{0,4},{1,5},{2,6},{3,7},{4,0},{5,1},{6,2},{7,3},{8,12},{9,13},{10,... | collective-permute-start | bytes 1572872 | tf_op jit(solution)/shard_map/ppermute | solution.py:172
  28.7 21.7 %collective-permute-start.7 = (bf16[2048,128]{1,0:T(8,128)(2,1)S(1)}, bf16[2048,128]{1,0:T(8,128)(2,1)S(1)}, u32[]{:S(2)}, u32[]{:S(2)}) collective-permute-start(bf16[2048,128]{1,0:T(8,128)(2,1)S(1)} %get-tuple-element.28), channel_id=1, source_target_pairs={{0,2},{1,3},{2,0},{3,1},{4,6},{5,7},{6,4},{7,5},{8,10},{9,11},{10,... | collective-permute-start | bytes 1572872 | tf_op jit(solution)/shard_map/ppermute | solution.py:172
  29.6 23.3 %collective-permute-start.3 = (bf16[2048,128]{1,0:T(8,128)(2,1)S(1)}, bf16[2048,128]{1,0:T(8,128)(2,1)S(1)}, u32[]{:S(2)}, u32[]{:S(2)}) collective-permute-start(bf16[2048,128]{1,0:T(8,128)(2,1)S(1)} %get-tuple-element.30), channel_id=1, source_target_pairs={{0,4},{1,5},{2,6},{3,7},{4,0},{5,1},{6,2},{7,3},{8,12},{9,13},{10,... | collective-permute-start | bytes 1572872 | tf_op jit(solution)/shard_map/ppermute | solution.py:172
  39.4 19.2 %collective-permute-start.16 = (bf16[1024,128]{1,0:T(8,128)(2,1)S(1)}, bf16[1024,128]{1,0:T(8,128)(2,1)S(1)}, u32[]{:S(2)}, u32[]{:S(2)}) collective-permute-start(bf16[1024,128]{1,0:T(8,128)(2,1)S(1)} %get-tuple-element.32), channel_id=1, source_target_pairs={{0,4},{1,5},{2,6},{3,7},{4,0},{5,1},{6,2},{7,3},{8,12},{9,13},{10,... | collective-permute-start | bytes 786440 | tf_op jit(solution)/shard_map/ppermute | solution.py:172
  41.8 20.0 %collective-permute-start.12 = (bf16[1024,128]{1,0:T(8,128)(2,1)S(1)}, bf16[1024,128]{1,0:T(8,128)(2,1)S(1)}, u32[]{:S(2)}, u32[]{:S(2)}) collective-permute-start(bf16[1024,128]{1,0:T(8,128)(2,1)S(1)} %get-tuple-element.34), channel_id=1, source_target_pairs={{0,2},{1,3},{2,0},{3,1},{4,6},{5,7},{6,4},{7,5},{8,10},{9,11},{10,... | collective-permute-start | bytes 786440 | tf_op jit(solution)/shard_map/ppermute | solution.py:172
  50.6 14.9 %collective-permute-start.8 = (bf16[1024,128]{1,0:T(8,128)(2,1)S(1)}, bf16[1024,128]{1,0:T(8,128)(2,1)S(1)}, u32[]{:S(2)}, u32[]{:S(2)}) collective-permute-start(bf16[1024,128]{1,0:T(8,128)(2,1)S(1)} %get-tuple-element.36), channel_id=1, source_target_pairs={{0,4},{1,5},{2,6},{3,7},{4,0},{5,1},{6,2},{7,3},{8,12},{9,13},{10,... | collective-permute-start | bytes 786440 | tf_op jit(solution)/shard_map/ppermute | solution.py:172
  52.9 17.0 %copy-start.9 = (s32[1,4]{1,0:T(1,128)S(1)}, s32[1,4]{1,0:T(1,128)}, u32[]{:S(2)}) copy-start(s32[1,4]{1,0:T(1,128)} %param.31) | copy-start | bytes 52
  53.1 14.6 %collective-permute-start.4 = (bf16[1024,128]{1,0:T(8,128)(2,1)S(1)}, bf16[1024,128]{1,0:T(8,128)(2,1)S(1)}, u32[]{:S(2)}, u32[]{:S(2)}) collective-permute-start(bf16[1024,128]{1,0:T(8,128)(2,1)S(1)} %get-tuple-element.38), channel_id=1, source_target_pairs={{0,2},{1,3},{2,0},{3,1},{4,6},{5,7},{6,4},{7,5},{8,10},{9,11},{10,... | collective-permute-start | bytes 786440 | tf_op jit(solution)/shard_map/ppermute | solution.py:172
  59.2 20.6 %collective-permute-start.17 = (bf16[512,128]{1,0:T(8,128)(2,1)S(1)}, bf16[512,128]{1,0:T(8,128)(2,1)S(1)}, u32[]{:S(2)}, u32[]{:S(2)}) collective-permute-start(bf16[512,128]{1,0:T(8,128)(2,1)S(1)} %get-tuple-element.41), channel_id=1, source_target_pairs={{0,8},{1,9},{2,10},{3,11},{4,12},{5,13},{6,14},{7,15},{8,0},{9,1},... | collective-permute-start | bytes 393224 | tf_op jit(solution)/shard_map/ppermute | solution.py:172
  62.5 18.0 %collective-permute-start.13 = (bf16[512,128]{1,0:T(8,128)(2,1)S(1)}, bf16[512,128]{1,0:T(8,128)(2,1)S(1)}, u32[]{:S(2)}, u32[]{:S(2)}) collective-permute-start(bf16[512,128]{1,0:T(8,128)(2,1)S(1)} %get-tuple-element.43), channel_id=1, source_target_pairs={{0,8},{1,9},{2,10},{3,11},{4,12},{5,13},{6,14},{7,15},{8,0},{9,1},... | collective-permute-start | bytes 393224 | tf_op jit(solution)/shard_map/ppermute | solution.py:172
  66.2 17.0 %collective-permute-start.9 = (bf16[512,128]{1,0:T(8,128)(2,1)S(1)}, bf16[512,128]{1,0:T(8,128)(2,1)S(1)}, u32[]{:S(2)}, u32[]{:S(2)}) collective-permute-start(bf16[512,128]{1,0:T(8,128)(2,1)S(1)} %get-tuple-element.45), channel_id=1, source_target_pairs={{0,8},{1,9},{2,10},{3,11},{4,12},{5,13},{6,14},{7,15},{8,0},{9,1},... | collective-permute-start | bytes 393224 | tf_op jit(solution)/shard_map/ppermute | solution.py:172
  68.4 16.3 %collective-permute-start.5 = (bf16[512,128]{1,0:T(8,128)(2,1)S(1)}, bf16[512,128]{1,0:T(8,128)(2,1)S(1)}, u32[]{:S(2)}, u32[]{:S(2)}) collective-permute-start(bf16[512,128]{1,0:T(8,128)(2,1)S(1)} %get-tuple-element.47), channel_id=1, source_target_pairs={{0,8},{1,9},{2,10},{3,11},{4,12},{5,13},{6,14},{7,15},{8,0},{9,1},... | collective-permute-start | bytes 393224 | tf_op jit(solution)/shard_map/ppermute | solution.py:172
  70.0 3.4 %collective-permute-start = (s32[2]{0:T(128)S(1)}, s32[2]{0:T(128)S(1)}, u32[]{:S(2)}, u32[]{:S(2)}) collective-permute-start(s32[2]{0:T(128)S(1)} %get-tuple-element.48), channel_id=1, source_target_pairs={{1,0},{2,1},{3,2},{4,3},{5,4},{6,5},{7,6},{8,7},{9,8},{10,9},{11,1... | collective-permute-start | bytes 32 | tf_op jit(solution)/shard_map/ppermute | solution.py:343
  73.4 5.8 %collective-permute-start.1 = (s32[2]{0:T(128)S(1)}, s32[2]{0:T(128)S(1)}, u32[]{:S(2)}, u32[]{:S(2)}) collective-permute-start(s32[2]{0:T(128)S(1)} %get-tuple-element.49), channel_id=1, source_target_pairs={{0,1},{1,2},{2,3},{3,4},{4,5},{5,6},{6,7},{7,8},{8,9},{9,10},{10,1... | collective-permute-start | bytes 32 | tf_op jit(solution)/shard_map/ppermute | solution.py:344
  79.8 4.9 %copy-start.5 = (bf16[512,128]{1,0:T(8,128)(2,1)}, bf16[512,128]{1,0:T(8,128)(2,1)S(1)}, u32[]{:S(2)}) copy-start(bf16[512,128]{1,0:T(8,128)(2,1)S(1)} %collective-permute-done.17.refs_3_) | copy-start | bytes 393220
  80.6 4.1 %copy-start.6 = (bf16[512,128]{1,0:T(8,128)(2,1)}, bf16[512,128]{1,0:T(8,128)(2,1)S(1)}, u32[]{:S(2)}) copy-start(bf16[512,128]{1,0:T(8,128)(2,1)S(1)} %collective-permute-done.13.refs_2_) | copy-start | bytes 393220
  83.3 1.4 %copy-start.7 = (bf16[512,128]{1,0:T(8,128)(2,1)}, bf16[512,128]{1,0:T(8,128)(2,1)S(1)}, u32[]{:S(2)}) copy-start(bf16[512,128]{1,0:T(8,128)(2,1)S(1)} %collective-permute-done.9.refs_1_) | copy-start | bytes 393220
  84.7 0.6 copy-start.8
  88.9 8.8 %collective-permute-start.18 = (bf16[256,512]{1,0:T(8,128)(2,1)}, bf16[256,512]{1,0:T(8,128)(2,1)S(1)}, u32[]{:S(2)}, u32[]{:S(2)}) collective-permute-start(bf16[256,512]{1,0:T(8,128)(2,1)} %get-tuple-element.22), channel_id=1, source_target_pairs={{0,1},{1,2},{2,3},{3,4},{4,5},{5,6},{6,7},{7,8},{8,9},{9,10},{10,1... | collective-permute-start | bytes 786440 | tf_op jit(solution)/shard_map/ppermute | solution.py:348
  88.9 8.8 %collective-permute-start.19 = (bf16[256,512]{1,0:T(8,128)(2,1)}, bf16[256,512]{1,0:T(8,128)(2,1)S(1)}, u32[]{:S(2)}, u32[]{:S(2)}) collective-permute-start(bf16[256,512]{1,0:T(8,128)(2,1)} %get-tuple-element.23), channel_id=1, source_target_pairs={{1,0},{2,1},{3,2},{4,3},{5,4},{6,5},{7,6},{8,7},{9,8},{10,9},{11,1... | collective-permute-start | bytes 786440 | tf_op jit(solution)/shard_map/ppermute | solution.py:349
  97.7 0.7 copy-start.3
  97.7 0.8 copy-start.4

commit v2 on v1

v2 whole, which is shorter than its diff:
```python
import functools

import jax
import jax.numpy as jnp
from jax import lax
from jax.experimental import pallas as pl
from jax.experimental.pallas import tpu as pltpu
from jax.sharding import PartitionSpec as P

EPSILON = 1e-05
ORDERS = ((1, 3, 2), (1, 2, 3), (3, 1, 2), (2, 1, 3), (2, 1, 3))
SHARES = (2, 2, 2, 1, 1)
TURNS = (0, 1, 2, 3, 4, 0, 3, 1, 2, 4, 3, 2, 4, 0, 1)
VMEM_BYTES = 24 * 1024 * 1024
GRID_VMEM_BYTES = 60 * 1024 * 1024
VMEM = pl.BlockSpec(memory_space=pltpu.VMEM)
SMEM = pl.BlockSpec(memory_space=pltpu.SMEM)
ANY = pl.BlockSpec(memory_space=pl.ANY)


def silu(values):
    half = 0.5 * values
    return half + half * jnp.tanh(half)


def normalize(values):
    average = jnp.mean(values, axis=-1, keepdims=True)
    centred = values - average
    variance = jnp.mean(centred * centred, axis=-1, keepdims=True)
    return centred * lax.rsqrt(variance + EPSILON)


def matmul(left, right):
    return jnp.dot(left, right, preferred_element_type=jnp.float32)


def transposed_matmul(left, right):
    return lax.dot_general(left, right, (((0,), (0,)), ((), ())), preferred_element_type=jnp.float32)


def add(left, right):
    return left.astype(jnp.float32) + right.astype(jnp.float32)


def place_of(step, order):
    place = 0
    for bit in order:
        place = place * 2 + ((step >> (bit - 1)) & 1)
    return place


def grid_kernel(
    held,
    capacity,
    orders,
    cuts,
    tile_rows,
    src_ref,
    dst_ref,
    place_ref,
    count_ref,
    gain_ref,
    inputs_hbm,
    embed_in_hbm,
    embed_out_hbm,
    values_hbm,
    *refs,
):
    chunks = len(orders)
    outs = (refs[chunks : 2 * chunks], refs[:chunks])
    (
        inputs_ref,
        embed_in_ref,
        embed_out_ref,
        values_ref,
        latent,
        staged,
        edge_of,
        filled,
        crowded_of,
        crowded,
        load_sems,
        store_sems,
    ) = refs[2 * chunks :]
    rows = values_ref.shape[1]
    edges = src_ref.shape[0]
    slots = edges // capacity
    pairs = slots // 2
    loads = [
        pltpu.make_async_copy(source, target, load_sems.at[index])
        for index, (source, target) in enumerate(
            (
                (inputs_hbm, inputs_ref),
                (embed_in_hbm, embed_in_ref),
                (embed_out_hbm, embed_out_ref),
                (values_hbm, values_ref),
            )
        )
    ]
    for load in loads:
        load.start()

    me = lax.axis_index("space")

    def clear(bin_, carry):
        filled[bin_] = 0
        for index in range(2):
            edge_of[bin_ * capacity + index] = 0
        return carry

    def clear_pair(pair, carry):
        crowded[pair] = 0
        return carry

    lax.fori_loop(0, slots * held, clear, 0)
    lax.fori_loop(0, pairs, clear_pair, 0)

    def sort(edge, carry):
        bin_ = place_ref[dst_ref[edge]] ^ (me * held)
        count = filled[bin_]
        edge_of[bin_ * capacity + count] = edge
        filled[bin_] = count + 1

        @pl.when(count == 2)
        def _():
            pair = lax.div(bin_, 2 * held)
            seen = crowded[pair]
            crowded_of[pair * 2 * held + seen] = bin_
            crowded[pair] = seen + 1

        return carry

    lax.fori_loop(0, edges, sort, 0)

    for load in loads[:3]:
        load.wait()

    def embed(tile, carry):
        first = pl.multiple_of(tile * tile_rows, tile_rows)
        columns = inputs_ref[:, pl.ds(first, tile_rows)]
        hidden = silu(transposed_matmul(columns, embed_in_ref[...])).astype(jnp.bfloat16)
        scaled = normalize(matmul(hidden, embed_out_ref[...])) * gain_ref[...]
        row = first + lax.broadcasted_iota(jnp.int32, (tile_rows, 1), 0)
        latent[pl.ds(first, tile_rows), :] = jnp.where(row < count_ref[0], scaled, 0.0).astype(jnp.bfloat16)
        return carry

    lax.fori_loop(0, latent.shape[0] // tile_rows, embed, 0)
    loads[3].wait()

    def stores(pair):
        copies = []
        for side in range(2):
            first = 0
            for chunk, order in enumerate(orders):
                count = held * cuts[chunk]
                start = pl.multiple_of(place_of(pair, order) * count, count)
                copies.append(
                    pltpu.make_async_copy(
                        staged.at[pair, side, pl.ds(first, count), :],
                        outs[side][chunk].at[pl.ds(start, count), :],
                        store_sems.at[pair, side, chunk],
                    )
                )
                first += count
        return copies

    def product(bin_, first, count):
        operator = []
        sources = []
        for index in range(first, first + 2):
            edge = jnp.where(count > index, edge_of[bin_ * capacity + index], 0)
            values = values_ref[edge]
            operator.append(jnp.where(count > index, values, jnp.zeros_like(values)))
            start = pl.multiple_of(src_ref[edge] * rows, rows)
            sources.append(latent[pl.ds(start, rows), :])
        return matmul(jnp.concatenate(operator, axis=1), jnp.concatenate(sources, axis=0))

    def stage(pair, side, block, summed):
        top = 0
        for cut in cuts:
            first = pl.multiple_of(top * held + block * cut, 16)
            staged[pair, side, pl.ds(first, cut), :] = summed[top : top + cut].astype(jnp.bfloat16)
            top += cut

    def multiply(pair, carry):
        for side in range(2):
            for block in range(held):
                bin_ = (2 * pair + side) * held + block
                stage(pair, side, block, product(bin_, 0, filled[bin_]))

        def revisit(index, carry):
            bin_ = crowded_of[pair * 2 * held + index]
            count = filled[bin_]
            summed = product(bin_, 0, count)
            for first in range(2, capacity, 2):
                summed = summed + product(bin_, first, count)
            stage(pair, lax.div(lax.rem(bin_, 2 * held), held), lax.rem(bin_, held), summed)
            return carry

        lax.fori_loop(0, crowded[pair], revisit, 0)
        for copy in stores(pair):
            copy.start()
        return carry

    lax.fori_loop(0, pairs, multiply, 0)

    def finish(pair, carry):
        for copy in stores(pair):
            copy.wait()
        return carry

    lax.fori_loop(0, pairs, finish, 0)


def slab_sums(
    grid_inputs,
    grid_count,
    embed_in,
    embed_out,
    grid_gain,
    g2m_values,
    g2m_src,
    g2m_dst,
    mesh_place,
    partitions,
    orders,
    cuts,
):
    slab_rows = grid_inputs.shape[1]
    channels = embed_out.shape[1]
    edges, rows, _ = g2m_values.shape
    held = mesh_place.shape[0] // partitions
    capacity = edges // partitions
    pairs = partitions // 2
    shapes = [jax.ShapeDtypeStruct((pairs * held * cut, channels), jnp.bfloat16) for cut in cuts]
    return pl.pallas_call(
        functools.partial(grid_kernel, held, capacity, orders, cuts, min(512, slab_rows)),
        in_specs=[SMEM] * 4 + [VMEM] + [ANY] * 4,
        out_specs=[ANY] * (2 * len(cuts)),
        out_shape=shapes * 2,
        scratch_shapes=[
            pltpu.VMEM(grid_inputs.shape, jnp.bfloat16),
            pltpu.VMEM(embed_in.shape, jnp.bfloat16),
            pltpu.VMEM(embed_out.shape, jnp.bfloat16),
            pltpu.VMEM(g2m_values.shape, jnp.bfloat16),
            pltpu.VMEM((slab_rows, channels), jnp.bfloat16),
            pltpu.VMEM((pairs, 2, held * rows, channels), jnp.bfloat16),
            pltpu.SMEM((partitions * held * capacity,), jnp.int32),
            pltpu.SMEM((partitions * held,), jnp.int32),
            pltpu.SMEM((partitions * held,), jnp.int32),
            pltpu.SMEM((pairs,), jnp.int32),
            pltpu.SemaphoreType.DMA((4,)),
            pltpu.SemaphoreType.DMA((pairs, 2, len(cuts))),
        ],
        compiler_params=pltpu.CompilerParams(vmem_limit_bytes=GRID_VMEM_BYTES),
        name="grid_to_mesh",
    )(
        g2m_src,
        g2m_dst,
        mesh_place,
        grid_count,
        grid_gain.reshape(1, -1),
        grid_inputs,
        embed_in,
        embed_out,
        g2m_values,
    )


def exchange(cells, bit):
    count = lax.axis_size("space")
    return lax.ppermute(cells, "space", [(i, i ^ (1 << bit)) for i in range(count)])


def reduce_chunks(mates, owns, orders, turns, lists):
    arrived = [exchange(mate, 0) for mate in mates]
    kept = list(owns)
    made = [0] * len(orders)
    for turn, chunk in enumerate(turns):
        received = arrived[chunk]
        if turn == len(orders):
            received, _, lists = lax.optimization_barrier((received, previous, lists))
        elif turn > 0:
            received, _ = lax.optimization_barrier((received, previous))
        half = kept[chunk].shape[0] // 2
        previous = add(received[half:], kept[chunk][half:]).astype(jnp.bfloat16)
        kept[chunk] = add(received[:half], kept[chunk][:half]).astype(jnp.bfloat16)
        arrived[chunk] = exchange(previous, orders[chunk][made[chunk]])
        made[chunk] += 1
    return arrived, kept, lists


def node_kernel(parts, reads, rows, mate_list_ref, other_list_ref, *refs):
    summands = refs[:parts]
    node_in_ref, node_out_ref, gain_ref, encoded_ref, to_mate_ref, to_other_ref = refs[parts:]
    if parts == 1:
        summed = summands[0][...]
    else:
        chunks = parts // 2
        held = encoded_ref.shape[0] // rows
        pieces = [add(summands[chunk][...], summands[chunks + chunk][...]) for chunk in range(chunks)]
        cuts = [piece.shape[0] // held for piece in pieces]
        summed = jnp.concatenate(
            [
                piece[block * cut : (block + 1) * cut]
                for block in range(held)
                for piece, cut in zip(pieces, cuts)
            ],
            axis=0,
        )
    hidden = silu(matmul(summed.astype(jnp.bfloat16), node_in_ref[...])).astype(jnp.bfloat16)
    encoded_ref[...] = (summed + gain_ref[...] * normalize(matmul(hidden, node_out_ref[...]))).astype(jnp.bfloat16)
    odd = lax.rem(lax.axis_index("space"), 2)
    for index in range(reads):
        for wanted_ref, first, out in (
            (mate_list_ref, odd * reads, to_mate_ref),
            (other_list_ref, (1 - odd) * reads, to_other_ref),
        ):
            start = pl.multiple_of(wanted_ref[0, first + index] * rows, rows)
            out[index * rows : (index + 1) * rows, :] = encoded_ref[pl.ds(start, rows), :]


def encode(summands, node_in, node_out, node_gain, lists, held, rows):
    channels = node_in.shape[0]
    reads = lists[0].shape[1] // 2
    return pl.pallas_call(
        functools.partial(node_kernel, len(summands), reads, rows),
        in_specs=[SMEM] * 2 + [VMEM] * (len(summands) + 3),
        out_specs=[VMEM] * 3,
        out_shape=[
            jax.ShapeDtypeStruct((held * rows, channels), jnp.bfloat16),
            jax.ShapeDtypeStruct((reads * rows, channels), jnp.bfloat16),
            jax.ShapeDtypeStruct((reads * rows, channels), jnp.bfloat16),
        ],
        compiler_params=pltpu.CompilerParams(vmem_limit_bytes=VMEM_BYTES),
        name="node_update",
    )(*lists, *summands, node_in, node_out, node_gain.reshape(1, -1))


def process_kernel(
    held,
    reads,
    dst_ref,
    src_ref,
    encoded_ref,
    mate_ref,
    other_ref,
    values_ref,
    proc_in_ref,
    proc_out_ref,
    gain_ref,
    processed_ref,
    frame,
):
    edges, rows, _ = values_ref.shape
    frame[: reads * rows, :] = mate_ref[...]
    frame[reads * rows : 2 * reads * rows, :] = other_ref[...]
    frame[2 * reads * rows :, :] = encoded_ref[...]
    odd = lax.rem(lax.axis_index("space"), 2)
    operator = []
    sources = []
    for edge in range(edges):
        values = values_ref[edge]
        zeros = jnp.zeros_like(values)
        local = dst_ref[edge]
        operator.append(
            jnp.concatenate([jnp.where(local == block, values, zeros) for block in range(held)], axis=0)
        )
        side = lax.div(src_ref[edge], held)
        index = lax.rem(src_ref[edge], held)
        across = (odd + lax.div(side, 2) + 1) & 1
        at = jnp.where(side == 1, 2 * reads, across * reads) + index
        start = pl.multiple_of(at * rows, rows)
        sources.append(frame[pl.ds(start, rows), :])
    message = matmul(jnp.concatenate(operator, axis=1), jnp.concatenate(sources, axis=0))
    hidden = silu(matmul(message.astype(jnp.bfloat16), proc_in_ref[...])).astype(jnp.bfloat16)
    update = gain_ref[...] * normalize(matmul(hidden, proc_out_ref[...]))
    processed_ref[...] = (encoded_ref[...].astype(jnp.float32) + update).astype(jnp.bfloat16)


def process(encoded, from_mate, from_other, mesh_values, mesh_dst, mesh_src, proc_in, proc_out, proc_gain, held, reads):
    rows = mesh_values.shape[1]
    return pl.pallas_call(
        functools.partial(process_kernel, held, reads),
        in_specs=[SMEM] * 2 + [VMEM] * 7,
        out_specs=VMEM,
        out_shape=jax.ShapeDtypeStruct(encoded.shape, jnp.bfloat16),
        scratch_shapes=[pltpu.VMEM(((2 * reads + held) * rows, encoded.shape[1]), jnp.bfloat16)],
        compiler_params=pltpu.CompilerParams(vmem_limit_bytes=VMEM_BYTES),
        name="process",
    )(mesh_dst, mesh_src, encoded, from_mate, from_other, mesh_values, proc_in, proc_out, proc_gain.reshape(1, -1))


def lookup(table, wanted):
    matches = wanted[:, None] == jnp.arange(table.shape[0], dtype=jnp.int32)[None, :]
    return jnp.sum(jnp.where(matches, table[None, :], 0), axis=1)


def routed_sum(
    grid_inputs, grid_count, embed_in, embed_out, grid_gain, g2m_values, g2m_src, g2m_dst, mesh_place, partitions
):
    slab_rows = grid_inputs.shape[1]
    edge_count, block_rows, _ = g2m_values.shape
    channels = embed_out.shape[1]
    held = mesh_place.shape[0] // partitions
    capacity = max(1, (edge_count + partitions - 1) // partitions)
    slot_count = partitions * capacity
    hidden = jax.nn.silu(transposed_matmul(grid_inputs, embed_in)).astype(jnp.bfloat16)
    alive = lax.iota(jnp.int32, slab_rows) < grid_count[0]
    latent = jnp.where(alive[:, None], normalize(matmul(hidden, embed_out)) * grid_gain, 0.0).astype(jnp.bfloat16)
    positions = lookup(mesh_place, g2m_dst)
    targets = positions // held
    ranking = jnp.sum(jnp.tril(targets[:, None] == targets[None, :], -1), axis=1)
    slot_index = targets * capacity + ranking
    labels = jnp.full((slot_count,), -1, jnp.int32).at[slot_index].set(positions % held)
    sources = latent.reshape(slab_rows // block_rows, block_rows, channels)[g2m_src]
    terms = jnp.einsum("eij,ejd->eid", g2m_values, sources, preferred_element_type=jnp.float32).astype(jnp.bfloat16)
    outgoing = jnp.zeros((slot_count, block_rows, channels), jnp.bfloat16).at[slot_index].set(terms)
    arrived = lax.all_to_all(outgoing, "space", split_axis=0, concat_axis=0, tiled=True)
    arrived_labels = lax.all_to_all(labels, "space", split_axis=0, concat_axis=0, tiled=True)
    selector = (arrived_labels[None, :] == jnp.arange(held, dtype=jnp.int32)[:, None]).astype(jnp.bfloat16)
    return matmul(selector, arrived.reshape(slot_count, -1)).reshape(held * block_rows, channels)


def shards(
    grid_inputs,
    grid_count,
    embed_in,
    embed_out,
    grid_gain,
    g2m_values,
    g2m_src,
    g2m_dst,
    mesh_place,
    node_in,
    node_out,
    node_gain,
    recv_blocks,
    mesh_values,
    mesh_dst,
    mesh_src,
    proc_in,
    proc_out,
    proc_gain,
):
    partitions = lax.axis_size("space")
    edges, rows, _ = g2m_values.shape
    mesh_blocks = mesh_place.shape[0]
    held = mesh_blocks // partitions
    reads = recv_blocks.shape[1] // 2
    mates = [(i, i ^ 1) for i in range(partitions)]
    others = [(i, (i + 1 if i % 2 else i - 1) % partitions) for i in range(partitions)]
    lists = (lax.ppermute(recv_blocks, "space", mates), lax.ppermute(recv_blocks, "space", others))
    grid_args = (grid_inputs, grid_count, embed_in, embed_out, grid_gain, g2m_values, g2m_src, g2m_dst, mesh_place)
    if partitions == 1 << (1 + len(ORDERS[0])) and edges % partitions == 0 and edges >= mesh_blocks:
        cuts = [share * rows // sum(SHARES) for share in SHARES]
        sums = slab_sums(*grid_args, partitions, ORDERS, cuts)
        arrived, kept, lists = reduce_chunks(sums[: len(cuts)], sums[len(cuts) :], ORDERS, TURNS, lists)
        summands = arrived + kept
    else:
        summands = [routed_sum(*grid_args, partitions)]
    encoded, to_mate, to_other = encode(summands, node_in, node_out, node_gain, lists, held, rows)
    from_other = lax.ppermute(to_other, "space", others)
    from_mate = lax.ppermute(to_mate, "space", mates)
    processed = process(
        encoded, from_mate, from_other, mesh_values, mesh_dst, mesh_src, proc_in, proc_out, proc_gain, held, reads
    )
    return (encoded, processed)


def solution(mesh):
    return jax.shard_map(
        shards,
        mesh=mesh,
        in_specs=(
            P(None, ("groups", "space")),
            P("space"),
            P(),
            P(),
            P(),
            P("space", None, None),
            P("space"),
            P("space"),
            P(),
            P(),
            P(),
            P(),
            P("space", None),
            P("space", None, None),
            P("space"),
            P("space"),
            P(),
            P(),
            P(),
        ),
        out_specs=(P(("groups", "space"), None), P(("groups", "space"), None)),
        check_vma=False,
    )
```

time: 103 us -> 93.9 us (0.912)
  Pallas kernels: 25.7 us -> 17.9 us
  waiting for transfers between devices: 42.3 us -> 45.4 us
  other arithmetic: 6.29 us -> 3.26 us
  starting transfers between devices: 25.7 us -> 24 us
    ppermute x16 -> x20, waiting for transfers between devices: 29.9 us -> 39.8 us  [exchange(): lax.ppermute(cells, 'space', [(i, i ^ 1 << bit) for i in range(count)])]
    ppermute x4, waiting for transfers between devices: 12.3 us -> 5.54 us  [the longest x1 5.53 us: shards(): from_other = lax.ppermute(to_other, 'space', others)]
    pallas_call x1, Pallas kernels: 17.8 us -> 12.2 us  [slab_sums(): pl.pallas_call(functools.partial(grid_kernel, held, capacity, orders, cut...]
    ppermute x16 -> x20, starting transfers between devices: 20 us -> 15 us  [exchange(): lax.ppermute(cells, 'space', [(i, i ^ 1 << bit) for i in range(count)])]
    ppermute x4, starting transfers between devices: 5.72 us -> 9.08 us  [the longest x1 5.93 us: shards(): lax.ppermute(recv_blocks, 'space', others)]
    convert_element_type x12 -> x15, other arithmetic: 5.73 us -> 3.26 us  [the longest x13 3.05 us: reduce_chunks(): kept[chunk] = add(received[:half], kept[chunk][:half]).astype(jnp.bfloat16)]
    pallas_call x1, Pallas kernels: 3.58 us -> 2.35 us  [encode(): pl.pallas_call(functools.partial(node_kernel, len(summands), reads, rows)...]
    pallas_call x1, Pallas kernels: 4.36 us -> 3.27 us  [process(): pl.pallas_call(functools.partial(process_kernel, held, reads), in_specs=[...]
  transfers between devices with their start and end apart: 20 -> 24, of which waited for: 13 -> 9; matrix products, arithmetic and copies ran while one was open for 6% -> 3% of each run, Pallas kernels for 0% -> 0%
where the time goes in v2:
time: 93.9 us; the launch traced here: 93.5 us
  waiting for transfers between devices  45.4 us (48%)
  starting transfers between devices  24 us (26%)
  Pallas kernels  17.9 us (19%)
  other arithmetic  3.26 us (3%)
  between operations  1.67 us (2%)
  local copies, waits for them, and re-layouts  1.31 us (1%)
    ppermute x20, waiting for transfers between devices, exchange(): lax.ppermute(cells, 'space', [(i, i ^ 1 << bit) for i in range(count)])  39.8 us
    ppermute x20, starting transfers between devices, exchange(): lax.ppermute(cells, 'space', [(i, i ^ 1 << bit) for i in range(count)])  15 us
    pallas_call x1, Pallas kernels, slab_sums(): pl.pallas_call(functools.partial(grid_kernel, held, capacity, orders, cut...  12.2 us
    ppermute x1, starting transfers between devices, shards(): lax.ppermute(recv_blocks, 'space', others)  5.93 us
    ppermute x1, waiting for transfers between devices, shards(): from_other = lax.ppermute(to_other, 'space', others)  5.53 us
    pallas_call x1, Pallas kernels, process(): pl.pallas_call(functools.partial(process_kernel, held, reads), in_specs=[...  3.27 us
    ppermute x1, starting transfers between devices, shards(): from_other = lax.ppermute(to_other, 'space', others)  3.07 us
    convert_element_type x13, other arithmetic, reduce_chunks(): kept[chunk] = add(received[:half], kept[chunk][:half]).astype(jnp.bfloat16)  3.05 us
  transfers between devices with their start and end apart: 24, of which 9 were waited for; matrix products, arithmetic and copies ran while one was open for 3% of the time, Pallas kernels for 0%

profile of v2, /device:TPU:0, one launch (start us, length us, event | category | flops | bytes accessed | tf_op | source)
XLA Modules:
  0.0 93.5 jit_solution(9165362603302405861)
XLA Ops:
  1.3 12.2 %grid_to_mesh.1 = (bf16[1024,512]{1,0:T(8,128)(2,1)}, bf16[1024,512]{1,0:T(8,128)(2,1)}, bf16[1024,512]{1,0:T(8,128)(2,1)}, bf16[512,512]{1,0:T(8,128)(2,1)}, bf...) custom-call(s32[64]{0:T(128)} %src_ref.2, ...), custom_call_target="tpu_custom_call" | custom-call | tf_op jit(solution)/shard_map/grid_to_mesh/pallas_call | solution.py:236
  13.6 0.0 copy-start.14
  13.6 0.8 collective-permute-start
  14.4 0.1 collective-permute-start.5
  14.4 0.4 collective-permute-start.4
  14.9 0.1 collective-permute-start.6
  15.0 5.9 %collective-permute-start.7 = (s32[1,4]{1,0:T(1,128)S(1)}, s32[1,4]{1,0:T(1,128)S(1)}, u32[]{:S(2)}, u32[]{:S(2)}) collective-permute-start(s32[1,4]{1,0:T(1,128)S(1)} %copy-done.15), channel_id=1, source_target_pairs={{0,15},{1,2},{2,1},{3,4},{4,3},{5,6},{6,5},{7,8},{8,7},{9,10},{10,... | collective-permute-start | bytes 56 | tf_op jit(solution)/shard_map/ppermute | solution.py:453
  20.9 1.5 %add_convert_fusion.2 = (bf16[512,512]{1,0:T(8,128)(2,1)S(1)}, bf16[512,512]{1,0:T(8,128)(2,1)S(1)}) fusion(bf16[1024,512]{1,0:T(8,128)(2,1)S(1)} %collective-permute-done, bf16[1024,512]{1,0:T(8,128)(2,1)} %get-tuple-element.32), kind=kLoop, calls=%fused_computation.2 | loop fusion | flops 2097152 | bytes 3145728 | tf_op jit(solution)/shard_map/convert_element_type | solution.py:287
  22.4 0.6 collective-permute-start.2
  23.0 0.3 add_convert_fusion.1
  23.3 0.0 collective-permute-done.4
  23.3 0.1 collective-permute-start.1
  23.4 0.2 copy-done.10
  23.6 0.3 add_convert_fusion
  24.0 1.9 %collective-permute-start.11 = (bf16[512,512]{1,0:T(8,128)(2,1)S(1)}, bf16[512,512]{1,0:T(8,128)(2,1)S(1)}, u32[]{:S(2)}, u32[]{:S(2)}) collective-permute-start(bf16[512,512]{1,0:T(8,128)(2,1)S(1)} %get-tuple-element.61), channel_id=1, source_target_pairs={{0,2},{1,3},{2,0},{3,1},{4,6},{5,7},{6,4},{7,5},{8,10},{9,11},{10,... | collective-permute-start | bytes 1572872 | tf_op jit(solution)/shard_map/ppermute | solution.py:272
  25.8 0.1 add_convert_fusion.12
  26.0 0.0 collective-permute-done.2
  26.0 0.1 collective-permute-start.12
  26.1 0.1 add_convert_fusion.9
  26.2 2.2 %collective-permute-start.10 = (bf16[512,512]{1,0:T(8,128)(2,1)S(1)}, bf16[512,512]{1,0:T(8,128)(2,1)S(1)}, u32[]{:S(2)}, u32[]{:S(2)}) collective-permute-start(bf16[512,512]{1,0:T(8,128)(2,1)S(1)} %get-tuple-element.63), channel_id=1, source_target_pairs={{0,8},{1,9},{2,10},{3,11},{4,12},{5,13},{6,14},{7,15},{8,0},{9,1},... | collective-permute-start | bytes 1572872 | tf_op jit(solution)/shard_map/ppermute | solution.py:272
  28.5 0.3 collective-permute-start.9
  28.7 9.5 %collective-permute-done.1 = bf16[512,512]{1,0:T(8,128)(2,1)S(1)} collective-permute-done((bf16[512,512]{1,0:T(8,128)(2,1)S(1)}, bf16[512,512]{1,0:T(8,128)(2,1)S(1)}, u32[]{:S(2)}, u32[]{:S(2)}) %collective-permute-start.1) | collective-permute-done | bytes 524320 | tf_op jit(solution)/shard_map/ppermute | solution.py:272
  38.2 0.1 add_convert_fusion.13
  38.3 0.1 collective-permute-start.8
  38.5 1.6 %collective-permute-done.12 = bf16[256,512]{1,0:T(8,128)(2,1)S(1)} collective-permute-done((bf16[256,512]{1,0:T(8,128)(2,1)S(1)}, bf16[256,512]{1,0:T(8,128)(2,1)S(1)}, u32[]{:S(2)}, u32[]{:S(2)}) %collective-permute-start.12) | collective-permute-done | bytes 262176 | tf_op jit(solution)/shard_map/ppermute | solution.py:272
  40.0 0.1 add_convert_fusion.23
  40.1 0.8 collective-permute-start.15
  41.0 8.5 %collective-permute-done.11 = bf16[512,512]{1,0:T(8,128)(2,1)S(1)} collective-permute-done((bf16[512,512]{1,0:T(8,128)(2,1)S(1)}, bf16[512,512]{1,0:T(8,128)(2,1)S(1)}, u32[]{:S(2)}, u32[]{:S(2)}) %collective-permute-start.11) | collective-permute-done | bytes 524320 | tf_op jit(solution)/shard_map/ppermute | solution.py:272
  49.4 0.1 add_convert_fusion.6
  49.6 0.1 collective-permute-start.17
  49.7 9.4 %collective-permute-done.10 = bf16[512,512]{1,0:T(8,128)(2,1)S(1)} collective-permute-done((bf16[512,512]{1,0:T(8,128)(2,1)S(1)}, bf16[512,512]{1,0:T(8,128)(2,1)S(1)}, u32[]{:S(2)}, u32[]{:S(2)}) %collective-permute-start.10) | collective-permute-done | bytes 524320 | tf_op jit(solution)/shard_map/ppermute | solution.py:272
  59.0 0.1 add_convert_fusion.8
  59.2 0.0 copy-start
  59.2 0.0 copy-start.1
  59.2 0.0 copy-start.6
  59.2 1.1 %collective-permute-start.14 = (bf16[256,512]{1,0:T(8,128)(2,1)S(1)}, bf16[256,512]{1,0:T(8,128)(2,1)S(1)}, u32[]{:S(2)}, u32[]{:S(2)}) collective-permute-start(bf16[256,512]{1,0:T(8,128)(2,1)S(1)} %get-tuple-element.69), channel_id=1, source_target_pairs={{0,2},{1,3},{2,0},{3,1},{4,6},{5,7},{6,4},{7,5},{8,10},{9,11},{10,... | collective-permute-start | bytes 786440 | tf_op jit(solution)/shard_map/ppermute | solution.py:272
  60.3 0.0 collective-permute-done.9
  60.3 0.1 add_convert_fusion.24
  60.3 1.1 %collective-permute-start.13 = (bf16[128,512]{1,0:T(8,128)(2,1)S(1)}, bf16[128,512]{1,0:T(8,128)(2,1)S(1)}, u32[]{:S(2)}, u32[]{:S(2)}) collective-permute-start(bf16[128,512]{1,0:T(8,128)(2,1)S(1)} %get-tuple-element.84), channel_id=1, source_target_pairs={{0,2},{1,3},{2,0},{3,1},{4,6},{5,7},{6,4},{7,5},{8,10},{9,11},{10,... | collective-permute-start | bytes 393224 | tf_op jit(solution)/shard_map/ppermute | solution.py:272
  61.4 0.0 collective-permute-done.15
  61.5 4.2 %collective-permute-done.14 = bf16[256,512]{1,0:T(8,128)(2,1)S(1)} collective-permute-done((bf16[256,512]{1,0:T(8,128)(2,1)S(1)}, bf16[256,512]{1,0:T(8,128)(2,1)S(1)}, u32[]{:S(2)}, u32[]{:S(2)}) %collective-permute-start.14) | collective-permute-done | bytes 262176 | tf_op jit(solution)/shard_map/ppermute | solution.py:272
  65.6 0.1 add_convert_fusion.16
  65.7 0.0 copy-start.2
  65.7 0.0 copy-start.3
  65.7 0.0 copy-start.5
  65.7 0.0 copy-start.7
  65.8 0.0 copy-start.8
  65.8 0.0 copy-start.9
  65.8 1.3 %collective-permute-done.13 = bf16[128,512]{1,0:T(8,128)(2,1)S(1)} collective-permute-done((bf16[128,512]{1,0:T(8,128)(2,1)S(1)}, bf16[128,512]{1,0:T(8,128)(2,1)S(1)}, u32[]{:S(2)}, u32[]{:S(2)}) %collective-permute-start.13) | collective-permute-done | bytes 131104 | tf_op jit(solution)/shard_map/ppermute | solution.py:272
  67.1 0.1 add_convert_fusion.18
  67.2 0.1 add_convert_fusion.17
  67.3 0.1 collective-permute-start.18
  67.3 2.4 %collective-permute-start.16 = (bf16[128,512]{1,0:T(8,128)(2,1)S(1)}, bf16[128,512]{1,0:T(8,128)(2,1)S(1)}, u32[]{:S(2)}, u32[]{:S(2)}) collective-permute-start(bf16[128,512]{1,0:T(8,128)(2,1)S(1)} %get-tuple-element.81), channel_id=1, source_target_pairs={{0,4},{1,5},{2,6},{3,7},{4,0},{5,1},{6,2},{7,3},{8,12},{9,13},{10,... | collective-permute-start | bytes 393224 | tf_op jit(solution)/shard_map/ppermute | solution.py:272
  69.7 0.0 collective-permute-start.19
  69.7 2.5 %collective-permute-start.20 = (bf16[64,512]{1,0:T(8,128)(2,1)S(1)}, bf16[64,512]{1,0:T(8,128)(2,1)S(1)}, u32[]{:S(2)}, u32[]{:S(2)}) collective-permute-start(bf16[64,512]{1,0:T(8,128)(2,1)S(1)} %get-tuple-element.89), channel_id=1, source_target_pairs={{0,8},{1,9},{2,10},{3,11},{4,12},{5,13},{6,14},{7,15},{8,0},{9,1},... | collective-permute-start | bytes 196616 | tf_op jit(solution)/shard_map/ppermute | solution.py:272
  72.3 0.4 collective-permute-start.21
  72.7 2.3 %collective-permute-done.20.refs_3_ = bf16[64,512]{1,0:T(8,128)(2,1)S(1)} collective-permute-done((bf16[64,512]{1,0:T(8,128)(2,1)S(1)}, bf16[64,512]{1,0:T(8,128)(2,1)S(1)}, u32[]{:S(2)}, u32[]{:S(2)}) %collective-permute-start.20) | collective-permute-done | bytes 65568 | tf_op jit(solution)/shard_map/ppermute | solution.py:272
  75.0 3.2 %collective-permute-done.21.refs_4_ = bf16[64,512]{1,0:T(8,128)(2,1)S(1)} collective-permute-done((bf16[64,512]{1,0:T(8,128)(2,1)S(1)}, bf16[64,512]{1,0:T(8,128)(2,1)S(1)}, u32[]{:S(2)}, u32[]{:S(2)}) %collective-permute-start.21) | collective-permute-done | bytes 65568 | tf_op jit(solution)/shard_map/ppermute | solution.py:272
  78.2 2.4 %node_update.1 = (bf16[512,512]{1,0:T(8,128)(2,1)}, bf16[256,512]{1,0:T(8,128)(2,1)S(1)}, bf16[256,512]{1,0:T(8,128)(2,1)S(1)}) custom-call(s32[1,4]{1,0:T(1,128)S(1)} %collective-permute-done.6.mate_list_ref, s32[1,4]{1,0:T(1,128)S(1)} %collective-permute-done.7.other_list_ref, bf16[128,512]{1,0:T(8,128)(2,1)S(1)} %collective-permute-done.16.refs_0_, ...), custom_call_target="tpu_custom_call" | custom-call | tf_op jit(solution)/shard_map/node_update/pallas_call | solution.py:326
  80.6 3.1 %collective-permute-start.23 = (bf16[256,512]{1,0:T(8,128)(2,1)S(1)}, bf16[256,512]{1,0:T(8,128)(2,1)S(1)}, u32[]{:S(2)}, u32[]{:S(2)}) collective-permute-start(bf16[256,512]{1,0:T(8,128)(2,1)S(1)} %get-tuple-element.59), channel_id=1, source_target_pairs={{0,15},{1,2},{2,1},{3,4},{4,3},{5,6},{6,5},{7,8},{8,7},{9,10},{10,... | collective-permute-start | bytes 786440 | tf_op jit(solution)/shard_map/ppermute | solution.py:463
  83.6 5.5 %collective-permute-done.23.other_ref = bf16[256,512]{1,0:T(8,128)(2,1)S(1)} collective-permute-done((bf16[256,512]{1,0:T(8,128)(2,1)S(1)}, bf16[256,512]{1,0:T(8,128)(2,1)S(1)}, u32[]{:S(2)}, u32[]{:S(2)}) %collective-permute-start.23) | collective-permute-done | bytes 262176 | tf_op jit(solution)/shard_map/ppermute | solution.py:463
  89.2 0.0 copy-start.4
  89.2 1.0 %copy-done.4 = bf16[512,512]{1,0:T(8,128)(2,1)S(1)} copy-done((bf16[512,512]{1,0:T(8,128)(2,1)S(1)}, bf16[512,512]{1,0:T(8,128)(2,1)}, u32[]{:S(2)}) %copy-start.4) | copy-done | bytes 524312
  90.3 3.3 %process.1 = bf16[512,512]{1,0:T(8,128)(2,1)} custom-call(s32[12]{0:T(128)S(1)} %copy-done.8, s32[12]{0:T(128)S(1)} %copy-done.9, bf16[512,512]{1,0:T(8,128)(2,1)S(1)} %copy-done.4, bf16[256,512]{1,0:T(8,128)(2,1)S(1)} %collective-permute-done.22.mate_ref, bf16[256,512]{1,0:T(8,128)(2,1)S(1)} %collective-permute-done.23.other_ref, ...), custom_call_target="tpu_custom_call" | custom-call | tf_op jit(solution)/shard_map/process/pallas_call | solution.py:383
  (34 shorter events, 0.1 us)
Async XLA Ops:
  0.6 14.2 %copy-start.15 = (s32[1,4]{1,0:T(1,128)S(1)}, s32[1,4]{1,0:T(1,128)}, u32[]{:S(2)}) copy-start(s32[1,4]{1,0:T(1,128)} %param.31) | copy-start | bytes 52
  13.6 8.9 %copy-start.14 = (bf16[512,512]{1,0:T(8,128)(2,1)S(1)}, bf16[512,512]{1,0:T(8,128)(2,1)}, u32[]{:S(2)}) copy-start(bf16[512,512]{1,0:T(8,128)(2,1)} %get-tuple-element.33) | copy-start | bytes 1572868
  13.6 9.4 %copy-start.11 = (bf16[1024,512]{1,0:T(8,128)(2,1)S(1)}, bf16[1024,512]{1,0:T(8,128)(2,1)}, u32[]{:S(2)}) copy-start(bf16[1024,512]{1,0:T(8,128)(2,1)} %get-tuple-element.38) | copy-start | bytes 3145732
  13.6 7.3 %collective-permute-start = (bf16[1024,512]{1,0:T(8,128)(2,1)}, bf16[1024,512]{1,0:T(8,128)(2,1)S(1)}, u32[]{:S(2)}, u32[]{:S(2)}) collective-permute-start(bf16[1024,512]{1,0:T(8,128)(2,1)} %get-tuple-element.31), channel_id=1, source_target_pairs={{0,1},{1,0},{2,3},{3,2},{4,5},{5,4},{6,7},{7,6},{8,9},{9,8},{10,11... | collective-permute-start | bytes 3145736 | tf_op jit(solution)/shard_map/ppermute | solution.py:272
  14.4 8.0 %collective-permute-start.5 = (bf16[1024,512]{1,0:T(8,128)(2,1)}, bf16[1024,512]{1,0:T(8,128)(2,1)S(1)}, u32[]{:S(2)}, u32[]{:S(2)}) collective-permute-start(bf16[1024,512]{1,0:T(8,128)(2,1)} %get-tuple-element.36), channel_id=1, source_target_pairs={{0,1},{1,0},{2,3},{3,2},{4,5},{5,4},{6,7},{7,6},{8,9},{9,8},{10,11... | collective-permute-start | bytes 3145736 | tf_op jit(solution)/shard_map/ppermute | solution.py:272
  14.4 8.9 %collective-permute-start.4 = (bf16[1024,512]{1,0:T(8,128)(2,1)}, bf16[1024,512]{1,0:T(8,128)(2,1)S(1)}, u32[]{:S(2)}, u32[]{:S(2)}) collective-permute-start(bf16[1024,512]{1,0:T(8,128)(2,1)} %get-tuple-element.35), channel_id=1, source_target_pairs={{0,1},{1,0},{2,3},{3,2},{4,5},{5,4},{6,7},{7,6},{8,9},{9,8},{10,11... | collective-permute-start | bytes 3145736 | tf_op jit(solution)/shard_map/ppermute | solution.py:272
  14.9 11.4 %collective-permute-start.6 = (s32[1,4]{1,0:T(1,128)S(1)}, s32[1,4]{1,0:T(1,128)S(1)}, u32[]{:S(2)}, u32[]{:S(2)}) collective-permute-start(s32[1,4]{1,0:T(1,128)S(1)} %copy-done.15), channel_id=1, source_target_pairs={{0,1},{1,0},{2,3},{3,2},{4,5},{5,4},{6,7},{7,6},{8,9},{9,8},{10,11... | collective-permute-start | bytes 56 | tf_op jit(solution)/shard_map/ppermute | solution.py:453
  15.0 13.5 %collective-permute-start.7 = (s32[1,4]{1,0:T(1,128)S(1)}, s32[1,4]{1,0:T(1,128)S(1)}, u32[]{:S(2)}, u32[]{:S(2)}) collective-permute-start(s32[1,4]{1,0:T(1,128)S(1)} %copy-done.15), channel_id=1, source_target_pairs={{0,15},{1,2},{2,1},{3,4},{4,3},{5,6},{6,5},{7,8},{8,7},{9,10},{10,... | collective-permute-start | bytes 56 | tf_op jit(solution)/shard_map/ppermute | solution.py:453
  20.9 3.1 %collective-permute-start.3 = (bf16[512,512]{1,0:T(8,128)(2,1)}, bf16[512,512]{1,0:T(8,128)(2,1)S(1)}, u32[]{:S(2)}, u32[]{:S(2)}) collective-permute-start(bf16[512,512]{1,0:T(8,128)(2,1)} %get-tuple-element.34), channel_id=1, source_target_pairs={{0,1},{1,0},{2,3},{3,2},{4,5},{5,4},{6,7},{7,6},{8,9},{9,8},{10,11... | collective-permute-start | bytes 1572872 | tf_op jit(solution)/shard_map/ppermute | solution.py:272
  22.4 1.2 %copy-start.10 = (bf16[1024,512]{1,0:T(8,128)(2,1)S(1)}, bf16[1024,512]{1,0:T(8,128)(2,1)}, u32[]{:S(2)}) copy-start(bf16[1024,512]{1,0:T(8,128)(2,1)} %get-tuple-element.40) | copy-start | bytes 3145732
  22.4 3.6 %collective-permute-start.2 = (bf16[512,512]{1,0:T(8,128)(2,1)S(1)}, bf16[512,512]{1,0:T(8,128)(2,1)S(1)}, u32[]{:S(2)}, u32[]{:S(2)}) collective-permute-start(bf16[512,512]{1,0:T(8,128)(2,1)S(1)} %copy-done.14), channel_id=1, source_target_pairs={{0,1},{1,0},{2,3},{3,2},{4,5},{5,4},{6,7},{7,6},{8,9},{9,8},{10,11... | collective-permute-start | bytes 1572872 | tf_op jit(solution)/shard_map/ppermute | solution.py:272
  23.3 2.5 %copy-start.13 = (bf16[512,512]{1,0:T(8,128)(2,1)S(1)}, bf16[512,512]{1,0:T(8,128)(2,1)}, u32[]{:S(2)}) copy-start(bf16[512,512]{1,0:T(8,128)(2,1)} %get-tuple-element.42) | copy-start | bytes 1572868
  23.3 14.9 %collective-permute-start.1 = (bf16[512,512]{1,0:T(8,128)(2,1)S(1)}, bf16[512,512]{1,0:T(8,128)(2,1)S(1)}, u32[]{:S(2)}, u32[]{:S(2)}) collective-permute-start(bf16[512,512]{1,0:T(8,128)(2,1)S(1)} %get-tuple-element.65), channel_id=1, source_target_pairs={{0,2},{1,3},{2,0},{3,1},{4,6},{5,7},{6,4},{7,5},{8,10},{9,11},{10,... | collective-permute-start | bytes 1572872 | tf_op jit(solution)/shard_map/ppermute | solution.py:272
  23.6 2.5 %copy-start.12 = (bf16[512,512]{1,0:T(8,128)(2,1)S(1)}, bf16[512,512]{1,0:T(8,128)(2,1)}, u32[]{:S(2)}) copy-start(bf16[512,512]{1,0:T(8,128)(2,1)} %get-tuple-element.44) | copy-start | bytes 1572868
  24.0 25.5 %collective-permute-start.11 = (bf16[512,512]{1,0:T(8,128)(2,1)S(1)}, bf16[512,512]{1,0:T(8,128)(2,1)S(1)}, u32[]{:S(2)}, u32[]{:S(2)}) collective-permute-start(bf16[512,512]{1,0:T(8,128)(2,1)S(1)} %get-tuple-element.61), channel_id=1, source_target_pairs={{0,2},{1,3},{2,0},{3,1},{4,6},{5,7},{6,4},{7,5},{8,10},{9,11},{10,... | collective-permute-start | bytes 1572872 | tf_op jit(solution)/shard_map/ppermute | solution.py:272
  26.0 14.0 %collective-permute-start.12 = (bf16[256,512]{1,0:T(8,128)(2,1)S(1)}, bf16[256,512]{1,0:T(8,128)(2,1)S(1)}, u32[]{:S(2)}, u32[]{:S(2)}) collective-permute-start(bf16[256,512]{1,0:T(8,128)(2,1)S(1)} %get-tuple-element.71), channel_id=1, source_target_pairs={{0,4},{1,5},{2,6},{3,7},{4,0},{5,1},{6,2},{7,3},{8,12},{9,13},{10,... | collective-permute-start | bytes 786440 | tf_op jit(solution)/shard_map/ppermute | solution.py:272
  26.2 32.8 %collective-permute-start.10 = (bf16[512,512]{1,0:T(8,128)(2,1)S(1)}, bf16[512,512]{1,0:T(8,128)(2,1)S(1)}, u32[]{:S(2)}, u32[]{:S(2)}) collective-permute-start(bf16[512,512]{1,0:T(8,128)(2,1)S(1)} %get-tuple-element.63), channel_id=1, source_target_pairs={{0,8},{1,9},{2,10},{3,11},{4,12},{5,13},{6,14},{7,15},{8,0},{9,1},... | collective-permute-start | bytes 1572872 | tf_op jit(solution)/shard_map/ppermute | solution.py:272
  28.5 31.8 %collective-permute-start.9 = (bf16[256,512]{1,0:T(8,128)(2,1)S(1)}, bf16[256,512]{1,0:T(8,128)(2,1)S(1)}, u32[]{:S(2)}, u32[]{:S(2)}) collective-permute-start(bf16[256,512]{1,0:T(8,128)(2,1)S(1)} %get-tuple-element.73), channel_id=1, source_target_pairs={{0,4},{1,5},{2,6},{3,7},{4,0},{5,1},{6,2},{7,3},{8,12},{9,13},{10,... | collective-permute-start | bytes 786440 | tf_op jit(solution)/shard_map/ppermute | solution.py:272
  38.3 28.7 %collective-permute-start.8 = (bf16[256,512]{1,0:T(8,128)(2,1)S(1)}, bf16[256,512]{1,0:T(8,128)(2,1)S(1)}, u32[]{:S(2)}, u32[]{:S(2)}) collective-permute-start(bf16[256,512]{1,0:T(8,128)(2,1)S(1)} %get-tuple-element.74), channel_id=1, source_target_pairs={{0,8},{1,9},{2,10},{3,11},{4,12},{5,13},{6,14},{7,15},{8,0},{9,1},... | collective-permute-start | bytes 786440 | tf_op jit(solution)/shard_map/ppermute | solution.py:272
  40.1 21.3 %collective-permute-start.15 = (bf16[128,512]{1,0:T(8,128)(2,1)S(1)}, bf16[128,512]{1,0:T(8,128)(2,1)S(1)}, u32[]{:S(2)}, u32[]{:S(2)}) collective-permute-start(bf16[128,512]{1,0:T(8,128)(2,1)S(1)} %get-tuple-element.83), channel_id=1, source_target_pairs={{0,2},{1,3},{2,0},{3,1},{4,6},{5,7},{6,4},{7,5},{8,10},{9,11},{10,... | collective-permute-start | bytes 393224 | tf_op jit(solution)/shard_map/ppermute | solution.py:272
  49.6 17.6 %collective-permute-start.17 = (bf16[256,512]{1,0:T(8,128)(2,1)S(1)}, bf16[256,512]{1,0:T(8,128)(2,1)S(1)}, u32[]{:S(2)}, u32[]{:S(2)}) collective-permute-start(bf16[256,512]{1,0:T(8,128)(2,1)S(1)} %get-tuple-element.67), channel_id=1, source_target_pairs={{0,4},{1,5},{2,6},{3,7},{4,0},{5,1},{6,2},{7,3},{8,12},{9,13},{10,... | collective-permute-start | bytes 786440 | tf_op jit(solution)/shard_map/ppermute | solution.py:272
  59.2 19.0 %copy-start = (bf16[512,512]{1,0:T(8,128)(2,1)S(1)}, bf16[512,512]{1,0:T(8,128)(2,1)}, u32[]{:S(2)}) copy-start(bf16[512,512]{1,0:T(8,128)(2,1)} %refs_10_.1) | copy-start | bytes 1572868
  59.2 19.0 %copy-start.1 = (bf16[512,512]{1,0:T(8,128)(2,1)S(1)}, bf16[512,512]{1,0:T(8,128)(2,1)}, u32[]{:S(2)}) copy-start(bf16[512,512]{1,0:T(8,128)(2,1)} %refs_11_.1) | copy-start | bytes 1572868
  59.2 19.0 %copy-start.6 = (f32[512]{0:T(512)S(1)}, f32[512]{0:T(512)}, u32[]{:S(2)}) copy-start(f32[512]{0:T(512)} %param.30) | copy-start | bytes 6148
  59.2 6.4 %collective-permute-start.14 = (bf16[256,512]{1,0:T(8,128)(2,1)S(1)}, bf16[256,512]{1,0:T(8,128)(2,1)S(1)}, u32[]{:S(2)}, u32[]{:S(2)}) collective-permute-start(bf16[256,512]{1,0:T(8,128)(2,1)S(1)} %get-tuple-element.69), channel_id=1, source_target_pairs={{0,2},{1,3},{2,0},{3,1},{4,6},{5,7},{6,4},{7,5},{8,10},{9,11},{10,... | collective-permute-start | bytes 786440 | tf_op jit(solution)/shard_map/ppermute | solution.py:272
  60.3 6.7 %collective-permute-start.13 = (bf16[128,512]{1,0:T(8,128)(2,1)S(1)}, bf16[128,512]{1,0:T(8,128)(2,1)S(1)}, u32[]{:S(2)}, u32[]{:S(2)}) collective-permute-start(bf16[128,512]{1,0:T(8,128)(2,1)S(1)} %get-tuple-element.84), channel_id=1, source_target_pairs={{0,2},{1,3},{2,0},{3,1},{4,6},{5,7},{6,4},{7,5},{8,10},{9,11},{10,... | collective-permute-start | bytes 393224 | tf_op jit(solution)/shard_map/ppermute | solution.py:272
  65.7 23.5 %copy-start.2 = (bf16[512,512]{1,0:T(8,128)(2,1)S(1)}, bf16[512,512]{1,0:T(8,128)(2,1)}, u32[]{:S(2)}) copy-start(bf16[512,512]{1,0:T(8,128)(2,1)} %proc_in_ref.1) | copy-start | bytes 1572868
  65.7 23.5 %copy-start.3 = (bf16[512,512]{1,0:T(8,128)(2,1)S(1)}, bf16[512,512]{1,0:T(8,128)(2,1)}, u32[]{:S(2)}) copy-start(bf16[512,512]{1,0:T(8,128)(2,1)} %proc_out_ref.1) | copy-start | bytes 1572868
  65.7 23.4 %copy-start.5 = (bf16[12,128,128]{2,1,0:T(8,128)(2,1)S(1)}, bf16[12,128,128]{2,1,0:T(8,128)(2,1)}, u32[]{:S(2)}) copy-start(bf16[12,128,128]{2,1,0:T(8,128)(2,1)} %values_ref.1) | copy-start | bytes 1179652
  65.7 23.4 %copy-start.7 = (f32[512]{0:T(512)S(1)}, f32[512]{0:T(512)}, u32[]{:S(2)}) copy-start(f32[512]{0:T(512)} %param.37) | copy-start | bytes 6148
  65.8 23.4 %copy-start.8 = (s32[12]{0:T(128)S(1)}, s32[12]{0:T(128)}, u32[]{:S(2)}) copy-start(s32[12]{0:T(128)} %dst_ref.3) | copy-start | bytes 148
  65.8 23.4 %copy-start.9 = (s32[12]{0:T(128)S(1)}, s32[12]{0:T(128)}, u32[]{:S(2)}) copy-start(s32[12]{0:T(128)} %src_ref.3) | copy-start | bytes 148
  67.3 10.9 %collective-permute-start.18 = (bf16[128,512]{1,0:T(8,128)(2,1)S(1)}, bf16[128,512]{1,0:T(8,128)(2,1)S(1)}, u32[]{:S(2)}, u32[]{:S(2)}) collective-permute-start(bf16[128,512]{1,0:T(8,128)(2,1)S(1)} %get-tuple-element.79), channel_id=1, source_target_pairs={{0,8},{1,9},{2,10},{3,11},{4,12},{5,13},{6,14},{7,15},{8,0},{9,1},... | collective-permute-start | bytes 393224 | tf_op jit(solution)/shard_map/ppermute | solution.py:272
  67.3 10.8 %collective-permute-start.16 = (bf16[128,512]{1,0:T(8,128)(2,1)S(1)}, bf16[128,512]{1,0:T(8,128)(2,1)S(1)}, u32[]{:S(2)}, u32[]{:S(2)}) collective-permute-start(bf16[128,512]{1,0:T(8,128)(2,1)S(1)} %get-tuple-element.81), channel_id=1, source_target_pairs={{0,4},{1,5},{2,6},{3,7},{4,0},{5,1},{6,2},{7,3},{8,12},{9,13},{10,... | collective-permute-start | bytes 393224 | tf_op jit(solution)/shard_map/ppermute | solution.py:272
  69.7 8.5 %collective-permute-start.19 = (bf16[128,512]{1,0:T(8,128)(2,1)S(1)}, bf16[128,512]{1,0:T(8,128)(2,1)S(1)}, u32[]{:S(2)}, u32[]{:S(2)}) collective-permute-start(bf16[128,512]{1,0:T(8,128)(2,1)S(1)} %get-tuple-element.77), channel_id=1, source_target_pairs={{0,4},{1,5},{2,6},{3,7},{4,0},{5,1},{6,2},{7,3},{8,12},{9,13},{10,... | collective-permute-start | bytes 393224 | tf_op jit(solution)/shard_map/ppermute | solution.py:272
  69.7 5.2 %collective-permute-start.20 = (bf16[64,512]{1,0:T(8,128)(2,1)S(1)}, bf16[64,512]{1,0:T(8,128)(2,1)S(1)}, u32[]{:S(2)}, u32[]{:S(2)}) collective-permute-start(bf16[64,512]{1,0:T(8,128)(2,1)S(1)} %get-tuple-element.89), channel_id=1, source_target_pairs={{0,8},{1,9},{2,10},{3,11},{4,12},{5,13},{6,14},{7,15},{8,0},{9,1},... | collective-permute-start | bytes 196616 | tf_op jit(solution)/shard_map/ppermute | solution.py:272
  72.3 5.9 %collective-permute-start.21 = (bf16[64,512]{1,0:T(8,128)(2,1)S(1)}, bf16[64,512]{1,0:T(8,128)(2,1)S(1)}, u32[]{:S(2)}, u32[]{:S(2)}) collective-permute-start(bf16[64,512]{1,0:T(8,128)(2,1)S(1)} %get-tuple-element.87), channel_id=1, source_target_pairs={{0,8},{1,9},{2,10},{3,11},{4,12},{5,13},{6,14},{7,15},{8,0},{9,1},... | collective-permute-start | bytes 196616 | tf_op jit(solution)/shard_map/ppermute | solution.py:272
  80.6 3.1 %collective-permute-start.22 = (bf16[256,512]{1,0:T(8,128)(2,1)S(1)}, bf16[256,512]{1,0:T(8,128)(2,1)S(1)}, u32[]{:S(2)}, u32[]{:S(2)}) collective-permute-start(bf16[256,512]{1,0:T(8,128)(2,1)S(1)} %get-tuple-element.58), channel_id=1, source_target_pairs={{0,1},{1,0},{2,3},{3,2},{4,5},{5,4},{6,7},{7,6},{8,9},{9,8},{10,11... | collective-permute-start | bytes 786440 | tf_op jit(solution)/shard_map/ppermute | solution.py:464
  80.6 8.6 %collective-permute-start.23 = (bf16[256,512]{1,0:T(8,128)(2,1)S(1)}, bf16[256,512]{1,0:T(8,128)(2,1)S(1)}, u32[]{:S(2)}, u32[]{:S(2)}) collective-permute-start(bf16[256,512]{1,0:T(8,128)(2,1)S(1)} %get-tuple-element.59), channel_id=1, source_target_pairs={{0,15},{1,2},{2,1},{3,4},{4,3},{5,6},{6,5},{7,8},{8,7},{9,10},{10,... | collective-permute-start | bytes 786440 | tf_op jit(solution)/shard_map/ppermute | solution.py:463
  89.2 1.0 %copy-start.4 = (bf16[512,512]{1,0:T(8,128)(2,1)S(1)}, bf16[512,512]{1,0:T(8,128)(2,1)}, u32[]{:S(2)}) copy-start(bf16[512,512]{1,0:T(8,128)(2,1)} %get-tuple-element.29.encoded_ref) | copy-start | bytes 1572868

commit v3 on v2

--- a/solution.py
+++ b/solution.py
@@ -97,7 +97,7 @@
             )
         )
     ]
-    for load in loads:
+    for load in loads[:3]:
         load.start()
 
     me = lax.axis_index("space")
@@ -115,27 +115,26 @@
     lax.fori_loop(0, slots * held, clear, 0)
     lax.fori_loop(0, pairs, clear_pair, 0)
 
-    def sort(edge, carry):
+    def sort(edge):
         bin_ = place_ref[dst_ref[edge]] ^ (me * held)
         count = filled[bin_]
         edge_of[bin_ * capacity + count] = edge
         filled[bin_] = count + 1
-
-        @pl.when(count == 2)
-        def _():
-            pair = lax.div(bin_, 2 * held)
-            seen = crowded[pair]
-            crowded_of[pair * 2 * held + seen] = bin_
-            crowded[pair] = seen + 1
-
-        return carry
-
-    lax.fori_loop(0, edges, sort, 0)
+        pair = lax.div(bin_, 2 * held)
+        seen = crowded[pair]
+        crowded_of[pair * 2 * held + seen] = bin_
+        crowded[pair] = seen + (count == 2).astype(jnp.int32)
 
     for load in loads[:3]:
         load.wait()
+    loads[3].start()
+
+    tiles = latent.shape[0] // tile_rows
+    sorted_each = edges // tiles
 
     def embed(tile, carry):
+        for index in range(sorted_each):
+            sort(tile * sorted_each + index)
         first = pl.multiple_of(tile * tile_rows, tile_rows)
         columns = inputs_ref[:, pl.ds(first, tile_rows)]
         hidden = silu(transposed_matmul(columns, embed_in_ref[...])).astype(jnp.bfloat16)
@@ -144,7 +143,9 @@
         latent[pl.ds(first, tile_rows), :] = jnp.where(row < count_ref[0], scaled, 0.0).astype(jnp.bfloat16)
         return carry
 
-    lax.fori_loop(0, latent.shape[0] // tile_rows, embed, 0)
+    lax.fori_loop(0, tiles, embed, 0, unroll=True)
+    for edge in range(tiles * sorted_each, edges):
+        sort(edge)
     loads[3].wait()
 
     def stores(pair):
@@ -182,13 +183,14 @@
             staged[pair, side, pl.ds(first, cut), :] = summed[top : top + cut].astype(jnp.bfloat16)
             top += cut
 
-    def multiply(pair, carry):
-        for side in range(2):
-            for block in range(held):
-                bin_ = (2 * pair + side) * held + block
-                stage(pair, side, block, product(bin_, 0, filled[bin_]))
-
-        def revisit(index, carry):
+    def multiply(turn, carry):
+        for pair in (2 * turn, 2 * turn + 1):
+            for side in range(2):
+                for block in range(held):
+                    bin_ = (2 * pair + side) * held + block
+                    stage(pair, side, block, product(bin_, 0, filled[bin_]))
+
+        def revisit(pair, index, carry):
             bin_ = crowded_of[pair * 2 * held + index]
             count = filled[bin_]
             summed = product(bin_, 0, count)
@@ -197,12 +199,13 @@
             stage(pair, lax.div(lax.rem(bin_, 2 * held), held), lax.rem(bin_, held), summed)
             return carry
 
-        lax.fori_loop(0, crowded[pair], revisit, 0)
-        for copy in stores(pair):
-            copy.start()
+        for pair in (2 * turn, 2 * turn + 1):
+            lax.fori_loop(0, crowded[pair], functools.partial(revisit, pair), 0)
+            for copy in stores(pair):
+                copy.start()
         return carry
 
-    lax.fori_loop(0, pairs, multiply, 0)
+    lax.fori_loop(0, pairs // 2, multiply, 0)
 
     def finish(pair, carry):
         for copy in stores(pair):
@@ -247,7 +250,7 @@
             pltpu.VMEM((pairs, 2, held * rows, channels), jnp.bfloat16),
             pltpu.SMEM((partitions * held * capacity,), jnp.int32),
             pltpu.SMEM((partitions * held,), jnp.int32),
-            pltpu.SMEM((partitions * held,), jnp.int32),
+            pltpu.SMEM((partitions * held + 1,), jnp.int32),
             pltpu.SMEM((pairs,), jnp.int32),
             pltpu.SemaphoreType.DMA((4,)),
             pltpu.SemaphoreType.DMA((pairs, 2, len(cuts))),
@@ -272,27 +275,27 @@
     return lax.ppermute(cells, "space", [(i, i ^ (1 << bit)) for i in range(count)])
 
 
-def reduce_chunks(mates, owns, orders, turns, lists):
+def reduce_chunks(mates, owns, orders, turns, later):
     arrived = [exchange(mate, 0) for mate in mates]
     kept = list(owns)
     made = [0] * len(orders)
     for turn, chunk in enumerate(turns):
         received = arrived[chunk]
-        if turn == len(orders):
-            received, _, lists = lax.optimization_barrier((received, previous, lists))
-        elif turn > 0:
+        if turn > 0:
             received, _ = lax.optimization_barrier((received, previous))
         half = kept[chunk].shape[0] // 2
         previous = add(received[half:], kept[chunk][half:]).astype(jnp.bfloat16)
         kept[chunk] = add(received[:half], kept[chunk][:half]).astype(jnp.bfloat16)
         arrived[chunk] = exchange(previous, orders[chunk][made[chunk]])
         made[chunk] += 1
-    return arrived, kept, lists
+        if turn == len(orders) - 1:
+            later = lax.optimization_barrier((later, previous))[0]
+    return arrived, kept, later
 
 
 def node_kernel(parts, reads, rows, mate_list_ref, other_list_ref, *refs):
     summands = refs[:parts]
-    node_in_ref, node_out_ref, gain_ref, encoded_ref, to_mate_ref, to_other_ref = refs[parts:]
+    node_in_ref, node_out_ref, gain_ref, encoded_ref, own_ref, to_mate_ref, to_other_ref = refs[parts:]
     if parts == 1:
         summed = summands[0][...]
     else:
@@ -309,7 +312,9 @@
             axis=0,
         )
     hidden = silu(matmul(summed.astype(jnp.bfloat16), node_in_ref[...])).astype(jnp.bfloat16)
-    encoded_ref[...] = (summed + gain_ref[...] * normalize(matmul(hidden, node_out_ref[...]))).astype(jnp.bfloat16)
+    encoded = (summed + gain_ref[...] * normalize(matmul(hidden, node_out_ref[...]))).astype(jnp.bfloat16)
+    encoded_ref[...] = encoded
+    own_ref[...] = encoded
     odd = lax.rem(lax.axis_index("space"), 2)
     for index in range(reads):
         for wanted_ref, first, out in (
@@ -326,8 +331,9 @@
     return pl.pallas_call(
         functools.partial(node_kernel, len(summands), reads, rows),
         in_specs=[SMEM] * 2 + [VMEM] * (len(summands) + 3),
-        out_specs=[VMEM] * 3,
+        out_specs=[VMEM] * 4,
         out_shape=[
+            jax.ShapeDtypeStruct((held * rows, channels), jnp.bfloat16),
             jax.ShapeDtypeStruct((held * rows, channels), jnp.bfloat16),
             jax.ShapeDtypeStruct((reads * rows, channels), jnp.bfloat16),
             jax.ShapeDtypeStruct((reads * rows, channels), jnp.bfloat16),
@@ -337,58 +343,58 @@
     )(*lists, *summands, node_in, node_out, node_gain.reshape(1, -1))
 
 
-def process_kernel(
-    held,
-    reads,
-    dst_ref,
-    src_ref,
-    encoded_ref,
-    mate_ref,
-    other_ref,
-    values_ref,
-    proc_in_ref,
-    proc_out_ref,
-    gain_ref,
-    processed_ref,
-    frame,
-):
+def operator_kernel(held, reads, dst_ref, src_ref, values_ref, operator_ref, total):
     edges, rows, _ = values_ref.shape
-    frame[: reads * rows, :] = mate_ref[...]
-    frame[reads * rows : 2 * reads * rows, :] = other_ref[...]
-    frame[2 * reads * rows :, :] = encoded_ref[...]
     odd = lax.rem(lax.axis_index("space"), 2)
-    operator = []
-    sources = []
+    total[...] = jnp.zeros_like(total)
     for edge in range(edges):
-        values = values_ref[edge]
-        zeros = jnp.zeros_like(values)
-        local = dst_ref[edge]
-        operator.append(
-            jnp.concatenate([jnp.where(local == block, values, zeros) for block in range(held)], axis=0)
-        )
         side = lax.div(src_ref[edge], held)
         index = lax.rem(src_ref[edge], held)
         across = (odd + lax.div(side, 2) + 1) & 1
-        at = jnp.where(side == 1, 2 * reads, across * reads) + index
-        start = pl.multiple_of(at * rows, rows)
-        sources.append(frame[pl.ds(start, rows), :])
-    message = matmul(jnp.concatenate(operator, axis=1), jnp.concatenate(sources, axis=0))
+        source = jnp.where(side == 1, 2 * reads, across * reads) + index
+        first = pl.multiple_of(dst_ref[edge] * rows, rows)
+        total[source, pl.ds(first, rows), :] += values_ref[edge].astype(jnp.float32)
+    for source in range(2 * reads + held):
+        operator_ref[:, source * rows : (source + 1) * rows] = total[source].astype(jnp.bfloat16)
+
+
+def mesh_operator(mesh_values, mesh_dst, mesh_src, held, reads):
+    rows = mesh_values.shape[1]
+    sources = 2 * reads + held
+    return pl.pallas_call(
+        functools.partial(operator_kernel, held, reads),
+        in_specs=[SMEM] * 2 + [VMEM],
+        out_specs=VMEM,
+        out_shape=jax.ShapeDtypeStruct((held * rows, sources * rows), jnp.bfloat16),
+        scratch_shapes=[pltpu.VMEM((sources, held * rows, rows), jnp.float32)],
+        compiler_params=pltpu.CompilerParams(vmem_limit_bytes=VMEM_BYTES),
+        name="mesh_operator",
+    )(mesh_dst, mesh_src, mesh_values)
+
+
+def process_kernel(
+    operator_ref, own_ref, mate_ref, other_ref, proc_in_ref, proc_out_ref, gain_ref, processed_ref
+):
+    message = 0.0
+    first = 0
+    for source_ref in (mate_ref, other_ref, own_ref):
+        last = first + source_ref.shape[0]
+        message = message + matmul(operator_ref[:, first:last], source_ref[...])
+        first = last
     hidden = silu(matmul(message.astype(jnp.bfloat16), proc_in_ref[...])).astype(jnp.bfloat16)
     update = gain_ref[...] * normalize(matmul(hidden, proc_out_ref[...]))
-    processed_ref[...] = (encoded_ref[...].astype(jnp.float32) + update).astype(jnp.bfloat16)
-
-
-def process(encoded, from_mate, from_other, mesh_values, mesh_dst, mesh_src, proc_in, proc_out, proc_gain, held, reads):
-    rows = mesh_values.shape[1]
+    processed_ref[...] = (own_ref[...].astype(jnp.float32) + update).astype(jnp.bfloat16)
+
+
+def process(operator, own, from_mate, from_other, proc_in, proc_out, proc_gain):
     return pl.pallas_call(
-        functools.partial(process_kernel, held, reads),
-        in_specs=[SMEM] * 2 + [VMEM] * 7,
+        process_kernel,
+        in_specs=[VMEM] * 7,
         out_specs=VMEM,
-        out_shape=jax.ShapeDtypeStruct(encoded.shape, jnp.bfloat16),
-        scratch_shapes=[pltpu.VMEM(((2 * reads + held) * rows, encoded.shape[1]), jnp.bfloat16)],
+        out_shape=jax.ShapeDtypeStruct(own.shape, jnp.bfloat16),
         compiler_params=pltpu.CompilerParams(vmem_limit_bytes=VMEM_BYTES),
         name="process",
-    )(mesh_dst, mesh_src, encoded, from_mate, from_other, mesh_values, proc_in, proc_out, proc_gain.reshape(1, -1))
+    )(operator, own, from_mate, from_other, proc_in, proc_out, proc_gain.reshape(1, -1))
 
 
 def lookup(table, wanted):
@@ -450,21 +456,22 @@
     reads = recv_blocks.shape[1] // 2
     mates = [(i, i ^ 1) for i in range(partitions)]
     others = [(i, (i + 1 if i % 2 else i - 1) % partitions) for i in range(partitions)]
-    lists = (lax.ppermute(recv_blocks, "space", mates), lax.ppermute(recv_blocks, "space", others))
     grid_args = (grid_inputs, grid_count, embed_in, embed_out, grid_gain, g2m_values, g2m_src, g2m_dst, mesh_place)
     if partitions == 1 << (1 + len(ORDERS[0])) and edges % partitions == 0 and edges >= mesh_blocks:
         cuts = [share * rows // sum(SHARES) for share in SHARES]
         sums = slab_sums(*grid_args, partitions, ORDERS, cuts)
-        arrived, kept, lists = reduce_chunks(sums[: len(cuts)], sums[len(cuts) :], ORDERS, TURNS, lists)
+        arrived, kept, (recv_blocks, mesh_values) = reduce_chunks(
+            sums[: len(cuts)], sums[len(cuts) :], ORDERS, TURNS, (recv_blocks, mesh_values)
+        )
         summands = arrived + kept
     else:
         summands = [routed_sum(*grid_args, partitions)]
-    encoded, to_mate, to_other = encode(summands, node_in, node_out, node_gain, lists, held, rows)
+    lists = (lax.ppermute(recv_blocks, "space", mates), lax.ppermute(recv_blocks, "space", others))
+    operator = mesh_operator(mesh_values, mesh_dst, mesh_src, held, reads)
+    encoded, own, to_mate, to_other = encode(summands, node_in, node_out, node_gain, lists, held, rows)
     from_other = lax.ppermute(to_other, "space", others)
     from_mate = lax.ppermute(to_mate, "space", mates)
-    processed = process(
-        encoded, from_mate, from_other, mesh_values, mesh_dst, mesh_src, proc_in, proc_out, proc_gain, held, reads
-    )
+    processed = process(operator, own, from_mate, from_other, proc_in, proc_out, proc_gain)
     return (encoded, processed)
 
 

time: 93.9 us -> 89.7 us (0.955)
  waiting for transfers between devices: 45.4 us -> 34.3 us
  starting transfers between devices: 24 us -> 33.6 us
  local copies, waits for them, and re-layouts: 1.31 us -> 0.08 us
  Pallas kernels: 17.9 us -> 16.7 us
    ppermute x20, waiting for transfers between devices: 39.8 us -> 25.5 us  [exchange(): lax.ppermute(cells, 'space', [(i, i ^ 1 << bit) for i in range(count)])]
    ppermute x20, starting transfers between devices: 15 us -> 29 us  [exchange(): lax.ppermute(cells, 'space', [(i, i ^ 1 << bit) for i in range(count)])]
    ppermute x1, starting transfers between devices: 5.93 us -> 0.01 us  [shards(): lax.ppermute(recv_blocks, 'space', others)]
    ppermute x1, waiting for transfers between devices: 0.01 us -> 3.99 us  [shards(): lax.ppermute(recv_blocks, 'space', others)]
    ppermute x1, starting transfers between devices: 0.08 us -> 1.85 us  [shards(): lax.ppermute(recv_blocks, 'space', mates)]
    pallas_call x1, Pallas kernels: 12.2 us -> 10.9 us  [slab_sums(): pl.pallas_call(functools.partial(grid_kernel, held, capacity, orders, cut...]
    unnamed x32 -> x28, local copies, waits for them, and re-layouts: 1.31 us -> 0.08 us
    pallas_call x1 -> x2, Pallas kernels: 3.27 us -> 3.45 us  [the longest x1 2.39 us: process(): pl.pallas_call(process_kernel, in_specs=[VMEM] * 7, out_specs=VMEM, out_s...]
  transfers between devices with their start and end apart: 24 -> 24, of which waited for: 9 -> 11; matrix products, arithmetic and copies ran while one was open for 3% -> 4% of each run, Pallas kernels for 0% -> 1%
where the time goes in v3:
time: 89.7 us; the launch traced here: 89.4 us
  waiting for transfers between devices  34.3 us (38%)
  starting transfers between devices  33.6 us (37%)
  Pallas kernels  16.7 us (19%)
  other arithmetic  3.23 us (4%)
  between operations  1.56 us (2%)
    ppermute x20, starting transfers between devices, exchange(): lax.ppermute(cells, 'space', [(i, i ^ 1 << bit) for i in range(count)])  29 us
    ppermute x20, waiting for transfers between devices, exchange(): lax.ppermute(cells, 'space', [(i, i ^ 1 << bit) for i in range(count)])  25.5 us
    pallas_call x1, Pallas kernels, slab_sums(): pl.pallas_call(functools.partial(grid_kernel, held, capacity, orders, cut...  10.9 us
    ppermute x1, waiting for transfers between devices, shards(): from_other = lax.ppermute(to_other, 'space', others)  4.77 us
    ppermute x1, waiting for transfers between devices, shards(): lax.ppermute(recv_blocks, 'space', others)  3.99 us
    convert_element_type x13, other arithmetic, reduce_chunks(): kept[chunk] = add(received[:half], kept[chunk][:half]).astype(jnp.bfloat16)  3.02 us
    ppermute x1, starting transfers between devices, shards(): from_other = lax.ppermute(to_other, 'space', others)  2.75 us
    pallas_call x1, Pallas kernels, process(): pl.pallas_call(process_kernel, in_specs=[VMEM] * 7, out_specs=VMEM, out_s...  2.39 us
  transfers between devices with their start and end apart: 24, of which 11 were waited for; matrix products, arithmetic and copies ran while one was open for 4% of the time, Pallas kernels for 1%

profile of v3, /device:TPU:0, one launch (start us, length us, event | category | flops | bytes accessed | tf_op | source)
XLA Modules:
  0.0 89.4 jit_solution(11724862276716010796)
XLA Ops:
  1.3 10.9 %grid_to_mesh.1 = (bf16[1024,512]{1,0:T(8,128)(2,1)}, bf16[1024,512]{1,0:T(8,128)(2,1)}, bf16[1024,512]{1,0:T(8,128)(2,1)}, bf16[512,512]{1,0:T(8,128)(2,1)}, bf...) custom-call(s32[64]{0:T(128)} %src_ref.2, ...), custom_call_target="tpu_custom_call" | custom-call | tf_op jit(solution)/shard_map/grid_to_mesh/pallas_call | solution.py:239
  12.2 0.3 collective-permute-start.4
  12.4 0.3 collective-permute-start.3
  12.7 0.2 collective-permute-start.2
  12.9 0.3 collective-permute-start
  13.2 0.2 collective-permute-start.1
  13.4 1.6 %collective-permute-done.4 = bf16[1024,512]{1,0:T(8,128)(2,1)S(1)} collective-permute-done((bf16[1024,512]{1,0:T(8,128)(2,1)}, bf16[1024,512]{1,0:T(8,128)(2,1)S(1)}, u32[]{:S(2)}, u32[]{:S(2)}) %collective-permute-start.4) | collective-permute-done | bytes 1048608 | tf_op jit(solution)/shard_map/ppermute | solution.py:275
  15.1 1.5 %add_convert_fusion.2 = (bf16[512,512]{1,0:T(8,128)(2,1)S(1)}, bf16[512,512]{1,0:T(8,128)(2,1)S(1)}) fusion(bf16[1024,512]{1,0:T(8,128)(2,1)S(1)} %collective-permute-done.4, bf16[1024,512]{1,0:T(8,128)(2,1)} %get-tuple-element.37), kind=kLoop, calls=%fused_computation.2 | loop fusion | flops 2097152 | bytes 3145728 | tf_op jit(solution)/shard_map/convert_element_type | solution.py:288
  16.6 3.0 %collective-permute-start.7 = (bf16[512,512]{1,0:T(8,128)(2,1)S(1)}, bf16[512,512]{1,0:T(8,128)(2,1)S(1)}, u32[]{:S(2)}, u32[]{:S(2)}) collective-permute-start(bf16[512,512]{1,0:T(8,128)(2,1)S(1)} %get-tuple-element.67), channel_id=1, source_target_pairs={{0,2},{1,3},{2,0},{3,1},{4,6},{5,7},{6,4},{7,5},{8,10},{9,11},{10,... | collective-permute-start | bytes 1572872 | tf_op jit(solution)/shard_map/ppermute | solution.py:275
  19.6 0.0 collective-permute-done.3
  19.6 0.3 add_convert_fusion.1
  20.0 0.1 collective-permute-start.11
  20.1 0.3 add_convert_fusion
  20.4 3.0 %collective-permute-start.10 = (bf16[512,512]{1,0:T(8,128)(2,1)S(1)}, bf16[512,512]{1,0:T(8,128)(2,1)S(1)}, u32[]{:S(2)}, u32[]{:S(2)}) collective-permute-start(bf16[512,512]{1,0:T(8,128)(2,1)S(1)} %get-tuple-element.65), channel_id=1, source_target_pairs={{0,8},{1,9},{2,10},{3,11},{4,12},{5,13},{6,14},{7,15},{8,0},{9,1},... | collective-permute-start | bytes 1572872 | tf_op jit(solution)/shard_map/ppermute | solution.py:275
  23.3 0.0 collective-permute-done.1
  23.3 0.1 add_convert_fusion.12
  23.5 1.8 %collective-permute-start.12 = (bf16[256,512]{1,0:T(8,128)(2,1)S(1)}, bf16[256,512]{1,0:T(8,128)(2,1)S(1)}, u32[]{:S(2)}, u32[]{:S(2)}) collective-permute-start(bf16[256,512]{1,0:T(8,128)(2,1)S(1)} %get-tuple-element.73), channel_id=1, source_target_pairs={{0,4},{1,5},{2,6},{3,7},{4,0},{5,1},{6,2},{7,3},{8,12},{9,13},{10,... | collective-permute-start | bytes 786440 | tf_op jit(solution)/shard_map/ppermute | solution.py:275
  25.3 0.1 add_convert_fusion.9
  25.4 0.4 collective-permute-start.9
  25.8 6.5 %collective-permute-done.7 = bf16[512,512]{1,0:T(8,128)(2,1)S(1)} collective-permute-done((bf16[512,512]{1,0:T(8,128)(2,1)S(1)}, bf16[512,512]{1,0:T(8,128)(2,1)S(1)}, u32[]{:S(2)}, u32[]{:S(2)}) %collective-permute-start.7) | collective-permute-done | bytes 524320 | tf_op jit(solution)/shard_map/ppermute | solution.py:275
  32.3 0.1 add_convert_fusion.13
  32.5 3.0 %collective-permute-start.8 = (bf16[256,512]{1,0:T(8,128)(2,1)S(1)}, bf16[256,512]{1,0:T(8,128)(2,1)S(1)}, u32[]{:S(2)}, u32[]{:S(2)}) collective-permute-start(bf16[256,512]{1,0:T(8,128)(2,1)S(1)} %get-tuple-element.76), channel_id=1, source_target_pairs={{0,8},{1,9},{2,10},{3,11},{4,12},{5,13},{6,14},{7,15},{8,0},{9,1},... | collective-permute-start | bytes 786440 | tf_op jit(solution)/shard_map/ppermute | solution.py:275
  35.4 5.9 %collective-permute-done.12 = bf16[256,512]{1,0:T(8,128)(2,1)S(1)} collective-permute-done((bf16[256,512]{1,0:T(8,128)(2,1)S(1)}, bf16[256,512]{1,0:T(8,128)(2,1)S(1)}, u32[]{:S(2)}, u32[]{:S(2)}) %collective-permute-start.12) | collective-permute-done | bytes 262176 | tf_op jit(solution)/shard_map/ppermute | solution.py:275
  41.3 0.1 add_convert_fusion.23
  41.4 2.1 %collective-permute-start.15 = (bf16[128,512]{1,0:T(8,128)(2,1)S(1)}, bf16[128,512]{1,0:T(8,128)(2,1)S(1)}, u32[]{:S(2)}, u32[]{:S(2)}) collective-permute-start(bf16[128,512]{1,0:T(8,128)(2,1)S(1)} %get-tuple-element.85), channel_id=1, source_target_pairs={{0,2},{1,3},{2,0},{3,1},{4,6},{5,7},{6,4},{7,5},{8,10},{9,11},{10,... | collective-permute-start | bytes 393224 | tf_op jit(solution)/shard_map/ppermute | solution.py:275
  43.5 0.1 collective-permute-done.11
  43.6 0.1 add_convert_fusion.6
  43.7 2.5 %collective-permute-start.17 = (bf16[256,512]{1,0:T(8,128)(2,1)S(1)}, bf16[256,512]{1,0:T(8,128)(2,1)S(1)}, u32[]{:S(2)}, u32[]{:S(2)}) collective-permute-start(bf16[256,512]{1,0:T(8,128)(2,1)S(1)} %get-tuple-element.69), channel_id=1, source_target_pairs={{0,4},{1,5},{2,6},{3,7},{4,0},{5,1},{6,2},{7,3},{8,12},{9,13},{10,... | collective-permute-start | bytes 786440 | tf_op jit(solution)/shard_map/ppermute | solution.py:275
  46.2 2.2 %collective-permute-done.10 = bf16[512,512]{1,0:T(8,128)(2,1)S(1)} collective-permute-done((bf16[512,512]{1,0:T(8,128)(2,1)S(1)}, bf16[512,512]{1,0:T(8,128)(2,1)S(1)}, u32[]{:S(2)}, u32[]{:S(2)}) %collective-permute-start.10) | collective-permute-done | bytes 524320 | tf_op jit(solution)/shard_map/ppermute | solution.py:275
  48.4 0.1 add_convert_fusion.8
  48.6 0.0 copy-start.13
  48.6 0.0 copy-start
  48.6 0.0 copy-start.1
  48.6 0.0 copy-start.5
  48.6 5.3 %collective-permute-start.14 = (bf16[256,512]{1,0:T(8,128)(2,1)S(1)}, bf16[256,512]{1,0:T(8,128)(2,1)S(1)}, u32[]{:S(2)}, u32[]{:S(2)}) collective-permute-start(bf16[256,512]{1,0:T(8,128)(2,1)S(1)} %get-tuple-element.71), channel_id=1, source_target_pairs={{0,2},{1,3},{2,0},{3,1},{4,6},{5,7},{6,4},{7,5},{8,10},{9,11},{10,... | collective-permute-start | bytes 786440 | tf_op jit(solution)/shard_map/ppermute | solution.py:275
  53.9 0.1 add_convert_fusion.24
  54.0 0.1 collective-permute-start.13
  54.1 4.1 %collective-permute-done.14 = bf16[256,512]{1,0:T(8,128)(2,1)S(1)} collective-permute-done((bf16[256,512]{1,0:T(8,128)(2,1)S(1)}, bf16[256,512]{1,0:T(8,128)(2,1)S(1)}, u32[]{:S(2)}, u32[]{:S(2)}) %collective-permute-start.14) | collective-permute-done | bytes 262176 | tf_op jit(solution)/shard_map/ppermute | solution.py:275
  58.2 0.1 add_convert_fusion.16
  58.3 0.0 copy-start.4
  58.3 0.0 copy-start.7
  58.3 0.0 copy-start.8
  58.3 0.1 collective-permute-start.19
  58.4 1.2 %collective-permute-done.13 = bf16[128,512]{1,0:T(8,128)(2,1)S(1)} collective-permute-done((bf16[128,512]{1,0:T(8,128)(2,1)S(1)}, bf16[128,512]{1,0:T(8,128)(2,1)S(1)}, u32[]{:S(2)}, u32[]{:S(2)}) %collective-permute-start.13) | collective-permute-done | bytes 131104 | tf_op jit(solution)/shard_map/ppermute | solution.py:275
  59.7 0.1 add_convert_fusion.18
  59.8 0.0 collective-permute-done.17
  59.8 0.0 copy-start.2
  59.8 0.0 copy-start.3
  59.8 0.0 copy-start.6
  59.8 0.1 add_convert_fusion.17
  59.9 1.9 %collective-permute-start.18 = (bf16[128,512]{1,0:T(8,128)(2,1)S(1)}, bf16[128,512]{1,0:T(8,128)(2,1)S(1)}, u32[]{:S(2)}, u32[]{:S(2)}) collective-permute-start(bf16[128,512]{1,0:T(8,128)(2,1)S(1)} %get-tuple-element.81), channel_id=1, source_target_pairs={{0,8},{1,9},{2,10},{3,11},{4,12},{5,13},{6,14},{7,15},{8,0},{9,1},... | collective-permute-start | bytes 393224 | tf_op jit(solution)/shard_map/ppermute | solution.py:275
  61.8 1.7 %collective-permute-start.16 = (bf16[128,512]{1,0:T(8,128)(2,1)S(1)}, bf16[128,512]{1,0:T(8,128)(2,1)S(1)}, u32[]{:S(2)}, u32[]{:S(2)}) collective-permute-start(bf16[128,512]{1,0:T(8,128)(2,1)S(1)} %get-tuple-element.83), channel_id=1, source_target_pairs={{0,4},{1,5},{2,6},{3,7},{4,0},{5,1},{6,2},{7,3},{8,12},{9,13},{10,... | collective-permute-start | bytes 393224 | tf_op jit(solution)/shard_map/ppermute | solution.py:275
  63.5 1.9 %collective-permute-start.5 = (s32[1,4]{1,0:T(1,128)S(1)}, s32[1,4]{1,0:T(1,128)S(1)}, u32[]{:S(2)}, u32[]{:S(2)}) collective-permute-start(s32[1,4]{1,0:T(1,128)S(1)} %copy-done.13), channel_id=1, source_target_pairs={{0,1},{1,0},{2,3},{3,2},{4,5},{5,4},{6,7},{7,6},{8,9},{9,8},{10,11... | collective-permute-start | bytes 56 | tf_op jit(solution)/shard_map/ppermute | solution.py:469
  65.4 4.0 %collective-permute-done.6.other_list_ref = s32[1,4]{1,0:T(1,128)S(1)} collective-permute-done((s32[1,4]{1,0:T(1,128)S(1)}, s32[1,4]{1,0:T(1,128)S(1)}, u32[]{:S(2)}, u32[]{:S(2)}) %collective-permute-start.6) | collective-permute-done | bytes 48 | tf_op jit(solution)/shard_map/ppermute | solution.py:469
  69.4 2.9 %collective-permute-start.21 = (bf16[64,512]{1,0:T(8,128)(2,1)S(1)}, bf16[64,512]{1,0:T(8,128)(2,1)S(1)}, u32[]{:S(2)}, u32[]{:S(2)}) collective-permute-start(bf16[64,512]{1,0:T(8,128)(2,1)S(1)} %get-tuple-element.89), channel_id=1, source_target_pairs={{0,8},{1,9},{2,10},{3,11},{4,12},{5,13},{6,14},{7,15},{8,0},{9,1},... | collective-permute-start | bytes 196616 | tf_op jit(solution)/shard_map/ppermute | solution.py:275
  72.3 2.3 %collective-permute-done.20.refs_3_ = bf16[64,512]{1,0:T(8,128)(2,1)S(1)} collective-permute-done((bf16[64,512]{1,0:T(8,128)(2,1)S(1)}, bf16[64,512]{1,0:T(8,128)(2,1)S(1)}, u32[]{:S(2)}, u32[]{:S(2)}) %collective-permute-start.20) | collective-permute-done | bytes 65568 | tf_op jit(solution)/shard_map/ppermute | solution.py:275
  74.6 1.4 %collective-permute-done.21.refs_4_ = bf16[64,512]{1,0:T(8,128)(2,1)S(1)} collective-permute-done((bf16[64,512]{1,0:T(8,128)(2,1)S(1)}, bf16[64,512]{1,0:T(8,128)(2,1)S(1)}, u32[]{:S(2)}, u32[]{:S(2)}) %collective-permute-start.21) | collective-permute-done | bytes 65568 | tf_op jit(solution)/shard_map/ppermute | solution.py:275
  76.0 0.0 collective-permute-done.19.refs_2_
  76.0 0.0 collective-permute-done.18.refs_1_
  76.0 2.4 %node_update.1 = (bf16[512,512]{1,0:T(8,128)(2,1)}, bf16[512,512]{1,0:T(8,128)(2,1)S(1)}, bf16[256,512]{1,0:T(8,128)(2,1)S(1)}, bf16[256,512]{1,0:T(8,128)(2,1)S(1)}) custom-call(s32[1,4]{1,0:T(1,128)S(1)} %collective-permute-done.5.mate_list_ref, s32[1,4]{1,0:T(1,128)S(1)} %collective-permute-done.6.other_list_ref, ...), custom_call_target="tpu_custom_call" | custom-call | tf_op jit(solution)/shard_map/node_update/pallas_call | solution.py:331
  78.4 2.7 %collective-permute-start.23 = (bf16[256,512]{1,0:T(8,128)(2,1)S(1)}, bf16[256,512]{1,0:T(8,128)(2,1)S(1)}, u32[]{:S(2)}, u32[]{:S(2)}) collective-permute-start(bf16[256,512]{1,0:T(8,128)(2,1)S(1)} %get-tuple-element.61), channel_id=1, source_target_pairs={{0,15},{1,2},{2,1},{3,4},{4,3},{5,6},{6,5},{7,8},{8,7},{9,10},{10,... | collective-permute-start | bytes 786440 | tf_op jit(solution)/shard_map/ppermute | solution.py:472
  81.1 1.1 %mesh_operator.1.operator_ref = bf16[512,1024]{1,0:T(8,128)(2,1)S(1)} custom-call(s32[12]{0:T(128)S(1)} %copy-done.7, s32[12]{0:T(128)S(1)} %copy-done.8, bf16[12,128,128]{2,1,0:T(8,128)(2,1)S(1)} %copy-done.4), custom_call_target="tpu_custom_call" | custom-call | tf_op jit(solution)/shard_map/mesh_operator/pallas_call | solution.py:364
  82.2 4.8 %collective-permute-done.23.other_ref = bf16[256,512]{1,0:T(8,128)(2,1)S(1)} collective-permute-done((bf16[256,512]{1,0:T(8,128)(2,1)S(1)}, bf16[256,512]{1,0:T(8,128)(2,1)S(1)}, u32[]{:S(2)}, u32[]{:S(2)}) %collective-permute-start.23) | collective-permute-done | bytes 262176 | tf_op jit(solution)/shard_map/ppermute | solution.py:472
  87.0 2.4 %process.1 = bf16[512,512]{1,0:T(8,128)(2,1)} custom-call(bf16[512,1024]{1,0:T(8,128)(2,1)S(1)} %mesh_operator.1.operator_ref, bf16[512,512]{1,0:T(8,128)(2,1)S(1)} %get-tuple-element.59.own_ref, bf16[256,512]{1,0:T(8,128)(2,1)S(1)} %collective-permute-done.22.mate_ref, bf16[256,512]{1,0:T(8,128)(2,1)S(1)} %collective-permute-done.23.other_ref, ...), custom_call_target="tpu_custom_call" | custom-call | tf_op jit(solution)/shard_map/process/pallas_call | solution.py:390
  (31 shorter events, 0.1 us)
Async XLA Ops:
  12.1 7.5 %copy-start.10 = (bf16[1024,512]{1,0:T(8,128)(2,1)S(1)}, bf16[1024,512]{1,0:T(8,128)(2,1)}, u32[]{:S(2)}) copy-start(bf16[1024,512]{1,0:T(8,128)(2,1)} %get-tuple-element.39) | copy-start | bytes 3145732
  12.2 2.9 %collective-permute-start.4 = (bf16[1024,512]{1,0:T(8,128)(2,1)}, bf16[1024,512]{1,0:T(8,128)(2,1)S(1)}, u32[]{:S(2)}, u32[]{:S(2)}) collective-permute-start(bf16[1024,512]{1,0:T(8,128)(2,1)} %get-tuple-element.36), channel_id=1, source_target_pairs={{0,1},{1,0},{2,3},{3,2},{4,5},{5,4},{6,7},{7,6},{8,9},{9,8},{10,11... | collective-permute-start | bytes 3145736 | tf_op jit(solution)/shard_map/ppermute | solution.py:275
  12.4 7.2 %collective-permute-start.3 = (bf16[1024,512]{1,0:T(8,128)(2,1)}, bf16[1024,512]{1,0:T(8,128)(2,1)S(1)}, u32[]{:S(2)}, u32[]{:S(2)}) collective-permute-start(bf16[1024,512]{1,0:T(8,128)(2,1)} %get-tuple-element.35), channel_id=1, source_target_pairs={{0,1},{1,0},{2,3},{3,2},{4,5},{5,4},{6,7},{7,6},{8,9},{9,8},{10,11... | collective-permute-start | bytes 3145736 | tf_op jit(solution)/shard_map/ppermute | solution.py:275
  12.7 7.3 %collective-permute-start.2 = (bf16[1024,512]{1,0:T(8,128)(2,1)}, bf16[1024,512]{1,0:T(8,128)(2,1)S(1)}, u32[]{:S(2)}, u32[]{:S(2)}) collective-permute-start(bf16[1024,512]{1,0:T(8,128)(2,1)} %get-tuple-element.34), channel_id=1, source_target_pairs={{0,1},{1,0},{2,3},{3,2},{4,5},{5,4},{6,7},{7,6},{8,9},{9,8},{10,11... | collective-permute-start | bytes 3145736 | tf_op jit(solution)/shard_map/ppermute | solution.py:275
  12.9 12.3 %collective-permute-start = (bf16[512,512]{1,0:T(8,128)(2,1)}, bf16[512,512]{1,0:T(8,128)(2,1)S(1)}, u32[]{:S(2)}, u32[]{:S(2)}) collective-permute-start(bf16[512,512]{1,0:T(8,128)(2,1)} %get-tuple-element.32), channel_id=1, source_target_pairs={{0,1},{1,0},{2,3},{3,2},{4,5},{5,4},{6,7},{7,6},{8,9},{9,8},{10,11... | collective-permute-start | bytes 1572872 | tf_op jit(solution)/shard_map/ppermute | solution.py:275
  13.2 10.1 %collective-permute-start.1 = (bf16[512,512]{1,0:T(8,128)(2,1)}, bf16[512,512]{1,0:T(8,128)(2,1)S(1)}, u32[]{:S(2)}, u32[]{:S(2)}) collective-permute-start(bf16[512,512]{1,0:T(8,128)(2,1)} %get-tuple-element.33), channel_id=1, source_target_pairs={{0,1},{1,0},{2,3},{3,2},{4,5},{5,4},{6,7},{7,6},{8,9},{9,8},{10,11... | collective-permute-start | bytes 1572872 | tf_op jit(solution)/shard_map/ppermute | solution.py:275
  16.6 3.5 %copy-start.9 = (bf16[1024,512]{1,0:T(8,128)(2,1)S(1)}, bf16[1024,512]{1,0:T(8,128)(2,1)}, u32[]{:S(2)}) copy-start(bf16[1024,512]{1,0:T(8,128)(2,1)} %get-tuple-element.41) | copy-start | bytes 3145732
  16.6 15.7 %collective-permute-start.7 = (bf16[512,512]{1,0:T(8,128)(2,1)S(1)}, bf16[512,512]{1,0:T(8,128)(2,1)S(1)}, u32[]{:S(2)}, u32[]{:S(2)}) collective-permute-start(bf16[512,512]{1,0:T(8,128)(2,1)S(1)} %get-tuple-element.67), channel_id=1, source_target_pairs={{0,2},{1,3},{2,0},{3,1},{4,6},{5,7},{6,4},{7,5},{8,10},{9,11},{10,... | collective-permute-start | bytes 1572872 | tf_op jit(solution)/shard_map/ppermute | solution.py:275
  19.9 3.4 %copy-start.12 = (bf16[512,512]{1,0:T(8,128)(2,1)S(1)}, bf16[512,512]{1,0:T(8,128)(2,1)}, u32[]{:S(2)}) copy-start(bf16[512,512]{1,0:T(8,128)(2,1)} %get-tuple-element.43) | copy-start | bytes 1572868
  20.0 23.6 %collective-permute-start.11 = (bf16[512,512]{1,0:T(8,128)(2,1)S(1)}, bf16[512,512]{1,0:T(8,128)(2,1)S(1)}, u32[]{:S(2)}, u32[]{:S(2)}) collective-permute-start(bf16[512,512]{1,0:T(8,128)(2,1)S(1)} %get-tuple-element.63), channel_id=1, source_target_pairs={{0,2},{1,3},{2,0},{3,1},{4,6},{5,7},{6,4},{7,5},{8,10},{9,11},{10,... | collective-permute-start | bytes 1572872 | tf_op jit(solution)/shard_map/ppermute | solution.py:275
  20.1 5.2 %copy-start.11 = (bf16[512,512]{1,0:T(8,128)(2,1)S(1)}, bf16[512,512]{1,0:T(8,128)(2,1)}, u32[]{:S(2)}) copy-start(bf16[512,512]{1,0:T(8,128)(2,1)} %get-tuple-element.45) | copy-start | bytes 1572868
  20.4 28.1 %collective-permute-start.10 = (bf16[512,512]{1,0:T(8,128)(2,1)S(1)}, bf16[512,512]{1,0:T(8,128)(2,1)S(1)}, u32[]{:S(2)}, u32[]{:S(2)}) collective-permute-start(bf16[512,512]{1,0:T(8,128)(2,1)S(1)} %get-tuple-element.65), channel_id=1, source_target_pairs={{0,8},{1,9},{2,10},{3,11},{4,12},{5,13},{6,14},{7,15},{8,0},{9,1},... | collective-permute-start | bytes 1572872 | tf_op jit(solution)/shard_map/ppermute | solution.py:275
  23.5 17.8 %collective-permute-start.12 = (bf16[256,512]{1,0:T(8,128)(2,1)S(1)}, bf16[256,512]{1,0:T(8,128)(2,1)S(1)}, u32[]{:S(2)}, u32[]{:S(2)}) collective-permute-start(bf16[256,512]{1,0:T(8,128)(2,1)S(1)} %get-tuple-element.73), channel_id=1, source_target_pairs={{0,4},{1,5},{2,6},{3,7},{4,0},{5,1},{6,2},{7,3},{8,12},{9,13},{10,... | collective-permute-start | bytes 786440 | tf_op jit(solution)/shard_map/ppermute | solution.py:275
  25.4 28.5 %collective-permute-start.9 = (bf16[256,512]{1,0:T(8,128)(2,1)S(1)}, bf16[256,512]{1,0:T(8,128)(2,1)S(1)}, u32[]{:S(2)}, u32[]{:S(2)}) collective-permute-start(bf16[256,512]{1,0:T(8,128)(2,1)S(1)} %get-tuple-element.75), channel_id=1, source_target_pairs={{0,4},{1,5},{2,6},{3,7},{4,0},{5,1},{6,2},{7,3},{8,12},{9,13},{10,... | collective-permute-start | bytes 786440 | tf_op jit(solution)/shard_map/ppermute | solution.py:275
  32.5 27.2 %collective-permute-start.8 = (bf16[256,512]{1,0:T(8,128)(2,1)S(1)}, bf16[256,512]{1,0:T(8,128)(2,1)S(1)}, u32[]{:S(2)}, u32[]{:S(2)}) collective-permute-start(bf16[256,512]{1,0:T(8,128)(2,1)S(1)} %get-tuple-element.76), channel_id=1, source_target_pairs={{0,8},{1,9},{2,10},{3,11},{4,12},{5,13},{6,14},{7,15},{8,0},{9,1},... | collective-permute-start | bytes 786440 | tf_op jit(solution)/shard_map/ppermute | solution.py:275
  41.4 12.7 %collective-permute-start.15 = (bf16[128,512]{1,0:T(8,128)(2,1)S(1)}, bf16[128,512]{1,0:T(8,128)(2,1)S(1)}, u32[]{:S(2)}, u32[]{:S(2)}) collective-permute-start(bf16[128,512]{1,0:T(8,128)(2,1)S(1)} %get-tuple-element.85), channel_id=1, source_target_pairs={{0,2},{1,3},{2,0},{3,1},{4,6},{5,7},{6,4},{7,5},{8,10},{9,11},{10,... | collective-permute-start | bytes 393224 | tf_op jit(solution)/shard_map/ppermute | solution.py:275
  43.7 16.1 %collective-permute-start.17 = (bf16[256,512]{1,0:T(8,128)(2,1)S(1)}, bf16[256,512]{1,0:T(8,128)(2,1)S(1)}, u32[]{:S(2)}, u32[]{:S(2)}) collective-permute-start(bf16[256,512]{1,0:T(8,128)(2,1)S(1)} %get-tuple-element.69), channel_id=1, source_target_pairs={{0,4},{1,5},{2,6},{3,7},{4,0},{5,1},{6,2},{7,3},{8,12},{9,13},{10,... | collective-permute-start | bytes 786440 | tf_op jit(solution)/shard_map/ppermute | solution.py:275
  48.6 14.9 %copy-start.13 = (s32[1,4]{1,0:T(1,128)S(1)}, s32[1,4]{1,0:T(1,128)}, u32[]{:S(2)}) copy-start(s32[1,4]{1,0:T(1,128)} %param.31) | copy-start | bytes 52
  48.6 27.4 %copy-start = (bf16[512,512]{1,0:T(8,128)(2,1)S(1)}, bf16[512,512]{1,0:T(8,128)(2,1)}, u32[]{:S(2)}) copy-start(bf16[512,512]{1,0:T(8,128)(2,1)} %refs_10_.1) | copy-start | bytes 1572868
  48.6 27.4 %copy-start.1 = (bf16[512,512]{1,0:T(8,128)(2,1)S(1)}, bf16[512,512]{1,0:T(8,128)(2,1)}, u32[]{:S(2)}) copy-start(bf16[512,512]{1,0:T(8,128)(2,1)} %refs_11_.1) | copy-start | bytes 1572868
  48.6 27.4 %copy-start.5 = (f32[512]{0:T(512)S(1)}, f32[512]{0:T(512)}, u32[]{:S(2)}) copy-start(f32[512]{0:T(512)} %param.30) | copy-start | bytes 6148
  48.6 9.6 %collective-permute-start.14 = (bf16[256,512]{1,0:T(8,128)(2,1)S(1)}, bf16[256,512]{1,0:T(8,128)(2,1)S(1)}, u32[]{:S(2)}, u32[]{:S(2)}) collective-permute-start(bf16[256,512]{1,0:T(8,128)(2,1)S(1)} %get-tuple-element.71), channel_id=1, source_target_pairs={{0,2},{1,3},{2,0},{3,1},{4,6},{5,7},{6,4},{7,5},{8,10},{9,11},{10,... | collective-permute-start | bytes 786440 | tf_op jit(solution)/shard_map/ppermute | solution.py:275
  54.0 5.7 %collective-permute-start.13 = (bf16[128,512]{1,0:T(8,128)(2,1)S(1)}, bf16[128,512]{1,0:T(8,128)(2,1)S(1)}, u32[]{:S(2)}, u32[]{:S(2)}) collective-permute-start(bf16[128,512]{1,0:T(8,128)(2,1)S(1)} %get-tuple-element.86), channel_id=1, source_target_pairs={{0,2},{1,3},{2,0},{3,1},{4,6},{5,7},{6,4},{7,5},{8,10},{9,11},{10,... | collective-permute-start | bytes 393224 | tf_op jit(solution)/shard_map/ppermute | solution.py:275
  58.3 22.8 %copy-start.4 = (bf16[12,128,128]{2,1,0:T(8,128)(2,1)S(1)}, bf16[12,128,128]{2,1,0:T(8,128)(2,1)}, u32[]{:S(2)}) copy-start(bf16[12,128,128]{2,1,0:T(8,128)(2,1)} %values_ref) | copy-start | bytes 1179652
  58.3 22.8 %copy-start.7 = (s32[12]{0:T(128)S(1)}, s32[12]{0:T(128)}, u32[]{:S(2)}) copy-start(s32[12]{0:T(128)} %dst_ref.3) | copy-start | bytes 148
  58.3 22.8 %copy-start.8 = (s32[12]{0:T(128)S(1)}, s32[12]{0:T(128)}, u32[]{:S(2)}) copy-start(s32[12]{0:T(128)} %src_ref.3) | copy-start | bytes 148
  58.3 17.6 %collective-permute-start.19 = (bf16[128,512]{1,0:T(8,128)(2,1)S(1)}, bf16[128,512]{1,0:T(8,128)(2,1)S(1)}, u32[]{:S(2)}, u32[]{:S(2)}) collective-permute-start(bf16[128,512]{1,0:T(8,128)(2,1)S(1)} %get-tuple-element.79), channel_id=1, source_target_pairs={{0,4},{1,5},{2,6},{3,7},{4,0},{5,1},{6,2},{7,3},{8,12},{9,13},{10,... | collective-permute-start | bytes 393224 | tf_op jit(solution)/shard_map/ppermute | solution.py:275
  59.8 27.2 %copy-start.2 = (bf16[512,512]{1,0:T(8,128)(2,1)S(1)}, bf16[512,512]{1,0:T(8,128)(2,1)}, u32[]{:S(2)}) copy-start(bf16[512,512]{1,0:T(8,128)(2,1)} %proc_in_ref.1) | copy-start | bytes 1572868
  59.8 27.2 %copy-start.3 = (bf16[512,512]{1,0:T(8,128)(2,1)S(1)}, bf16[512,512]{1,0:T(8,128)(2,1)}, u32[]{:S(2)}) copy-start(bf16[512,512]{1,0:T(8,128)(2,1)} %proc_out_ref.1) | copy-start | bytes 1572868
  59.8 27.2 %copy-start.6 = (f32[512]{0:T(512)S(1)}, f32[512]{0:T(512)}, u32[]{:S(2)}) copy-start(f32[512]{0:T(512)} %param.37) | copy-start | bytes 6148
  59.9 16.1 %collective-permute-start.18 = (bf16[128,512]{1,0:T(8,128)(2,1)S(1)}, bf16[128,512]{1,0:T(8,128)(2,1)S(1)}, u32[]{:S(2)}, u32[]{:S(2)}) collective-permute-start(bf16[128,512]{1,0:T(8,128)(2,1)S(1)} %get-tuple-element.81), channel_id=1, source_target_pairs={{0,8},{1,9},{2,10},{3,11},{4,12},{5,13},{6,14},{7,15},{8,0},{9,1},... | collective-permute-start | bytes 393224 | tf_op jit(solution)/shard_map/ppermute | solution.py:275
  61.8 14.2 %collective-permute-start.16 = (bf16[128,512]{1,0:T(8,128)(2,1)S(1)}, bf16[128,512]{1,0:T(8,128)(2,1)S(1)}, u32[]{:S(2)}, u32[]{:S(2)}) collective-permute-start(bf16[128,512]{1,0:T(8,128)(2,1)S(1)} %get-tuple-element.83), channel_id=1, source_target_pairs={{0,4},{1,5},{2,6},{3,7},{4,0},{5,1},{6,2},{7,3},{8,12},{9,13},{10,... | collective-permute-start | bytes 393224 | tf_op jit(solution)/shard_map/ppermute | solution.py:275
  63.5 5.9 %collective-permute-start.6 = (s32[1,4]{1,0:T(1,128)S(1)}, s32[1,4]{1,0:T(1,128)S(1)}, u32[]{:S(2)}, u32[]{:S(2)}) collective-permute-start(s32[1,4]{1,0:T(1,128)S(1)} %copy-done.13), channel_id=1, source_target_pairs={{0,15},{1,2},{2,1},{3,4},{4,3},{5,6},{6,5},{7,8},{8,7},{9,10},{10,... | collective-permute-start | bytes 56 | tf_op jit(solution)/shard_map/ppermute | solution.py:469
  63.5 5.9 %collective-permute-start.5 = (s32[1,4]{1,0:T(1,128)S(1)}, s32[1,4]{1,0:T(1,128)S(1)}, u32[]{:S(2)}, u32[]{:S(2)}) collective-permute-start(s32[1,4]{1,0:T(1,128)S(1)} %copy-done.13), channel_id=1, source_target_pairs={{0,1},{1,0},{2,3},{3,2},{4,5},{5,4},{6,7},{7,6},{8,9},{9,8},{10,11... | collective-permute-start | bytes 56 | tf_op jit(solution)/shard_map/ppermute | solution.py:469
  69.3 5.2 %collective-permute-start.20 = (bf16[64,512]{1,0:T(8,128)(2,1)S(1)}, bf16[64,512]{1,0:T(8,128)(2,1)S(1)}, u32[]{:S(2)}, u32[]{:S(2)}) collective-permute-start(bf16[64,512]{1,0:T(8,128)(2,1)S(1)} %get-tuple-element.91), channel_id=1, source_target_pairs={{0,8},{1,9},{2,10},{3,11},{4,12},{5,13},{6,14},{7,15},{8,0},{9,1},... | collective-permute-start | bytes 196616 | tf_op jit(solution)/shard_map/ppermute | solution.py:275
  69.4 6.6 %collective-permute-start.21 = (bf16[64,512]{1,0:T(8,128)(2,1)S(1)}, bf16[64,512]{1,0:T(8,128)(2,1)S(1)}, u32[]{:S(2)}, u32[]{:S(2)}) collective-permute-start(bf16[64,512]{1,0:T(8,128)(2,1)S(1)} %get-tuple-element.89), channel_id=1, source_target_pairs={{0,8},{1,9},{2,10},{3,11},{4,12},{5,13},{6,14},{7,15},{8,0},{9,1},... | collective-permute-start | bytes 196616 | tf_op jit(solution)/shard_map/ppermute | solution.py:275
  78.4 3.8 %collective-permute-start.22 = (bf16[256,512]{1,0:T(8,128)(2,1)S(1)}, bf16[256,512]{1,0:T(8,128)(2,1)S(1)}, u32[]{:S(2)}, u32[]{:S(2)}) collective-permute-start(bf16[256,512]{1,0:T(8,128)(2,1)S(1)} %get-tuple-element.60), channel_id=1, source_target_pairs={{0,1},{1,0},{2,3},{3,2},{4,5},{5,4},{6,7},{7,6},{8,9},{9,8},{10,11... | collective-permute-start | bytes 786440 | tf_op jit(solution)/shard_map/ppermute | solution.py:473
  78.4 8.6 %collective-permute-start.23 = (bf16[256,512]{1,0:T(8,128)(2,1)S(1)}, bf16[256,512]{1,0:T(8,128)(2,1)S(1)}, u32[]{:S(2)}, u32[]{:S(2)}) collective-permute-start(bf16[256,512]{1,0:T(8,128)(2,1)S(1)} %get-tuple-element.61), channel_id=1, source_target_pairs={{0,15},{1,2},{2,1},{3,4},{4,3},{5,6},{6,5},{7,8},{8,7},{9,10},{10,... | collective-permute-start | bytes 786440 | tf_op jit(solution)/shard_map/ppermute | solution.py:472

commit v4 on v3

--- a/solution.py
+++ b/solution.py
@@ -8,9 +8,10 @@
 from jax.sharding import PartitionSpec as P
 
 EPSILON = 1e-05
-ORDERS = ((1, 3, 2), (1, 2, 3), (3, 1, 2), (2, 1, 3), (2, 1, 3))
-SHARES = (2, 2, 2, 1, 1)
-TURNS = (0, 1, 2, 3, 4, 0, 3, 1, 2, 4, 3, 2, 4, 0, 1)
+ORDERS = ((1, 2, 3), (2, 1, 3), (3, 1, 2), (1, 2, 3))
+SHARES = (2, 2, 2, 2)
+TURNS = (2, 0, 1, 3, 0, 1, 2, 3, 0, 1, 2, 3)
+EARLY = 1
 VMEM_BYTES = 24 * 1024 * 1024
 GRID_VMEM_BYTES = 60 * 1024 * 1024
 VMEM = pl.BlockSpec(memory_space=pltpu.VMEM)
@@ -275,75 +276,81 @@
     return lax.ppermute(cells, "space", [(i, i ^ (1 << bit)) for i in range(count)])
 
 
-def reduce_chunks(mates, owns, orders, turns, later):
+def reduce_chunks(mates, owns, orders, turns, lists):
     arrived = [exchange(mate, 0) for mate in mates]
     kept = list(owns)
     made = [0] * len(orders)
     for turn, chunk in enumerate(turns):
         received = arrived[chunk]
-        if turn > 0:
+        if turn == len(orders):
+            received, _, lists = lax.optimization_barrier((received, previous, lists))
+        elif turn > 0:
             received, _ = lax.optimization_barrier((received, previous))
         half = kept[chunk].shape[0] // 2
         previous = add(received[half:], kept[chunk][half:]).astype(jnp.bfloat16)
         kept[chunk] = add(received[:half], kept[chunk][:half]).astype(jnp.bfloat16)
         arrived[chunk] = exchange(previous, orders[chunk][made[chunk]])
         made[chunk] += 1
-        if turn == len(orders) - 1:
-            later = lax.optimization_barrier((later, previous))[0]
-    return arrived, kept, later
-
-
-def node_kernel(parts, reads, rows, mate_list_ref, other_list_ref, *refs):
-    summands = refs[:parts]
-    node_in_ref, node_out_ref, gain_ref, encoded_ref, own_ref, to_mate_ref, to_other_ref = refs[parts:]
+    return arrived, kept, lists
+
+
+def node_kernel(held, parts, earlier, reads, mate_list_ref, other_list_ref, *refs):
+    summands, refs = refs[:parts], refs[parts:]
+    if earlier:
+        earlier_ref, refs = refs[0], refs[1:]
+    node_in_ref, node_out_ref, gain_ref, to_mate_ref, to_other_ref = refs[:5]
+    encoded_refs = refs[5:]
     if parts == 1:
         summed = summands[0][...]
     else:
-        chunks = parts // 2
-        held = encoded_ref.shape[0] // rows
-        pieces = [add(summands[chunk][...], summands[chunks + chunk][...]) for chunk in range(chunks)]
-        cuts = [piece.shape[0] // held for piece in pieces]
-        summed = jnp.concatenate(
-            [
-                piece[block * cut : (block + 1) * cut]
-                for block in range(held)
-                for piece, cut in zip(pieces, cuts)
-            ],
-            axis=0,
-        )
+        pieces = []
+        for block in range(held):
+            for arrived, kept in zip(summands[: parts // 2], summands[parts // 2 :]):
+                cut = arrived.shape[0] // held
+                piece = slice(block * cut, (block + 1) * cut)
+                pieces.append(add(arrived[piece, :], kept[piece, :]))
+        summed = jnp.concatenate(pieces, axis=0)
+    rows = summed.shape[0] // held
     hidden = silu(matmul(summed.astype(jnp.bfloat16), node_in_ref[...])).astype(jnp.bfloat16)
     encoded = (summed + gain_ref[...] * normalize(matmul(hidden, node_out_ref[...]))).astype(jnp.bfloat16)
-    encoded_ref[...] = encoded
-    own_ref[...] = encoded
+    for out in encoded_refs:
+        if earlier:
+            ahead = earlier_ref.shape[0] // held
+            for block in range(held):
+                first = block * (ahead + rows)
+                out[first : first + ahead, :] = earlier_ref[block * ahead : (block + 1) * ahead, :]
+                out[first + ahead : first + ahead + rows, :] = encoded[block * rows : (block + 1) * rows]
+        else:
+            out[...] = encoded
+    encoded_ref = encoded_refs[0]
     odd = lax.rem(lax.axis_index("space"), 2)
+    whole = encoded_ref.shape[0] // held
     for index in range(reads):
         for wanted_ref, first, out in (
             (mate_list_ref, odd * reads, to_mate_ref),
             (other_list_ref, (1 - odd) * reads, to_other_ref),
         ):
-            start = pl.multiple_of(wanted_ref[0, first + index] * rows, rows)
+            start = pl.multiple_of(wanted_ref[0, first + index] * whole + (whole - rows), 16)
             out[index * rows : (index + 1) * rows, :] = encoded_ref[pl.ds(start, rows), :]
 
 
-def encode(summands, node_in, node_out, node_gain, lists, held, rows):
+def encode(summands, earlier, node_in, node_out, node_gain, lists, held, copies):
     channels = node_in.shape[0]
     reads = lists[0].shape[1] // 2
+    count = sum(summand.shape[0] for summand in summands) // (2 if len(summands) > 1 else 1)
+    sent = jax.ShapeDtypeStruct((count // held * reads, channels), jnp.bfloat16)
+    total = jax.ShapeDtypeStruct((count + sum(part.shape[0] for part in earlier), channels), jnp.bfloat16)
     return pl.pallas_call(
-        functools.partial(node_kernel, len(summands), reads, rows),
-        in_specs=[SMEM] * 2 + [VMEM] * (len(summands) + 3),
-        out_specs=[VMEM] * 4,
-        out_shape=[
-            jax.ShapeDtypeStruct((held * rows, channels), jnp.bfloat16),
-            jax.ShapeDtypeStruct((held * rows, channels), jnp.bfloat16),
-            jax.ShapeDtypeStruct((reads * rows, channels), jnp.bfloat16),
-            jax.ShapeDtypeStruct((reads * rows, channels), jnp.bfloat16),
-        ],
+        functools.partial(node_kernel, held, len(summands), len(earlier), reads),
+        in_specs=[SMEM] * 2 + [VMEM] * (len(summands) + len(earlier) + 3),
+        out_specs=[VMEM] * (2 + copies),
+        out_shape=[sent] * 2 + [total] * copies,
         compiler_params=pltpu.CompilerParams(vmem_limit_bytes=VMEM_BYTES),
         name="node_update",
-    )(*lists, *summands, node_in, node_out, node_gain.reshape(1, -1))
-
-
-def operator_kernel(held, reads, dst_ref, src_ref, values_ref, operator_ref, total):
+    )(*lists, *summands, *earlier, node_in, node_out, node_gain.reshape(1, -1))
+
+
+def operator_kernel(held, reads, splits, dst_ref, src_ref, values_ref, operator_ref, total):
     edges, rows, _ = values_ref.shape
     odd = lax.rem(lax.axis_index("space"), 2)
     total[...] = jnp.zeros_like(total)
@@ -354,15 +361,18 @@
         source = jnp.where(side == 1, 2 * reads, across * reads) + index
         first = pl.multiple_of(dst_ref[edge] * rows, rows)
         total[source, pl.ds(first, rows), :] += values_ref[edge].astype(jnp.float32)
-    for source in range(2 * reads + held):
-        operator_ref[:, source * rows : (source + 1) * rows] = total[source].astype(jnp.bfloat16)
-
-
-def mesh_operator(mesh_values, mesh_dst, mesh_src, held, reads):
+    columns = [
+        total[source][:, low:high].astype(jnp.bfloat16) for low, high in splits for source in range(2 * reads)
+    ]
+    columns += [total[source].astype(jnp.bfloat16) for source in range(2 * reads, 2 * reads + held)]
+    operator_ref[...] = jnp.concatenate(columns, axis=1)
+
+
+def mesh_operator(mesh_values, mesh_dst, mesh_src, held, reads, splits):
     rows = mesh_values.shape[1]
     sources = 2 * reads + held
     return pl.pallas_call(
-        functools.partial(operator_kernel, held, reads),
+        functools.partial(operator_kernel, held, reads, splits),
         in_specs=[SMEM] * 2 + [VMEM],
         out_specs=VMEM,
         out_shape=jax.ShapeDtypeStruct((held * rows, sources * rows), jnp.bfloat16),
@@ -372,29 +382,24 @@
     )(mesh_dst, mesh_src, mesh_values)
 
 
-def process_kernel(
-    operator_ref, own_ref, mate_ref, other_ref, proc_in_ref, proc_out_ref, gain_ref, processed_ref
-):
-    message = 0.0
-    first = 0
-    for source_ref in (mate_ref, other_ref, own_ref):
-        last = first + source_ref.shape[0]
-        message = message + matmul(operator_ref[:, first:last], source_ref[...])
-        first = last
+def process_kernel(operator_ref, own_ref, *refs):
+    halos, (proc_in_ref, proc_out_ref, gain_ref, processed_ref) = refs[:-4], refs[-4:]
+    sources = jnp.concatenate([halo[...] for halo in halos] + [own_ref[...]], axis=0)
+    message = matmul(operator_ref[...], sources)
     hidden = silu(matmul(message.astype(jnp.bfloat16), proc_in_ref[...])).astype(jnp.bfloat16)
     update = gain_ref[...] * normalize(matmul(hidden, proc_out_ref[...]))
     processed_ref[...] = (own_ref[...].astype(jnp.float32) + update).astype(jnp.bfloat16)
 
 
-def process(operator, own, from_mate, from_other, proc_in, proc_out, proc_gain):
+def process(operator, own, halos, proc_in, proc_out, proc_gain):
     return pl.pallas_call(
         process_kernel,
-        in_specs=[VMEM] * 7,
+        in_specs=[VMEM] * (5 + len(halos)),
         out_specs=VMEM,
         out_shape=jax.ShapeDtypeStruct(own.shape, jnp.bfloat16),
         compiler_params=pltpu.CompilerParams(vmem_limit_bytes=VMEM_BYTES),
         name="process",
-    )(operator, own, from_mate, from_other, proc_in, proc_out, proc_gain.reshape(1, -1))
+    )(operator, own, *halos, proc_in, proc_out, proc_gain.reshape(1, -1))
 
 
 def lookup(table, wanted):
@@ -457,21 +462,30 @@
     mates = [(i, i ^ 1) for i in range(partitions)]
     others = [(i, (i + 1 if i % 2 else i - 1) % partitions) for i in range(partitions)]
     grid_args = (grid_inputs, grid_count, embed_in, embed_out, grid_gain, g2m_values, g2m_src, g2m_dst, mesh_place)
+    lists = (lax.ppermute(recv_blocks, "space", mates), lax.ppermute(recv_blocks, "space", others))
+    splits = [(0, rows)]
+    halos = []
+    earlier = []
     if partitions == 1 << (1 + len(ORDERS[0])) and edges % partitions == 0 and edges >= mesh_blocks:
         cuts = [share * rows // sum(SHARES) for share in SHARES]
         sums = slab_sums(*grid_args, partitions, ORDERS, cuts)
-        arrived, kept, (recv_blocks, mesh_values) = reduce_chunks(
-            sums[: len(cuts)], sums[len(cuts) :], ORDERS, TURNS, (recv_blocks, mesh_values)
-        )
-        summands = arrived + kept
+        arrived, kept, lists = reduce_chunks(sums[: len(cuts)], sums[len(cuts) :], ORDERS, TURNS, lists)
+        if EARLY:
+            first = sum(cuts[:EARLY])
+            splits = [(0, first), (first, rows)]
+            to_mate, to_other, ahead = encode(
+                arrived[:EARLY] + kept[:EARLY], [], node_in, node_out, node_gain, lists, held, 1
+            )
+            halos = [lax.ppermute(to_mate, "space", mates), lax.ppermute(to_other, "space", others)]
+            arrived[-1], ahead, halos = lax.optimization_barrier((arrived[-1], ahead, halos))
+            earlier = [ahead]
+        summands = arrived[EARLY:] + kept[EARLY:]
     else:
         summands = [routed_sum(*grid_args, partitions)]
-    lists = (lax.ppermute(recv_blocks, "space", mates), lax.ppermute(recv_blocks, "space", others))
-    operator = mesh_operator(mesh_values, mesh_dst, mesh_src, held, reads)
-    encoded, own, to_mate, to_other = encode(summands, node_in, node_out, node_gain, lists, held, rows)
-    from_other = lax.ppermute(to_other, "space", others)
-    from_mate = lax.ppermute(to_mate, "space", mates)
-    processed = process(operator, own, from_mate, from_other, proc_in, proc_out, proc_gain)
+    operator = mesh_operator(mesh_values, mesh_dst, mesh_src, held, reads, splits)
+    to_mate, to_other, encoded, own = encode(summands, earlier, node_in, node_out, node_gain, lists, held, 2)
+    halos += [lax.ppermute(to_mate, "space", mates), lax.ppermute(to_other, "space", others)]
+    processed = process(operator, own, halos, proc_in, proc_out, proc_gain)
     return (encoded, processed)
 
 

time: 89.7 us -> 86.7 us (0.967)
  starting transfers between devices: 33.6 us -> 23.8 us
  waiting for transfers between devices: 34.3 us -> 39.2 us
  Pallas kernels: 16.7 us -> 17.6 us
    ppermute x20 -> x16, starting transfers between devices: 29 us -> 10.4 us  [exchange(): lax.ppermute(cells, 'space', [(i, i ^ 1 << bit) for i in range(count)])]
    ppermute x20 -> x16, waiting for transfers between devices: 25.5 us -> 34.8 us  [exchange(): lax.ppermute(cells, 'space', [(i, i ^ 1 << bit) for i in range(count)])]
    ppermute x1, starting transfers between devices: 0.01 us -> 6.16 us  [shards(): lax.ppermute(recv_blocks, 'space', others)]
    ppermute x2 -> x4, starting transfers between devices: 2.75 us -> 6.88 us  [the longest x2 6.81 us: shards(): lax.ppermute(to_other, 'space', others)]
    ppermute x1, waiting for transfers between devices: 3.99 us -> 0.01 us  [shards(): lax.ppermute(recv_blocks, 'space', others)]
    ppermute x1, starting transfers between devices: 1.85 us -> 0.43 us  [shards(): lax.ppermute(recv_blocks, 'space', mates)]
    pallas_call x3 -> x4, Pallas kernels: 5.8 us -> 6.9 us  [the longest x2 3.39 us: encode(): pl.pallas_call(functools.partial(node_kernel, held, len(summands), len(ea...]
    ppermute x2 -> x4, waiting for transfers between devices: 4.78 us -> 4.39 us  [the longest x2 4.39 us: shards(): lax.ppermute(to_other, 'space', others)]
  transfers between devices with their start and end apart: 24 -> 22, of which waited for: 11 -> 11; matrix products, arithmetic and copies ran while one was open for 4% -> 4% of each run, Pallas kernels for 1% -> 3%
where the time goes in v4:
time: 86.7 us; the launch traced here: 86.2 us
  waiting for transfers between devices  39.2 us (45%)
  starting transfers between devices  23.8 us (27%)
  Pallas kernels  17.6 us (20%)
  other arithmetic  3.28 us (4%)
  between operations  1.56 us (2%)
    ppermute x16, waiting for transfers between devices, exchange(): lax.ppermute(cells, 'space', [(i, i ^ 1 << bit) for i in range(count)])  34.8 us
    pallas_call x1, Pallas kernels, slab_sums(): pl.pallas_call(functools.partial(grid_kernel, held, capacity, orders, cut...  10.8 us
    ppermute x16, starting transfers between devices, exchange(): lax.ppermute(cells, 'space', [(i, i ^ 1 << bit) for i in range(count)])  10.4 us
    ppermute x2, starting transfers between devices, shards(): lax.ppermute(to_other, 'space', others)  6.81 us
    ppermute x1, starting transfers between devices, shards(): lax.ppermute(recv_blocks, 'space', others)  6.16 us
    ppermute x2, waiting for transfers between devices, shards(): lax.ppermute(to_other, 'space', others)  4.39 us
    pallas_call x2, Pallas kernels, encode(): pl.pallas_call(functools.partial(node_kernel, held, len(summands), len(ea...  3.39 us
    convert_element_type x11, other arithmetic, reduce_chunks(): kept[chunk] = add(received[:half], kept[chunk][:half]).astype(jnp.bfloat16)  3.14 us
  transfers between devices with their start and end apart: 22, of which 11 were waited for; matrix products, arithmetic and copies ran while one was open for 4% of the time, Pallas kernels for 3%

profile of v4, /device:TPU:0, one launch (start us, length us, event | category | flops | bytes accessed | tf_op | source)
XLA Modules:
  0.0 86.2 jit_solution(16995759583426106658)
XLA Ops:
  1.3 10.8 %grid_to_mesh.1 = (bf16[1024,512]{1,0:T(8,128)(2,1)}, bf16[1024,512]{1,0:T(8,128)(2,1)}, bf16[1024,512]{1,0:T(8,128)(2,1)}, bf16[1024,512]{1,0:T(8,128)(2,1)}, b...) custom-call(s32[64]{0:T(128)} %src_ref.2, ...), custom_call_target="tpu_custom_call" | custom-call | tf_op jit(solution)/shard_map/grid_to_mesh/pallas_call | solution.py:240
  12.1 0.7 collective-permute-start.1
  12.8 0.1 collective-permute-start
  12.9 0.4 collective-permute-start.4
  13.3 0.1 collective-permute-start.3
  13.4 0.4 collective-permute-start.5
  13.8 1.5 %collective-permute-done.1 = bf16[1024,512]{1,0:T(8,128)(2,1)S(1)} collective-permute-done((bf16[1024,512]{1,0:T(8,128)(2,1)}, bf16[1024,512]{1,0:T(8,128)(2,1)S(1)}, u32[]{:S(2)}, u32[]{:S(2)}) %collective-permute-start.1) | collective-permute-done | bytes 1048608 | tf_op jit(solution)/shard_map/ppermute | solution.py:276
  15.3 6.2 %collective-permute-start.6 = (s32[1,4]{1,0:T(1,128)S(1)}, s32[1,4]{1,0:T(1,128)S(1)}, u32[]{:S(2)}, u32[]{:S(2)}) collective-permute-start(s32[1,4]{1,0:T(1,128)S(1)} %copy-done.12), channel_id=1, source_target_pairs={{0,15},{1,2},{2,1},{3,4},{4,3},{5,6},{6,5},{7,8},{8,7},{9,10},{10,... | collective-permute-start | bytes 56 | tf_op jit(solution)/shard_map/ppermute | solution.py:465
  21.5 1.5 %add_convert_fusion.1 = (bf16[512,512]{1,0:T(8,128)(2,1)S(1)}, bf16[512,512]{1,0:T(8,128)(2,1)S(1)}) fusion(bf16[1024,512]{1,0:T(8,128)(2,1)S(1)} %collective-permute-done.1, bf16[1024,512]{1,0:T(8,128)(2,1)} %get-tuple-element.36), kind=kLoop, calls=%fused_computation.1 | loop fusion | flops 2097152 | bytes 3145728 | tf_op jit(solution)/shard_map/convert_element_type | solution.py:291
  23.0 0.0 collective-permute-done
  23.0 0.1 collective-permute-start.11
  23.1 0.3 add_convert_fusion.3
  23.4 0.0 collective-permute-done.4
  23.4 0.1 collective-permute-start.2
  23.5 0.7 copy-done.10
  24.2 0.3 add_convert_fusion.2
  24.5 0.0 collective-permute-done.3
  24.5 0.7 collective-permute-start.7
  25.3 0.3 add_convert_fusion
  25.6 1.2 %collective-permute-start.10 = (bf16[512,512]{1,0:T(8,128)(2,1)S(1)}, bf16[512,512]{1,0:T(8,128)(2,1)S(1)}, u32[]{:S(2)}, u32[]{:S(2)}) collective-permute-start(bf16[512,512]{1,0:T(8,128)(2,1)S(1)} %get-tuple-element.69), channel_id=1, source_target_pairs={{0,2},{1,3},{2,0},{3,1},{4,6},{5,7},{6,4},{7,5},{8,10},{9,11},{10,... | collective-permute-start | bytes 1572872 | tf_op jit(solution)/shard_map/ppermute | solution.py:276
  26.8 0.0 collective-permute-done.6.other_list_ref
  26.8 11.6 %collective-permute-done.2 = bf16[512,512]{1,0:T(8,128)(2,1)S(1)} collective-permute-done((bf16[512,512]{1,0:T(8,128)(2,1)S(1)}, bf16[512,512]{1,0:T(8,128)(2,1)S(1)}, u32[]{:S(2)}, u32[]{:S(2)}) %collective-permute-start.2) | collective-permute-done | bytes 524320 | tf_op jit(solution)/shard_map/ppermute | solution.py:276
  38.3 0.1 add_convert_fusion.11
  38.5 0.4 collective-permute-start.9
  38.9 10.1 %collective-permute-done.7 = bf16[512,512]{1,0:T(8,128)(2,1)S(1)} collective-permute-done((bf16[512,512]{1,0:T(8,128)(2,1)S(1)}, bf16[512,512]{1,0:T(8,128)(2,1)S(1)}, u32[]{:S(2)}, u32[]{:S(2)}) %collective-permute-start.7) | collective-permute-done | bytes 524320 | tf_op jit(solution)/shard_map/ppermute | solution.py:276
  49.0 0.1 add_convert_fusion.14
  49.2 1.5 %collective-permute-start.8 = (bf16[256,512]{1,0:T(8,128)(2,1)S(1)}, bf16[256,512]{1,0:T(8,128)(2,1)S(1)}, u32[]{:S(2)}, u32[]{:S(2)}) collective-permute-start(bf16[256,512]{1,0:T(8,128)(2,1)S(1)} %get-tuple-element.80), channel_id=1, source_target_pairs={{0,2},{1,3},{2,0},{3,1},{4,6},{5,7},{6,4},{7,5},{8,10},{9,11},{10,... | collective-permute-start | bytes 786440 | tf_op jit(solution)/shard_map/ppermute | solution.py:276
  50.7 0.0 collective-permute-done.11
  50.7 0.1 add_convert_fusion.9
  50.8 0.6 collective-permute-start.13
  51.5 0.0 collective-permute-done.10
  51.5 0.1 add_convert_fusion.8
  51.6 0.2 collective-permute-start.15
  51.9 2.8 %collective-permute-done.9 = bf16[256,512]{1,0:T(8,128)(2,1)S(1)} collective-permute-done((bf16[256,512]{1,0:T(8,128)(2,1)S(1)}, bf16[256,512]{1,0:T(8,128)(2,1)S(1)}, u32[]{:S(2)}, u32[]{:S(2)}) %collective-permute-start.9) | collective-permute-done | bytes 262176 | tf_op jit(solution)/shard_map/ppermute | solution.py:276
  54.7 0.1 add_convert_fusion.19
  54.7 0.9 %collective-permute-start.17 = (bf16[128,512]{1,0:T(8,128)(2,1)S(1)}, bf16[128,512]{1,0:T(8,128)(2,1)S(1)}, u32[]{:S(2)}, u32[]{:S(2)}) collective-permute-start(bf16[128,512]{1,0:T(8,128)(2,1)S(1)} %get-tuple-element.89), channel_id=1, source_target_pairs={{0,8},{1,9},{2,10},{3,11},{4,12},{5,13},{6,14},{7,15},{8,0},{9,1},... | collective-permute-start | bytes 393224 | tf_op jit(solution)/shard_map/ppermute | solution.py:276
  55.7 2.6 %collective-permute-done.8 = bf16[256,512]{1,0:T(8,128)(2,1)S(1)} collective-permute-done((bf16[256,512]{1,0:T(8,128)(2,1)S(1)}, bf16[256,512]{1,0:T(8,128)(2,1)S(1)}, u32[]{:S(2)}, u32[]{:S(2)}) %collective-permute-start.8) | collective-permute-done | bytes 262176 | tf_op jit(solution)/shard_map/ppermute | solution.py:276
  58.2 0.1 add_convert_fusion.18
  58.3 2.7 %collective-permute-done.13 = bf16[256,512]{1,0:T(8,128)(2,1)S(1)} collective-permute-done((bf16[256,512]{1,0:T(8,128)(2,1)S(1)}, bf16[256,512]{1,0:T(8,128)(2,1)S(1)}, u32[]{:S(2)}, u32[]{:S(2)}) %collective-permute-start.13) | collective-permute-done | bytes 262176 | tf_op jit(solution)/shard_map/ppermute | solution.py:276
  61.1 0.1 add_convert_fusion.17
  61.1 0.0 copy-start.4
  61.1 0.0 copy-start.7
  61.2 0.0 copy-start.8
  61.2 0.5 collective-permute-done.15
  61.7 0.1 add_convert_fusion.16
  61.7 0.6 collective-permute-start.16
  62.4 1.6 %collective-permute-start.14 = (bf16[128,512]{1,0:T(8,128)(2,1)S(1)}, bf16[128,512]{1,0:T(8,128)(2,1)S(1)}, u32[]{:S(2)}, u32[]{:S(2)}) collective-permute-start(bf16[128,512]{1,0:T(8,128)(2,1)S(1)} %get-tuple-element.85), channel_id=1, source_target_pairs={{0,4},{1,5},{2,6},{3,7},{4,0},{5,1},{6,2},{7,3},{8,12},{9,13},{10,... | collective-permute-start | bytes 393224 | tf_op jit(solution)/shard_map/ppermute | solution.py:276
  64.0 1.0 %collective-permute-start.12 = (bf16[128,512]{1,0:T(8,128)(2,1)S(1)}, bf16[128,512]{1,0:T(8,128)(2,1)S(1)}, u32[]{:S(2)}, u32[]{:S(2)}) collective-permute-start(bf16[128,512]{1,0:T(8,128)(2,1)S(1)} %get-tuple-element.87), channel_id=1, source_target_pairs={{0,8},{1,9},{2,10},{3,11},{4,12},{5,13},{6,14},{7,15},{8,0},{9,1},... | collective-permute-start | bytes 393224 | tf_op jit(solution)/shard_map/ppermute | solution.py:276
  65.0 0.0 copy-start.2
  65.0 0.0 copy-start.3
  65.0 0.0 copy-start.6
  65.0 1.2 %node_update.2 = (bf16[64,512]{1,0:T(8,128)(2,1)S(1)}, bf16[64,512]{1,0:T(8,128)(2,1)S(1)}, bf16[128,512]{1,0:T(8,128)(2,1)S(1)}) custom-call(s32[1,4]{1,0:T(1,128)S(1)} %collective-permute-done.5.mate_list_ref, s32[1,4]{1,0:T(1,128)S(1)} %collective-permute-done.6.other_list_ref, bf16[128,512]{1,0:T(8,128)(2,1)S(1)} %collective-permute-done.17.refs_0_, ...), custom_call_target="tpu_custom_call" | custom-call | tf_op jit(solution)/shard_map/node_update/pallas_call | solution.py:343
  66.2 0.1 collective-permute-start.18
  66.3 3.2 %collective-permute-start.19 = (bf16[64,512]{1,0:T(8,128)(2,1)S(1)}, bf16[64,512]{1,0:T(8,128)(2,1)S(1)}, u32[]{:S(2)}, u32[]{:S(2)}) collective-permute-start(bf16[64,512]{1,0:T(8,128)(2,1)S(1)} %get-tuple-element.57), channel_id=1, source_target_pairs={{0,15},{1,2},{2,1},{3,4},{4,3},{5,6},{6,5},{7,8},{8,7},{9,10},{10,... | collective-permute-start | bytes 196616 | tf_op jit(solution)/shard_map/ppermute | solution.py:479
  69.4 2.9 %collective-permute-done.16.refs_2_ = bf16[128,512]{1,0:T(8,128)(2,1)S(1)} collective-permute-done((bf16[128,512]{1,0:T(8,128)(2,1)S(1)}, bf16[128,512]{1,0:T(8,128)(2,1)S(1)}, u32[]{:S(2)}, u32[]{:S(2)}) %collective-permute-start.16) | collective-permute-done | bytes 131104 | tf_op jit(solution)/shard_map/ppermute | solution.py:276
  72.3 1.3 %collective-permute-done.19.refs_1_ = bf16[64,512]{1,0:T(8,128)(2,1)S(1)} collective-permute-done((bf16[64,512]{1,0:T(8,128)(2,1)S(1)}, bf16[64,512]{1,0:T(8,128)(2,1)S(1)}, u32[]{:S(2)}, u32[]{:S(2)}) %collective-permute-start.19) | collective-permute-done | bytes 65568 | tf_op jit(solution)/shard_map/ppermute | solution.py:479
  73.6 0.0 collective-permute-done.14.refs_1_
  73.6 0.1 collective-permute-done.12.refs_0_
  73.7 2.2 %node_update.3 = (bf16[192,512]{1,0:T(8,128)(2,1)S(1)}, bf16[192,512]{1,0:T(8,128)(2,1)S(1)}, bf16[512,512]{1,0:T(8,128)(2,1)}, bf16[512,512]{1,0:T(8,128)(2,1)S(1)}) custom-call(s32[1,4]{1,0:T(1,128)S(1)} %collective-permute-done.5.mate_list_ref, s32[1,4]{1,0:T(1,128)S(1)} %collective-permute-done.6.other_list_ref, ...), custom_call_target="tpu_custom_call" | custom-call | tf_op jit(solution)/shard_map/node_update/pallas_call | solution.py:343
  75.9 3.6 %collective-permute-start.21 = (bf16[192,512]{1,0:T(8,128)(2,1)S(1)}, bf16[192,512]{1,0:T(8,128)(2,1)S(1)}, u32[]{:S(2)}, u32[]{:S(2)}) collective-permute-start(bf16[192,512]{1,0:T(8,128)(2,1)S(1)} %get-tuple-element.65), channel_id=1, source_target_pairs={{0,15},{1,2},{2,1},{3,4},{4,3},{5,6},{6,5},{7,8},{8,7},{9,10},{10,... | collective-permute-start | bytes 589832 | tf_op jit(solution)/shard_map/ppermute | solution.py:487
  79.6 1.1 %mesh_operator.1.operator_ref = bf16[512,1024]{1,0:T(8,128)(2,1)S(1)} custom-call(s32[12]{0:T(128)S(1)} %copy-done.7, s32[12]{0:T(128)S(1)} %copy-done.8, bf16[12,128,128]{2,1,0:T(8,128)(2,1)S(1)} %copy-done.4), custom_call_target="tpu_custom_call" | custom-call | tf_op jit(solution)/shard_map/mesh_operator/pallas_call | solution.py:374
  80.7 0.0 collective-permute-done.20.refs_2_
  80.7 3.1 %collective-permute-done.21.refs_3_ = bf16[192,512]{1,0:T(8,128)(2,1)S(1)} collective-permute-done((bf16[192,512]{1,0:T(8,128)(2,1)S(1)}, bf16[192,512]{1,0:T(8,128)(2,1)S(1)}, u32[]{:S(2)}, u32[]{:S(2)}) %collective-permute-start.21) | collective-permute-done | bytes 196640 | tf_op jit(solution)/shard_map/ppermute | solution.py:487
  83.8 2.4 %process.1 = bf16[512,512]{1,0:T(8,128)(2,1)} custom-call(bf16[512,1024]{1,0:T(8,128)(2,1)S(1)} %mesh_operator.1.operator_ref, bf16[512,512]{1,0:T(8,128)(2,1)S(1)} %get-tuple-element.61.own_ref, bf16[64,512]{1,0:T(8,128)(2,1)S(1)} %collective-permute-done.18.refs_0_, bf16[64,512]{1,0:T(8,128)(2,1)S(1)} %collective-permute-done.19.refs_1_, ...), custom_call_target="tpu_custom_call" | custom-call | tf_op jit(solution)/shard_map/process/pallas_call | solution.py:395
  (23 shorter events, 0.0 us)
Async XLA Ops:
  0.6 12.8 %copy-start.12 = (s32[1,4]{1,0:T(1,128)S(1)}, s32[1,4]{1,0:T(1,128)}, u32[]{:S(2)}) copy-start(s32[1,4]{1,0:T(1,128)} %param.31) | copy-start | bytes 52
  12.1 11.0 %copy-start.11 = (bf16[1024,512]{1,0:T(8,128)(2,1)S(1)}, bf16[1024,512]{1,0:T(8,128)(2,1)}, u32[]{:S(2)}) copy-start(bf16[1024,512]{1,0:T(8,128)(2,1)} %get-tuple-element.38) | copy-start | bytes 3145732
  12.1 3.2 %collective-permute-start.1 = (bf16[1024,512]{1,0:T(8,128)(2,1)}, bf16[1024,512]{1,0:T(8,128)(2,1)S(1)}, u32[]{:S(2)}, u32[]{:S(2)}) collective-permute-start(bf16[1024,512]{1,0:T(8,128)(2,1)} %get-tuple-element.35), channel_id=1, source_target_pairs={{0,1},{1,0},{2,3},{3,2},{4,5},{5,4},{6,7},{7,6},{8,9},{9,8},{10,11... | collective-permute-start | bytes 3145736 | tf_op jit(solution)/shard_map/ppermute | solution.py:276
  12.8 10.2 %collective-permute-start = (bf16[1024,512]{1,0:T(8,128)(2,1)}, bf16[1024,512]{1,0:T(8,128)(2,1)S(1)}, u32[]{:S(2)}, u32[]{:S(2)}) collective-permute-start(bf16[1024,512]{1,0:T(8,128)(2,1)} %get-tuple-element.34), channel_id=1, source_target_pairs={{0,1},{1,0},{2,3},{3,2},{4,5},{5,4},{6,7},{7,6},{8,9},{9,8},{10,11... | collective-permute-start | bytes 3145736 | tf_op jit(solution)/shard_map/ppermute | solution.py:276
  12.9 10.5 %collective-permute-start.4 = (bf16[1024,512]{1,0:T(8,128)(2,1)}, bf16[1024,512]{1,0:T(8,128)(2,1)S(1)}, u32[]{:S(2)}, u32[]{:S(2)}) collective-permute-start(bf16[1024,512]{1,0:T(8,128)(2,1)} %get-tuple-element.40), channel_id=1, source_target_pairs={{0,1},{1,0},{2,3},{3,2},{4,5},{5,4},{6,7},{7,6},{8,9},{9,8},{10,11... | collective-permute-start | bytes 3145736 | tf_op jit(solution)/shard_map/ppermute | solution.py:276
  13.3 11.2 %collective-permute-start.3 = (bf16[1024,512]{1,0:T(8,128)(2,1)}, bf16[1024,512]{1,0:T(8,128)(2,1)S(1)}, u32[]{:S(2)}, u32[]{:S(2)}) collective-permute-start(bf16[1024,512]{1,0:T(8,128)(2,1)} %get-tuple-element.39), channel_id=1, source_target_pairs={{0,1},{1,0},{2,3},{3,2},{4,5},{5,4},{6,7},{7,6},{8,9},{9,8},{10,11... | collective-permute-start | bytes 3145736 | tf_op jit(solution)/shard_map/ppermute | solution.py:276
  13.4 12.2 %collective-permute-start.5 = (s32[1,4]{1,0:T(1,128)S(1)}, s32[1,4]{1,0:T(1,128)S(1)}, u32[]{:S(2)}, u32[]{:S(2)}) collective-permute-start(s32[1,4]{1,0:T(1,128)S(1)} %copy-done.12), channel_id=1, source_target_pairs={{0,1},{1,0},{2,3},{3,2},{4,5},{5,4},{6,7},{7,6},{8,9},{9,8},{10,11... | collective-permute-start | bytes 56 | tf_op jit(solution)/shard_map/ppermute | solution.py:465
  15.3 11.4 %collective-permute-start.6 = (s32[1,4]{1,0:T(1,128)S(1)}, s32[1,4]{1,0:T(1,128)S(1)}, u32[]{:S(2)}, u32[]{:S(2)}) collective-permute-start(s32[1,4]{1,0:T(1,128)S(1)} %copy-done.12), channel_id=1, source_target_pairs={{0,15},{1,2},{2,1},{3,4},{4,3},{5,6},{6,5},{7,8},{8,7},{9,10},{10,... | collective-permute-start | bytes 56 | tf_op jit(solution)/shard_map/ppermute | solution.py:465
  23.0 1.2 %copy-start.10 = (bf16[1024,512]{1,0:T(8,128)(2,1)S(1)}, bf16[1024,512]{1,0:T(8,128)(2,1)}, u32[]{:S(2)}) copy-start(bf16[1024,512]{1,0:T(8,128)(2,1)} %get-tuple-element.42) | copy-start | bytes 3145732
  23.0 27.7 %collective-permute-start.11 = (bf16[512,512]{1,0:T(8,128)(2,1)S(1)}, bf16[512,512]{1,0:T(8,128)(2,1)S(1)}, u32[]{:S(2)}, u32[]{:S(2)}) collective-permute-start(bf16[512,512]{1,0:T(8,128)(2,1)S(1)} %get-tuple-element.67), channel_id=1, source_target_pairs={{0,8},{1,9},{2,10},{3,11},{4,12},{5,13},{6,14},{7,15},{8,0},{9,1},... | collective-permute-start | bytes 1572872 | tf_op jit(solution)/shard_map/ppermute | solution.py:276
  23.4 1.9 %copy-start.9 = (bf16[1024,512]{1,0:T(8,128)(2,1)S(1)}, bf16[1024,512]{1,0:T(8,128)(2,1)}, u32[]{:S(2)}) copy-start(bf16[1024,512]{1,0:T(8,128)(2,1)} %get-tuple-element.44) | copy-start | bytes 3145732
  23.4 14.9 %collective-permute-start.2 = (bf16[512,512]{1,0:T(8,128)(2,1)S(1)}, bf16[512,512]{1,0:T(8,128)(2,1)S(1)}, u32[]{:S(2)}, u32[]{:S(2)}) collective-permute-start(bf16[512,512]{1,0:T(8,128)(2,1)S(1)} %get-tuple-element.71), channel_id=1, source_target_pairs={{0,2},{1,3},{2,0},{3,1},{4,6},{5,7},{6,4},{7,5},{8,10},{9,11},{10,... | collective-permute-start | bytes 1572872 | tf_op jit(solution)/shard_map/ppermute | solution.py:276
  24.5 24.5 %collective-permute-start.7 = (bf16[512,512]{1,0:T(8,128)(2,1)S(1)}, bf16[512,512]{1,0:T(8,128)(2,1)S(1)}, u32[]{:S(2)}, u32[]{:S(2)}) collective-permute-start(bf16[512,512]{1,0:T(8,128)(2,1)S(1)} %get-tuple-element.73), channel_id=1, source_target_pairs={{0,4},{1,5},{2,6},{3,7},{4,0},{5,1},{6,2},{7,3},{8,12},{9,13},{10,... | collective-permute-start | bytes 1572872 | tf_op jit(solution)/shard_map/ppermute | solution.py:276
  25.6 25.9 %collective-permute-start.10 = (bf16[512,512]{1,0:T(8,128)(2,1)S(1)}, bf16[512,512]{1,0:T(8,128)(2,1)S(1)}, u32[]{:S(2)}, u32[]{:S(2)}) collective-permute-start(bf16[512,512]{1,0:T(8,128)(2,1)S(1)} %get-tuple-element.69), channel_id=1, source_target_pairs={{0,2},{1,3},{2,0},{3,1},{4,6},{5,7},{6,4},{7,5},{8,10},{9,11},{10,... | collective-permute-start | bytes 1572872 | tf_op jit(solution)/shard_map/ppermute | solution.py:276
  38.5 16.2 %collective-permute-start.9 = (bf16[256,512]{1,0:T(8,128)(2,1)S(1)}, bf16[256,512]{1,0:T(8,128)(2,1)S(1)}, u32[]{:S(2)}, u32[]{:S(2)}) collective-permute-start(bf16[256,512]{1,0:T(8,128)(2,1)S(1)} %get-tuple-element.79), channel_id=1, source_target_pairs={{0,4},{1,5},{2,6},{3,7},{4,0},{5,1},{6,2},{7,3},{8,12},{9,13},{10,... | collective-permute-start | bytes 786440 | tf_op jit(solution)/shard_map/ppermute | solution.py:276
  49.2 9.1 %collective-permute-start.8 = (bf16[256,512]{1,0:T(8,128)(2,1)S(1)}, bf16[256,512]{1,0:T(8,128)(2,1)S(1)}, u32[]{:S(2)}, u32[]{:S(2)}) collective-permute-start(bf16[256,512]{1,0:T(8,128)(2,1)S(1)} %get-tuple-element.80), channel_id=1, source_target_pairs={{0,2},{1,3},{2,0},{3,1},{4,6},{5,7},{6,4},{7,5},{8,10},{9,11},{10,... | collective-permute-start | bytes 786440 | tf_op jit(solution)/shard_map/ppermute | solution.py:276
  50.8 10.2 %collective-permute-start.13 = (bf16[256,512]{1,0:T(8,128)(2,1)S(1)}, bf16[256,512]{1,0:T(8,128)(2,1)S(1)}, u32[]{:S(2)}, u32[]{:S(2)}) collective-permute-start(bf16[256,512]{1,0:T(8,128)(2,1)S(1)} %get-tuple-element.77), channel_id=1, source_target_pairs={{0,2},{1,3},{2,0},{3,1},{4,6},{5,7},{6,4},{7,5},{8,10},{9,11},{10,... | collective-permute-start | bytes 786440 | tf_op jit(solution)/shard_map/ppermute | solution.py:276
  51.5 13.5 %copy-start = (bf16[512,512]{1,0:T(8,128)(2,1)S(1)}, bf16[512,512]{1,0:T(8,128)(2,1)}, u32[]{:S(2)}) copy-start(bf16[512,512]{1,0:T(8,128)(2,1)} %refs_7_.1) | copy-start | bytes 1572868
  51.5 13.5 %copy-start.1 = (bf16[512,512]{1,0:T(8,128)(2,1)S(1)}, bf16[512,512]{1,0:T(8,128)(2,1)}, u32[]{:S(2)}) copy-start(bf16[512,512]{1,0:T(8,128)(2,1)} %refs_8_.1) | copy-start | bytes 1572868
  51.5 13.5 %copy-start.5 = (f32[512]{0:T(512)S(1)}, f32[512]{0:T(512)}, u32[]{:S(2)}) copy-start(f32[512]{0:T(512)} %param.30) | copy-start | bytes 6148
  51.6 10.0 %collective-permute-start.15 = (bf16[256,512]{1,0:T(8,128)(2,1)S(1)}, bf16[256,512]{1,0:T(8,128)(2,1)S(1)}, u32[]{:S(2)}, u32[]{:S(2)}) collective-permute-start(bf16[256,512]{1,0:T(8,128)(2,1)S(1)} %get-tuple-element.75), channel_id=1, source_target_pairs={{0,4},{1,5},{2,6},{3,7},{4,0},{5,1},{6,2},{7,3},{8,12},{9,13},{10,... | collective-permute-start | bytes 786440 | tf_op jit(solution)/shard_map/ppermute | solution.py:276
  54.7 10.2 %collective-permute-start.17 = (bf16[128,512]{1,0:T(8,128)(2,1)S(1)}, bf16[128,512]{1,0:T(8,128)(2,1)S(1)}, u32[]{:S(2)}, u32[]{:S(2)}) collective-permute-start(bf16[128,512]{1,0:T(8,128)(2,1)S(1)} %get-tuple-element.89), channel_id=1, source_target_pairs={{0,8},{1,9},{2,10},{3,11},{4,12},{5,13},{6,14},{7,15},{8,0},{9,1},... | collective-permute-start | bytes 393224 | tf_op jit(solution)/shard_map/ppermute | solution.py:276
  61.1 18.4 %copy-start.4 = (bf16[12,128,128]{2,1,0:T(8,128)(2,1)S(1)}, bf16[12,128,128]{2,1,0:T(8,128)(2,1)}, u32[]{:S(2)}) copy-start(bf16[12,128,128]{2,1,0:T(8,128)(2,1)} %values_ref.1) | copy-start | bytes 1179652
  61.1 18.4 %copy-start.7 = (s32[12]{0:T(128)S(1)}, s32[12]{0:T(128)}, u32[]{:S(2)}) copy-start(s32[12]{0:T(128)} %dst_ref.3) | copy-start | bytes 148
  61.2 18.4 %copy-start.8 = (s32[12]{0:T(128)S(1)}, s32[12]{0:T(128)}, u32[]{:S(2)}) copy-start(s32[12]{0:T(128)} %src_ref.3) | copy-start | bytes 148
  61.7 10.6 %collective-permute-start.16 = (bf16[128,512]{1,0:T(8,128)(2,1)S(1)}, bf16[128,512]{1,0:T(8,128)(2,1)S(1)}, u32[]{:S(2)}, u32[]{:S(2)}) collective-permute-start(bf16[128,512]{1,0:T(8,128)(2,1)S(1)} %get-tuple-element.83), channel_id=1, source_target_pairs={{0,8},{1,9},{2,10},{3,11},{4,12},{5,13},{6,14},{7,15},{8,0},{9,1},... | collective-permute-start | bytes 393224 | tf_op jit(solution)/shard_map/ppermute | solution.py:276
  62.4 11.2 %collective-permute-start.14 = (bf16[128,512]{1,0:T(8,128)(2,1)S(1)}, bf16[128,512]{1,0:T(8,128)(2,1)S(1)}, u32[]{:S(2)}, u32[]{:S(2)}) collective-permute-start(bf16[128,512]{1,0:T(8,128)(2,1)S(1)} %get-tuple-element.85), channel_id=1, source_target_pairs={{0,4},{1,5},{2,6},{3,7},{4,0},{5,1},{6,2},{7,3},{8,12},{9,13},{10,... | collective-permute-start | bytes 393224 | tf_op jit(solution)/shard_map/ppermute | solution.py:276
  64.0 9.7 %collective-permute-start.12 = (bf16[128,512]{1,0:T(8,128)(2,1)S(1)}, bf16[128,512]{1,0:T(8,128)(2,1)S(1)}, u32[]{:S(2)}, u32[]{:S(2)}) collective-permute-start(bf16[128,512]{1,0:T(8,128)(2,1)S(1)} %get-tuple-element.87), channel_id=1, source_target_pairs={{0,8},{1,9},{2,10},{3,11},{4,12},{5,13},{6,14},{7,15},{8,0},{9,1},... | collective-permute-start | bytes 393224 | tf_op jit(solution)/shard_map/ppermute | solution.py:276
  65.0 18.9 %copy-start.2 = (bf16[512,512]{1,0:T(8,128)(2,1)S(1)}, bf16[512,512]{1,0:T(8,128)(2,1)}, u32[]{:S(2)}) copy-start(bf16[512,512]{1,0:T(8,128)(2,1)} %refs_4_.1) | copy-start | bytes 1572868
  65.0 18.9 %copy-start.3 = (bf16[512,512]{1,0:T(8,128)(2,1)S(1)}, bf16[512,512]{1,0:T(8,128)(2,1)}, u32[]{:S(2)}) copy-start(bf16[512,512]{1,0:T(8,128)(2,1)} %refs_5_.1) | copy-start | bytes 1572868
  65.0 18.8 %copy-start.6 = (f32[512]{0:T(512)S(1)}, f32[512]{0:T(512)}, u32[]{:S(2)}) copy-start(f32[512]{0:T(512)} %param.37) | copy-start | bytes 6148
  66.2 6.1 %collective-permute-start.18 = (bf16[64,512]{1,0:T(8,128)(2,1)S(1)}, bf16[64,512]{1,0:T(8,128)(2,1)S(1)}, u32[]{:S(2)}, u32[]{:S(2)}) collective-permute-start(bf16[64,512]{1,0:T(8,128)(2,1)S(1)} %get-tuple-element.56), channel_id=1, source_target_pairs={{0,1},{1,0},{2,3},{3,2},{4,5},{5,4},{6,7},{7,6},{8,9},{9,8},{10,11... | collective-permute-start | bytes 196616 | tf_op jit(solution)/shard_map/ppermute | solution.py:479
  66.3 7.3 %collective-permute-start.19 = (bf16[64,512]{1,0:T(8,128)(2,1)S(1)}, bf16[64,512]{1,0:T(8,128)(2,1)S(1)}, u32[]{:S(2)}, u32[]{:S(2)}) collective-permute-start(bf16[64,512]{1,0:T(8,128)(2,1)S(1)} %get-tuple-element.57), channel_id=1, source_target_pairs={{0,15},{1,2},{2,1},{3,4},{4,3},{5,6},{6,5},{7,8},{8,7},{9,10},{10,... | collective-permute-start | bytes 196616 | tf_op jit(solution)/shard_map/ppermute | solution.py:479
  75.9 4.8 %collective-permute-start.20 = (bf16[192,512]{1,0:T(8,128)(2,1)S(1)}, bf16[192,512]{1,0:T(8,128)(2,1)S(1)}, u32[]{:S(2)}, u32[]{:S(2)}) collective-permute-start(bf16[192,512]{1,0:T(8,128)(2,1)S(1)} %get-tuple-element.64), channel_id=1, source_target_pairs={{0,1},{1,0},{2,3},{3,2},{4,5},{5,4},{6,7},{7,6},{8,9},{9,8},{10,11... | collective-permute-start | bytes 589832 | tf_op jit(solution)/shard_map/ppermute | solution.py:487
  75.9 7.9 %collective-permute-start.21 = (bf16[192,512]{1,0:T(8,128)(2,1)S(1)}, bf16[192,512]{1,0:T(8,128)(2,1)S(1)}, u32[]{:S(2)}, u32[]{:S(2)}) collective-permute-start(bf16[192,512]{1,0:T(8,128)(2,1)S(1)} %get-tuple-element.65), channel_id=1, source_target_pairs={{0,15},{1,2},{2,1},{3,4},{4,3},{5,6},{6,5},{7,8},{8,7},{9,10},{10,... | collective-permute-start | bytes 589832 | tf_op jit(solution)/shard_map/ppermute | solution.py:487

commit v5 on v4

--- a/solution.py
+++ b/solution.py
@@ -13,10 +13,10 @@
 TURNS = (2, 0, 1, 3, 0, 1, 2, 3, 0, 1, 2, 3)
 EARLY = 1
 VMEM_BYTES = 24 * 1024 * 1024
-GRID_VMEM_BYTES = 60 * 1024 * 1024
+GRID_VMEM_BYTES = 43 * 1024 * 1024
 VMEM = pl.BlockSpec(memory_space=pltpu.VMEM)
 SMEM = pl.BlockSpec(memory_space=pltpu.SMEM)
-ANY = pl.BlockSpec(memory_space=pl.ANY)
+HBM = pl.BlockSpec(memory_space=pltpu.HBM)
 
 
 def silu(values):
@@ -56,50 +56,30 @@
     orders,
     cuts,
     tile_rows,
-    src_ref,
-    dst_ref,
-    place_ref,
-    count_ref,
-    gain_ref,
-    inputs_hbm,
-    embed_in_hbm,
-    embed_out_hbm,
+    edges,
+    table_ref,
+    inputs_ref,
+    embed_in_ref,
+    embed_out_ref,
     values_hbm,
     *refs,
 ):
     chunks = len(orders)
     outs = (refs[chunks : 2 * chunks], refs[:chunks])
     (
-        inputs_ref,
-        embed_in_ref,
-        embed_out_ref,
         values_ref,
         latent,
-        staged,
         edge_of,
         filled,
         crowded_of,
         crowded,
-        load_sems,
-        store_sems,
+        load_sem,
     ) = refs[2 * chunks :]
     rows = values_ref.shape[1]
-    edges = src_ref.shape[0]
     slots = edges // capacity
     pairs = slots // 2
-    loads = [
-        pltpu.make_async_copy(source, target, load_sems.at[index])
-        for index, (source, target) in enumerate(
-            (
-                (inputs_hbm, inputs_ref),
-                (embed_in_hbm, embed_in_ref),
-                (embed_out_hbm, embed_out_ref),
-                (values_hbm, values_ref),
-            )
-        )
-    ]
-    for load in loads[:3]:
-        load.start()
+    load = pltpu.make_async_copy(values_hbm, values_ref, load_sem)
+    load.start()
 
     me = lax.axis_index("space")
 
@@ -109,27 +89,20 @@
             edge_of[bin_ * capacity + index] = 0
         return carry
 
-    def clear_pair(pair, carry):
-        crowded[pair] = 0
-        return carry
-
     lax.fori_loop(0, slots * held, clear, 0)
-    lax.fori_loop(0, pairs, clear_pair, 0)
+    crowded[0] = 0
 
     def sort(edge):
-        bin_ = place_ref[dst_ref[edge]] ^ (me * held)
+        bin_ = table_ref[2 * edges + table_ref[edges + edge]] ^ (me * held)
         count = filled[bin_]
         edge_of[bin_ * capacity + count] = edge
         filled[bin_] = count + 1
-        pair = lax.div(bin_, 2 * held)
-        seen = crowded[pair]
-        crowded_of[pair * 2 * held + seen] = bin_
-        crowded[pair] = seen + (count == 2).astype(jnp.int32)
-
-    for load in loads[:3]:
-        load.wait()
-    loads[3].start()
-
+        seen = crowded[0]
+        crowded_of[seen] = bin_
+        crowded[0] = seen + (count == 2).astype(jnp.int32)
+
+
+    alive = table_ref[table_ref.shape[0] - 1]
     tiles = latent.shape[0] // tile_rows
     sorted_each = edges // tiles
 
@@ -139,32 +112,15 @@
         first = pl.multiple_of(tile * tile_rows, tile_rows)
         columns = inputs_ref[:, pl.ds(first, tile_rows)]
         hidden = silu(transposed_matmul(columns, embed_in_ref[...])).astype(jnp.bfloat16)
-        scaled = normalize(matmul(hidden, embed_out_ref[...])) * gain_ref[...]
+        normal = normalize(matmul(hidden, embed_out_ref[...]))
         row = first + lax.broadcasted_iota(jnp.int32, (tile_rows, 1), 0)
-        latent[pl.ds(first, tile_rows), :] = jnp.where(row < count_ref[0], scaled, 0.0).astype(jnp.bfloat16)
+        latent[pl.ds(first, tile_rows), :] = jnp.where(row < alive, normal, 0.0).astype(jnp.bfloat16)
         return carry
 
     lax.fori_loop(0, tiles, embed, 0, unroll=True)
     for edge in range(tiles * sorted_each, edges):
         sort(edge)
-    loads[3].wait()
-
-    def stores(pair):
-        copies = []
-        for side in range(2):
-            first = 0
-            for chunk, order in enumerate(orders):
-                count = held * cuts[chunk]
-                start = pl.multiple_of(place_of(pair, order) * count, count)
-                copies.append(
-                    pltpu.make_async_copy(
-                        staged.at[pair, side, pl.ds(first, count), :],
-                        outs[side][chunk].at[pl.ds(start, count), :],
-                        store_sems.at[pair, side, chunk],
-                    )
-                )
-                first += count
-        return copies
+    load.wait()
 
     def product(bin_, first, count):
         operator = []
@@ -173,15 +129,15 @@
             edge = jnp.where(count > index, edge_of[bin_ * capacity + index], 0)
             values = values_ref[edge]
             operator.append(jnp.where(count > index, values, jnp.zeros_like(values)))
-            start = pl.multiple_of(src_ref[edge] * rows, rows)
+            start = pl.multiple_of(table_ref[edge] * rows, rows)
             sources.append(latent[pl.ds(start, rows), :])
         return matmul(jnp.concatenate(operator, axis=1), jnp.concatenate(sources, axis=0))
 
-    def stage(pair, side, block, summed):
+    def store(pair, side, block, summed):
         top = 0
-        for cut in cuts:
-            first = pl.multiple_of(top * held + block * cut, 16)
-            staged[pair, side, pl.ds(first, cut), :] = summed[top : top + cut].astype(jnp.bfloat16)
+        for out, order, cut in zip(outs[side], orders, cuts):
+            first = pl.multiple_of((place_of(pair, order) * held + block) * cut, 16)
+            out[pl.ds(first, cut), :] = summed[top : top + cut].astype(jnp.bfloat16)
             top += cut
 
     def multiply(turn, carry):
@@ -189,31 +145,29 @@
             for side in range(2):
                 for block in range(held):
                     bin_ = (2 * pair + side) * held + block
-                    stage(pair, side, block, product(bin_, 0, filled[bin_]))
-
-        def revisit(pair, index, carry):
-            bin_ = crowded_of[pair * 2 * held + index]
-            count = filled[bin_]
-            summed = product(bin_, 0, count)
-            for first in range(2, capacity, 2):
-                summed = summed + product(bin_, first, count)
-            stage(pair, lax.div(lax.rem(bin_, 2 * held), held), lax.rem(bin_, held), summed)
-            return carry
-
-        for pair in (2 * turn, 2 * turn + 1):
-            lax.fori_loop(0, crowded[pair], functools.partial(revisit, pair), 0)
-            for copy in stores(pair):
-                copy.start()
+                    store(pair, side, block, product(bin_, 0, filled[bin_]))
+
         return carry
 
     lax.fori_loop(0, pairs // 2, multiply, 0)
 
-    def finish(pair, carry):
-        for copy in stores(pair):
-            copy.wait()
+    def revisit(index, carry):
+        bin_ = crowded_of[index]
+        count = filled[bin_]
+        summed = product(bin_, 0, count)
+        for first in range(2, capacity, 2):
+            summed = summed + product(bin_, first, count)
+        pair = lax.div(bin_, 2 * held)
+        side = lax.rem(lax.div(bin_, held), 2)
+        for each in range(2):
+
+            @pl.when(side == each)
+            def _(each=each):
+                store(pair, each, lax.rem(bin_, held), summed)
+
         return carry
 
-    lax.fori_loop(0, pairs, finish, 0)
+    lax.fori_loop(0, crowded[0], revisit, 0)
 
 
 def slab_sums(
@@ -221,7 +175,6 @@
     grid_count,
     embed_in,
     embed_out,
-    grid_gain,
     g2m_values,
     g2m_src,
     g2m_dst,
@@ -238,37 +191,22 @@
     pairs = partitions // 2
     shapes = [jax.ShapeDtypeStruct((pairs * held * cut, channels), jnp.bfloat16) for cut in cuts]
     return pl.pallas_call(
-        functools.partial(grid_kernel, held, capacity, orders, cuts, min(512, slab_rows)),
-        in_specs=[SMEM] * 4 + [VMEM] + [ANY] * 4,
-        out_specs=[ANY] * (2 * len(cuts)),
+        functools.partial(grid_kernel, held, capacity, orders, cuts, min(512, slab_rows), edges),
+        in_specs=[SMEM] + [VMEM] * 3 + [HBM],
+        out_specs=[VMEM] * (2 * len(cuts)),
         out_shape=shapes * 2,
         scratch_shapes=[
-            pltpu.VMEM(grid_inputs.shape, jnp.bfloat16),
-            pltpu.VMEM(embed_in.shape, jnp.bfloat16),
-            pltpu.VMEM(embed_out.shape, jnp.bfloat16),
             pltpu.VMEM(g2m_values.shape, jnp.bfloat16),
             pltpu.VMEM((slab_rows, channels), jnp.bfloat16),
-            pltpu.VMEM((pairs, 2, held * rows, channels), jnp.bfloat16),
             pltpu.SMEM((partitions * held * capacity,), jnp.int32),
             pltpu.SMEM((partitions * held,), jnp.int32),
             pltpu.SMEM((partitions * held + 1,), jnp.int32),
-            pltpu.SMEM((pairs,), jnp.int32),
-            pltpu.SemaphoreType.DMA((4,)),
-            pltpu.SemaphoreType.DMA((pairs, 2, len(cuts))),
+            pltpu.SMEM((1,), jnp.int32),
+            pltpu.SemaphoreType.DMA,
         ],
         compiler_params=pltpu.CompilerParams(vmem_limit_bytes=GRID_VMEM_BYTES),
         name="grid_to_mesh",
-    )(
-        g2m_src,
-        g2m_dst,
-        mesh_place,
-        grid_count,
-        grid_gain.reshape(1, -1),
-        grid_inputs,
-        embed_in,
-        embed_out,
-        g2m_values,
-    )
+    )(jnp.concatenate([g2m_src, g2m_dst, mesh_place, grid_count]), grid_inputs, embed_in, embed_out, g2m_values)
 
 
 def exchange(cells, bit):
@@ -298,10 +236,10 @@
     summands, refs = refs[:parts], refs[parts:]
     if earlier:
         earlier_ref, refs = refs[0], refs[1:]
-    node_in_ref, node_out_ref, gain_ref, to_mate_ref, to_other_ref = refs[:5]
-    encoded_refs = refs[5:]
+    node_in_ref, node_out_ref, gain_ref, scale_ref, to_mate_ref, to_other_ref = refs[:6]
+    encoded_refs = refs[6:]
     if parts == 1:
-        summed = summands[0][...]
+        summed = summands[0][...] * scale_ref[...]
     else:
         pieces = []
         for block in range(held):
@@ -309,7 +247,7 @@
                 cut = arrived.shape[0] // held
                 piece = slice(block * cut, (block + 1) * cut)
                 pieces.append(add(arrived[piece, :], kept[piece, :]))
-        summed = jnp.concatenate(pieces, axis=0)
+        summed = jnp.concatenate(pieces, axis=0) * scale_ref[...]
     rows = summed.shape[0] // held
     hidden = silu(matmul(summed.astype(jnp.bfloat16), node_in_ref[...])).astype(jnp.bfloat16)
     encoded = (summed + gain_ref[...] * normalize(matmul(hidden, node_out_ref[...]))).astype(jnp.bfloat16)
@@ -334,7 +272,7 @@
             out[index * rows : (index + 1) * rows, :] = encoded_ref[pl.ds(start, rows), :]
 
 
-def encode(summands, earlier, node_in, node_out, node_gain, lists, held, copies):
+def encode(summands, earlier, scale, node_in, node_out, node_gain, lists, held, copies):
     channels = node_in.shape[0]
     reads = lists[0].shape[1] // 2
     count = sum(summand.shape[0] for summand in summands) // (2 if len(summands) > 1 else 1)
@@ -342,12 +280,12 @@
     total = jax.ShapeDtypeStruct((count + sum(part.shape[0] for part in earlier), channels), jnp.bfloat16)
     return pl.pallas_call(
         functools.partial(node_kernel, held, len(summands), len(earlier), reads),
-        in_specs=[SMEM] * 2 + [VMEM] * (len(summands) + len(earlier) + 3),
+        in_specs=[SMEM] * 2 + [VMEM] * (len(summands) + len(earlier) + 4),
         out_specs=[VMEM] * (2 + copies),
         out_shape=[sent] * 2 + [total] * copies,
         compiler_params=pltpu.CompilerParams(vmem_limit_bytes=VMEM_BYTES),
         name="node_update",
-    )(*lists, *summands, *earlier, node_in, node_out, node_gain.reshape(1, -1))
+    )(*lists, *summands, *earlier, node_in, node_out, node_gain.reshape(1, -1), scale.reshape(1, -1))
 
 
 def operator_kernel(held, reads, splits, dst_ref, src_ref, values_ref, operator_ref, total):
@@ -408,7 +346,7 @@
 
 
 def routed_sum(
-    grid_inputs, grid_count, embed_in, embed_out, grid_gain, g2m_values, g2m_src, g2m_dst, mesh_place, partitions
+    grid_inputs, grid_count, embed_in, embed_out, g2m_values, g2m_src, g2m_dst, mesh_place, partitions
 ):
     slab_rows = grid_inputs.shape[1]
     edge_count, block_rows, _ = g2m_values.shape
@@ -418,7 +356,7 @@
     slot_count = partitions * capacity
     hidden = jax.nn.silu(transposed_matmul(grid_inputs, embed_in)).astype(jnp.bfloat16)
     alive = lax.iota(jnp.int32, slab_rows) < grid_count[0]
-    latent = jnp.where(alive[:, None], normalize(matmul(hidden, embed_out)) * grid_gain, 0.0).astype(jnp.bfloat16)
+    latent = jnp.where(alive[:, None], normalize(matmul(hidden, embed_out)), 0.0).astype(jnp.bfloat16)
     positions = lookup(mesh_place, g2m_dst)
     targets = positions // held
     ranking = jnp.sum(jnp.tril(targets[:, None] == targets[None, :], -1), axis=1)
@@ -461,7 +399,7 @@
     reads = recv_blocks.shape[1] // 2
     mates = [(i, i ^ 1) for i in range(partitions)]
     others = [(i, (i + 1 if i % 2 else i - 1) % partitions) for i in range(partitions)]
-    grid_args = (grid_inputs, grid_count, embed_in, embed_out, grid_gain, g2m_values, g2m_src, g2m_dst, mesh_place)
+    grid_args = (grid_inputs, grid_count, embed_in, embed_out, g2m_values, g2m_src, g2m_dst, mesh_place)
     lists = (lax.ppermute(recv_blocks, "space", mates), lax.ppermute(recv_blocks, "space", others))
     splits = [(0, rows)]
     halos = []
@@ -474,7 +412,7 @@
             first = sum(cuts[:EARLY])
             splits = [(0, first), (first, rows)]
             to_mate, to_other, ahead = encode(
-                arrived[:EARLY] + kept[:EARLY], [], node_in, node_out, node_gain, lists, held, 1
+                arrived[:EARLY] + kept[:EARLY], [], grid_gain, node_in, node_out, node_gain, lists, held, 1
             )
             halos = [lax.ppermute(to_mate, "space", mates), lax.ppermute(to_other, "space", others)]
             arrived[-1], ahead, halos = lax.optimization_barrier((arrived[-1], ahead, halos))
@@ -483,7 +421,9 @@
     else:
         summands = [routed_sum(*grid_args, partitions)]
     operator = mesh_operator(mesh_values, mesh_dst, mesh_src, held, reads, splits)
-    to_mate, to_other, encoded, own = encode(summands, earlier, node_in, node_out, node_gain, lists, held, 2)
+    to_mate, to_other, encoded, own = encode(
+        summands, earlier, grid_gain, node_in, node_out, node_gain, lists, held, 2
+    )
     halos += [lax.ppermute(to_mate, "space", mates), lax.ppermute(to_other, "space", others)]
     processed = process(operator, own, halos, proc_in, proc_out, proc_gain)
     return (encoded, processed)

time: 86.7 us -> 86.6 us (level)
  Pallas kernels: 17.6 us -> 14.3 us
  local copies, waits for them, and re-layouts: 0.76 us -> 3.23 us
  starting transfers between devices: 23.8 us -> 25.9 us
    pallas_call x1, Pallas kernels: 10.8 us -> 7.46 us  [slab_sums(): pl.pallas_call(functools.partial(grid_kernel, held, capacity, orders, cut...]
    unnamed x26 -> x28, local copies, waits for them, and re-layouts: 0.76 us -> 3.23 us
    ppermute x16, starting transfers between devices: 10.4 us -> 12.8 us  [exchange(): lax.ppermute(cells, 'space', [(i, i ^ 1 << bit) for i in range(count)])]
    convert_element_type x11, other arithmetic: 3.14 us -> 1.94 us  [reduce_chunks(): kept[chunk] = add(received[:half], kept[chunk][:half]).astype(jnp.bfloat16)]
  transfers between devices with their start and end apart: 22 -> 22, of which waited for: 11 -> 11; matrix products, arithmetic and copies ran while one was open for 4% -> 2% of each run, Pallas kernels for 3% -> 3%
where the time goes in v5:
time: 86.6 us; the launch traced here: 87 us
  waiting for transfers between devices  39.1 us (45%)
  starting transfers between devices  25.9 us (30%)
  Pallas kernels  14.3 us (17%)
  local copies, waits for them, and re-layouts  3.23 us (4%)
  other arithmetic  2.85 us (3%)
  between operations  1.54 us (2%)
    ppermute x16, waiting for transfers between devices, exchange(): lax.ppermute(cells, 'space', [(i, i ^ 1 << bit) for i in range(count)])  34.7 us
    ppermute x16, starting transfers between devices, exchange(): lax.ppermute(cells, 'space', [(i, i ^ 1 << bit) for i in range(count)])  12.8 us
    pallas_call x1, Pallas kernels, slab_sums(): pl.pallas_call(functools.partial(grid_kernel, held, capacity, orders, cut...  7.46 us
    ppermute x1, starting transfers between devices, shards(): lax.ppermute(recv_blocks, 'space', others)  6.67 us
    ppermute x2, starting transfers between devices, shards(): lax.ppermute(to_other, 'space', others)  5.97 us
    ppermute x2, waiting for transfers between devices, shards(): lax.ppermute(to_other, 'space', others)  4.36 us
    pallas_call x2, Pallas kernels, encode(): pl.pallas_call(functools.partial(node_kernel, held, len(summands), len(ea...  3.39 us
    unnamed x28, local copies, waits for them, and re-layouts  3.23 us
  transfers between devices with their start and end apart: 22, of which 11 were waited for; matrix products, arithmetic and copies ran while one was open for 2% of the time, Pallas kernels for 3%

profile of v5, /device:TPU:0, one launch (start us, length us, event | category | flops | bytes accessed | tf_op | source)
XLA Modules:
  0.0 87.0 jit_solution(15865755260590820328)
XLA Ops:
  1.3 0.8 pad_add_fusion.table_ref
  2.1 1.2 %copy-done.2 = bf16[227,2048]{1,0:T(8,128)(2,1)S(1)} copy-done((bf16[227,2048]{1,0:T(8,128)(2,1)S(1)}, bf16[227,2048]{1,0:T(8,128)(2,1)}, u32[]{:S(2)}) %copy-start.2) | copy-done | bytes 929816
  3.3 1.0 %copy-done.5 = bf16[512,512]{1,0:T(8,128)(2,1)S(1)} copy-done((bf16[512,512]{1,0:T(8,128)(2,1)S(1)}, bf16[512,512]{1,0:T(8,128)(2,1)}, u32[]{:S(2)}) %copy-start.5) | copy-done | bytes 524312
  4.3 0.9 %copy-done.7 = bf16[227,512]{1,0:T(8,128)(2,1)S(1)} copy-done((bf16[227,512]{1,0:T(8,128)(2,1)S(1)}, bf16[227,512]{1,0:T(8,128)(2,1)}, u32[]{:S(2)}) %copy-start.7) | copy-done | bytes 232472
  5.2 7.5 %grid_to_mesh.1 = (bf16[1024,512]{1,0:T(8,128)(2,1)S(1)}, bf16[1024,512]{1,0:T(8,128)(2,1)S(1)}, bf16[1024,512]{1,0:T(8,128)(2,1)S(1)}, bf16[1024,512]{1,0:T(8,1...) custom-call(s32[193]{0:T(256)S(1)} %pad_add_fusion.table_ref, ...), custom_call_target="tpu_custom_call" | custom-call | tf_op jit(solution)/shard_map/grid_to_mesh/pallas_call | solution.py:193
  12.7 0.5 collective-permute-start.1
  13.2 0.1 collective-permute-start
  13.3 0.4 collective-permute-start.4
  13.7 0.1 collective-permute-start.3
  13.8 0.4 collective-permute-start.5
  14.2 1.3 %collective-permute-done.1 = bf16[1024,512]{1,0:T(8,128)(2,1)S(1)} collective-permute-done((bf16[1024,512]{1,0:T(8,128)(2,1)S(1)}, bf16[1024,512]{1,0:T(8,128)(2,1)S(1)}, u32[]{:S(2)}, u32[]{:S(2)}) %collective-permute-start.1) | collective-permute-done | bytes 1048608 | tf_op jit(solution)/shard_map/ppermute | solution.py:214
  15.5 6.7 %collective-permute-start.6 = (s32[1,4]{1,0:T(1,128)S(1)}, s32[1,4]{1,0:T(1,128)S(1)}, u32[]{:S(2)}, u32[]{:S(2)}) collective-permute-start(s32[1,4]{1,0:T(1,128)S(1)} %copy-done.13), channel_id=1, source_target_pairs={{0,15},{1,2},{2,1},{3,4},{4,3},{5,6},{6,5},{7,8},{8,7},{9,10},{10,... | collective-permute-start | bytes 56 | tf_op jit(solution)/shard_map/ppermute | solution.py:403
  22.2 0.3 add_convert_fusion.1
  22.5 0.1 collective-permute-start.11
  22.6 0.3 add_convert_fusion.3
  22.9 0.0 collective-permute-done.4
  22.9 0.7 collective-permute-start.2
  23.7 0.3 add_convert_fusion.2
  24.0 1.6 %collective-permute-start.7 = (bf16[512,512]{1,0:T(8,128)(2,1)S(1)}, bf16[512,512]{1,0:T(8,128)(2,1)S(1)}, u32[]{:S(2)}, u32[]{:S(2)}) collective-permute-start(bf16[512,512]{1,0:T(8,128)(2,1)S(1)} %get-tuple-element.73), channel_id=1, source_target_pairs={{0,4},{1,5},{2,6},{3,7},{4,0},{5,1},{6,2},{7,3},{8,12},{9,13},{10,... | collective-permute-start | bytes 1572872 | tf_op jit(solution)/shard_map/ppermute | solution.py:214
  25.6 0.3 add_convert_fusion
  25.9 0.0 collective-permute-done.5.mate_list_ref
  26.0 0.6 collective-permute-start.10
  26.6 0.0 collective-permute-done.6.other_list_ref
  26.6 11.3 %collective-permute-done.2 = bf16[512,512]{1,0:T(8,128)(2,1)S(1)} collective-permute-done((bf16[512,512]{1,0:T(8,128)(2,1)S(1)}, bf16[512,512]{1,0:T(8,128)(2,1)S(1)}, u32[]{:S(2)}, u32[]{:S(2)}) %collective-permute-start.2) | collective-permute-done | bytes 524320 | tf_op jit(solution)/shard_map/ppermute | solution.py:214
  37.8 0.1 add_convert_fusion.11
  38.0 0.8 collective-permute-start.9
  38.7 10.3 %collective-permute-done.7 = bf16[512,512]{1,0:T(8,128)(2,1)S(1)} collective-permute-done((bf16[512,512]{1,0:T(8,128)(2,1)S(1)}, bf16[512,512]{1,0:T(8,128)(2,1)S(1)}, u32[]{:S(2)}, u32[]{:S(2)}) %collective-permute-start.7) | collective-permute-done | bytes 524320 | tf_op jit(solution)/shard_map/ppermute | solution.py:214
  49.0 0.1 add_convert_fusion.14
  49.2 1.1 %collective-permute-start.8 = (bf16[256,512]{1,0:T(8,128)(2,1)S(1)}, bf16[256,512]{1,0:T(8,128)(2,1)S(1)}, u32[]{:S(2)}, u32[]{:S(2)}) collective-permute-start(bf16[256,512]{1,0:T(8,128)(2,1)S(1)} %get-tuple-element.80), channel_id=1, source_target_pairs={{0,2},{1,3},{2,0},{3,1},{4,6},{5,7},{6,4},{7,5},{8,10},{9,11},{10,... | collective-permute-start | bytes 786440 | tf_op jit(solution)/shard_map/ppermute | solution.py:214
  50.3 0.1 add_convert_fusion.9
  50.4 1.0 %collective-permute-start.13 = (bf16[256,512]{1,0:T(8,128)(2,1)S(1)}, bf16[256,512]{1,0:T(8,128)(2,1)S(1)}, u32[]{:S(2)}, u32[]{:S(2)}) collective-permute-start(bf16[256,512]{1,0:T(8,128)(2,1)S(1)} %get-tuple-element.77), channel_id=1, source_target_pairs={{0,2},{1,3},{2,0},{3,1},{4,6},{5,7},{6,4},{7,5},{8,10},{9,11},{10,... | collective-permute-start | bytes 786440 | tf_op jit(solution)/shard_map/ppermute | solution.py:214
  51.5 0.0 copy-start.9
  51.5 0.1 add_convert_fusion.8
  51.6 0.1 collective-permute-start.15
  51.7 2.9 %collective-permute-done.9 = bf16[256,512]{1,0:T(8,128)(2,1)S(1)} collective-permute-done((bf16[256,512]{1,0:T(8,128)(2,1)S(1)}, bf16[256,512]{1,0:T(8,128)(2,1)S(1)}, u32[]{:S(2)}, u32[]{:S(2)}) %collective-permute-start.9) | collective-permute-done | bytes 262176 | tf_op jit(solution)/shard_map/ppermute | solution.py:214
  54.6 0.1 add_convert_fusion.19
  54.7 1.2 %collective-permute-start.17 = (bf16[128,512]{1,0:T(8,128)(2,1)S(1)}, bf16[128,512]{1,0:T(8,128)(2,1)S(1)}, u32[]{:S(2)}, u32[]{:S(2)}) collective-permute-start(bf16[128,512]{1,0:T(8,128)(2,1)S(1)} %get-tuple-element.89), channel_id=1, source_target_pairs={{0,8},{1,9},{2,10},{3,11},{4,12},{5,13},{6,14},{7,15},{8,0},{9,1},... | collective-permute-start | bytes 393224 | tf_op jit(solution)/shard_map/ppermute | solution.py:214
  55.9 1.7 %collective-permute-done.8 = bf16[256,512]{1,0:T(8,128)(2,1)S(1)} collective-permute-done((bf16[256,512]{1,0:T(8,128)(2,1)S(1)}, bf16[256,512]{1,0:T(8,128)(2,1)S(1)}, u32[]{:S(2)}, u32[]{:S(2)}) %collective-permute-start.8) | collective-permute-done | bytes 262176 | tf_op jit(solution)/shard_map/ppermute | solution.py:214
  57.6 0.1 add_convert_fusion.18
  57.7 2.7 %collective-permute-done.13 = bf16[256,512]{1,0:T(8,128)(2,1)S(1)} collective-permute-done((bf16[256,512]{1,0:T(8,128)(2,1)S(1)}, bf16[256,512]{1,0:T(8,128)(2,1)S(1)}, u32[]{:S(2)}, u32[]{:S(2)}) %collective-permute-start.13) | collective-permute-done | bytes 262176 | tf_op jit(solution)/shard_map/ppermute | solution.py:214
  60.4 0.1 add_convert_fusion.17
  60.5 0.0 copy-start.6
  60.5 0.0 copy-start.11
  60.5 0.0 copy-start.12
  60.5 0.9 collective-permute-done.15
  61.4 0.1 add_convert_fusion.16
  61.5 1.9 %collective-permute-start.16 = (bf16[128,512]{1,0:T(8,128)(2,1)S(1)}, bf16[128,512]{1,0:T(8,128)(2,1)S(1)}, u32[]{:S(2)}, u32[]{:S(2)}) collective-permute-start(bf16[128,512]{1,0:T(8,128)(2,1)S(1)} %get-tuple-element.83), channel_id=1, source_target_pairs={{0,8},{1,9},{2,10},{3,11},{4,12},{5,13},{6,14},{7,15},{8,0},{9,1},... | collective-permute-start | bytes 393224 | tf_op jit(solution)/shard_map/ppermute | solution.py:214
  63.4 2.4 %collective-permute-start.14 = (bf16[128,512]{1,0:T(8,128)(2,1)S(1)}, bf16[128,512]{1,0:T(8,128)(2,1)S(1)}, u32[]{:S(2)}, u32[]{:S(2)}) collective-permute-start(bf16[128,512]{1,0:T(8,128)(2,1)S(1)} %get-tuple-element.85), channel_id=1, source_target_pairs={{0,4},{1,5},{2,6},{3,7},{4,0},{5,1},{6,2},{7,3},{8,12},{9,13},{10,... | collective-permute-start | bytes 393224 | tf_op jit(solution)/shard_map/ppermute | solution.py:214
  65.8 0.1 collective-permute-start.12
  65.9 0.0 collective-permute-done.17.refs_0_
  65.9 0.0 copy-start.3
  66.0 0.0 copy-start.4
  66.0 0.0 copy-start.10
  66.0 1.2 %node_update.2 = (bf16[64,512]{1,0:T(8,128)(2,1)S(1)}, bf16[64,512]{1,0:T(8,128)(2,1)S(1)}, bf16[128,512]{1,0:T(8,128)(2,1)S(1)}) custom-call(s32[1,4]{1,0:T(1,128)S(1)} %collective-permute-done.5.mate_list_ref, s32[1,4]{1,0:T(1,128)S(1)} %collective-permute-done.6.other_list_ref, bf16[128,512]{1,0:T(8,128)(2,1)S(1)} %collective-permute-done.17.refs_0_, ...), custom_call_target="tpu_custom_call" | custom-call | tf_op jit(solution)/shard_map/node_update/pallas_call | solution.py:281
  67.2 0.1 collective-permute-start.18
  67.2 2.8 %collective-permute-start.19 = (bf16[64,512]{1,0:T(8,128)(2,1)S(1)}, bf16[64,512]{1,0:T(8,128)(2,1)S(1)}, u32[]{:S(2)}, u32[]{:S(2)}) collective-permute-start(bf16[64,512]{1,0:T(8,128)(2,1)S(1)} %get-tuple-element.57), channel_id=1, source_target_pairs={{0,15},{1,2},{2,1},{3,4},{4,3},{5,6},{6,5},{7,8},{8,7},{9,10},{10,... | collective-permute-start | bytes 196616 | tf_op jit(solution)/shard_map/ppermute | solution.py:417
  70.1 3.0 %collective-permute-done.16.refs_2_ = bf16[128,512]{1,0:T(8,128)(2,1)S(1)} collective-permute-done((bf16[128,512]{1,0:T(8,128)(2,1)S(1)}, bf16[128,512]{1,0:T(8,128)(2,1)S(1)}, u32[]{:S(2)}, u32[]{:S(2)}) %collective-permute-start.16) | collective-permute-done | bytes 131104 | tf_op jit(solution)/shard_map/ppermute | solution.py:214
  73.0 0.7 collective-permute-done.19.refs_1_
  73.8 0.7 collective-permute-done.12.refs_0_
  74.4 2.2 %node_update.3 = (bf16[192,512]{1,0:T(8,128)(2,1)S(1)}, bf16[192,512]{1,0:T(8,128)(2,1)S(1)}, bf16[512,512]{1,0:T(8,128)(2,1)}, bf16[512,512]{1,0:T(8,128)(2,1)S(1)}) custom-call(s32[1,4]{1,0:T(1,128)S(1)} %collective-permute-done.5.mate_list_ref, s32[1,4]{1,0:T(1,128)S(1)} %collective-permute-done.6.other_list_ref, ...), custom_call_target="tpu_custom_call" | custom-call | tf_op jit(solution)/shard_map/node_update/pallas_call | solution.py:281
  76.7 3.1 %collective-permute-start.21 = (bf16[192,512]{1,0:T(8,128)(2,1)S(1)}, bf16[192,512]{1,0:T(8,128)(2,1)S(1)}, u32[]{:S(2)}, u32[]{:S(2)}) collective-permute-start(bf16[192,512]{1,0:T(8,128)(2,1)S(1)} %get-tuple-element.65), channel_id=1, source_target_pairs={{0,15},{1,2},{2,1},{3,4},{4,3},{5,6},{6,5},{7,8},{8,7},{9,10},{10,... | collective-permute-start | bytes 589832 | tf_op jit(solution)/shard_map/ppermute | solution.py:427
  79.8 1.1 %mesh_operator.1.operator_ref = bf16[512,1024]{1,0:T(8,128)(2,1)S(1)} custom-call(s32[12]{0:T(128)S(1)} %copy-done.11, s32[12]{0:T(128)S(1)} %copy-done.12, bf16[12,128,128]{2,1,0:T(8,128)(2,1)S(1)} %copy-done.6), custom_call_target="tpu_custom_call" | custom-call | tf_op jit(solution)/shard_map/mesh_operator/pallas_call | solution.py:312
  80.9 3.6 %collective-permute-done.21.refs_3_ = bf16[192,512]{1,0:T(8,128)(2,1)S(1)} collective-permute-done((bf16[192,512]{1,0:T(8,128)(2,1)S(1)}, bf16[192,512]{1,0:T(8,128)(2,1)S(1)}, u32[]{:S(2)}, u32[]{:S(2)}) %collective-permute-start.21) | collective-permute-done | bytes 196640 | tf_op jit(solution)/shard_map/ppermute | solution.py:427
  84.6 2.4 %process.1 = bf16[512,512]{1,0:T(8,128)(2,1)} custom-call(bf16[512,1024]{1,0:T(8,128)(2,1)S(1)} %mesh_operator.1.operator_ref, bf16[512,512]{1,0:T(8,128)(2,1)S(1)} %get-tuple-element.61.own_ref, bf16[64,512]{1,0:T(8,128)(2,1)S(1)} %collective-permute-done.18.refs_0_, bf16[64,512]{1,0:T(8,128)(2,1)S(1)} %collective-permute-done.19.refs_1_, ...), custom_call_target="tpu_custom_call" | custom-call | tf_op jit(solution)/shard_map/process/pallas_call | solution.py:333
  (26 shorter events, 0.1 us)
Async XLA Ops:
  0.6 13.2 %copy-start.13 = (s32[1,4]{1,0:T(1,128)S(1)}, s32[1,4]{1,0:T(1,128)}, u32[]{:S(2)}) copy-start(s32[1,4]{1,0:T(1,128)} %param.31) | copy-start | bytes 52
  2.1 1.2 %copy-start.2 = (bf16[227,2048]{1,0:T(8,128)(2,1)S(1)}, bf16[227,2048]{1,0:T(8,128)(2,1)}, u32[]{:S(2)}) copy-start(bf16[227,2048]{1,0:T(8,128)(2,1)} %inputs_ref.1) | copy-start | bytes 2789380
  3.3 1.0 %copy-start.5 = (bf16[512,512]{1,0:T(8,128)(2,1)S(1)}, bf16[512,512]{1,0:T(8,128)(2,1)}, u32[]{:S(2)}) copy-start(bf16[512,512]{1,0:T(8,128)(2,1)} %embed_out_ref.1) | copy-start | bytes 1572868
  4.3 0.9 %copy-start.7 = (bf16[227,512]{1,0:T(8,128)(2,1)S(1)}, bf16[227,512]{1,0:T(8,128)(2,1)}, u32[]{:S(2)}) copy-start(bf16[227,512]{1,0:T(8,128)(2,1)} %embed_in_ref.1) | copy-start | bytes 697348
  12.7 2.8 %collective-permute-start.1 = (bf16[1024,512]{1,0:T(8,128)(2,1)S(1)}, bf16[1024,512]{1,0:T(8,128)(2,1)S(1)}, u32[]{:S(2)}, u32[]{:S(2)}) collective-permute-start(bf16[1024,512]{1,0:T(8,128)(2,1)S(1)} %get-tuple-element.35), channel_id=1, source_target_pairs={{0,1},{1,0},{2,3},{3,2},{4,5},{5,4},{6,7},{7,6},{8,9},{9,8},{10,11... | collective-permute-start | bytes 3145736 | tf_op jit(solution)/shard_map/ppermute | solution.py:214
  13.2 9.3 %collective-permute-start = (bf16[1024,512]{1,0:T(8,128)(2,1)S(1)}, bf16[1024,512]{1,0:T(8,128)(2,1)S(1)}, u32[]{:S(2)}, u32[]{:S(2)}) collective-permute-start(bf16[1024,512]{1,0:T(8,128)(2,1)S(1)} %get-tuple-element.34), channel_id=1, source_target_pairs={{0,1},{1,0},{2,3},{3,2},{4,5},{5,4},{6,7},{7,6},{8,9},{9,8},{10,11... | collective-permute-start | bytes 3145736 | tf_op jit(solution)/shard_map/ppermute | solution.py:214
  13.3 9.6 %collective-permute-start.4 = (bf16[1024,512]{1,0:T(8,128)(2,1)S(1)}, bf16[1024,512]{1,0:T(8,128)(2,1)S(1)}, u32[]{:S(2)}, u32[]{:S(2)}) collective-permute-start(bf16[1024,512]{1,0:T(8,128)(2,1)S(1)} %get-tuple-element.40), channel_id=1, source_target_pairs={{0,1},{1,0},{2,3},{3,2},{4,5},{5,4},{6,7},{7,6},{8,9},{9,8},{10,11... | collective-permute-start | bytes 3145736 | tf_op jit(solution)/shard_map/ppermute | solution.py:214
  13.7 10.3 %collective-permute-start.3 = (bf16[1024,512]{1,0:T(8,128)(2,1)S(1)}, bf16[1024,512]{1,0:T(8,128)(2,1)S(1)}, u32[]{:S(2)}, u32[]{:S(2)}) collective-permute-start(bf16[1024,512]{1,0:T(8,128)(2,1)S(1)} %get-tuple-element.39), channel_id=1, source_target_pairs={{0,1},{1,0},{2,3},{3,2},{4,5},{5,4},{6,7},{7,6},{8,9},{9,8},{10,11... | collective-permute-start | bytes 3145736 | tf_op jit(solution)/shard_map/ppermute | solution.py:214
  13.8 12.1 %collective-permute-start.5 = (s32[1,4]{1,0:T(1,128)S(1)}, s32[1,4]{1,0:T(1,128)S(1)}, u32[]{:S(2)}, u32[]{:S(2)}) collective-permute-start(s32[1,4]{1,0:T(1,128)S(1)} %copy-done.13), channel_id=1, source_target_pairs={{0,1},{1,0},{2,3},{3,2},{4,5},{5,4},{6,7},{7,6},{8,9},{9,8},{10,11... | collective-permute-start | bytes 56 | tf_op jit(solution)/shard_map/ppermute | solution.py:403
  15.5 11.1 %collective-permute-start.6 = (s32[1,4]{1,0:T(1,128)S(1)}, s32[1,4]{1,0:T(1,128)S(1)}, u32[]{:S(2)}, u32[]{:S(2)}) collective-permute-start(s32[1,4]{1,0:T(1,128)S(1)} %copy-done.13), channel_id=1, source_target_pairs={{0,15},{1,2},{2,1},{3,4},{4,3},{5,6},{6,5},{7,8},{8,7},{9,10},{10,... | collective-permute-start | bytes 56 | tf_op jit(solution)/shard_map/ppermute | solution.py:403
  22.5 27.8 %collective-permute-start.11 = (bf16[512,512]{1,0:T(8,128)(2,1)S(1)}, bf16[512,512]{1,0:T(8,128)(2,1)S(1)}, u32[]{:S(2)}, u32[]{:S(2)}) collective-permute-start(bf16[512,512]{1,0:T(8,128)(2,1)S(1)} %get-tuple-element.67), channel_id=1, source_target_pairs={{0,8},{1,9},{2,10},{3,11},{4,12},{5,13},{6,14},{7,15},{8,0},{9,1},... | collective-permute-start | bytes 1572872 | tf_op jit(solution)/shard_map/ppermute | solution.py:214
  22.9 14.9 %collective-permute-start.2 = (bf16[512,512]{1,0:T(8,128)(2,1)S(1)}, bf16[512,512]{1,0:T(8,128)(2,1)S(1)}, u32[]{:S(2)}, u32[]{:S(2)}) collective-permute-start(bf16[512,512]{1,0:T(8,128)(2,1)S(1)} %get-tuple-element.71), channel_id=1, source_target_pairs={{0,2},{1,3},{2,0},{3,1},{4,6},{5,7},{6,4},{7,5},{8,10},{9,11},{10,... | collective-permute-start | bytes 1572872 | tf_op jit(solution)/shard_map/ppermute | solution.py:214
  24.0 25.0 %collective-permute-start.7 = (bf16[512,512]{1,0:T(8,128)(2,1)S(1)}, bf16[512,512]{1,0:T(8,128)(2,1)S(1)}, u32[]{:S(2)}, u32[]{:S(2)}) collective-permute-start(bf16[512,512]{1,0:T(8,128)(2,1)S(1)} %get-tuple-element.73), channel_id=1, source_target_pairs={{0,4},{1,5},{2,6},{3,7},{4,0},{5,1},{6,2},{7,3},{8,12},{9,13},{10,... | collective-permute-start | bytes 1572872 | tf_op jit(solution)/shard_map/ppermute | solution.py:214
  26.0 25.5 %collective-permute-start.10 = (bf16[512,512]{1,0:T(8,128)(2,1)S(1)}, bf16[512,512]{1,0:T(8,128)(2,1)S(1)}, u32[]{:S(2)}, u32[]{:S(2)}) collective-permute-start(bf16[512,512]{1,0:T(8,128)(2,1)S(1)} %get-tuple-element.69), channel_id=1, source_target_pairs={{0,2},{1,3},{2,0},{3,1},{4,6},{5,7},{6,4},{7,5},{8,10},{9,11},{10,... | collective-permute-start | bytes 1572872 | tf_op jit(solution)/shard_map/ppermute | solution.py:214
  38.0 16.7 %collective-permute-start.9 = (bf16[256,512]{1,0:T(8,128)(2,1)S(1)}, bf16[256,512]{1,0:T(8,128)(2,1)S(1)}, u32[]{:S(2)}, u32[]{:S(2)}) collective-permute-start(bf16[256,512]{1,0:T(8,128)(2,1)S(1)} %get-tuple-element.79), channel_id=1, source_target_pairs={{0,4},{1,5},{2,6},{3,7},{4,0},{5,1},{6,2},{7,3},{8,12},{9,13},{10,... | collective-permute-start | bytes 786440 | tf_op jit(solution)/shard_map/ppermute | solution.py:214
  49.2 8.4 %collective-permute-start.8 = (bf16[256,512]{1,0:T(8,128)(2,1)S(1)}, bf16[256,512]{1,0:T(8,128)(2,1)S(1)}, u32[]{:S(2)}, u32[]{:S(2)}) collective-permute-start(bf16[256,512]{1,0:T(8,128)(2,1)S(1)} %get-tuple-element.80), channel_id=1, source_target_pairs={{0,2},{1,3},{2,0},{3,1},{4,6},{5,7},{6,4},{7,5},{8,10},{9,11},{10,... | collective-permute-start | bytes 786440 | tf_op jit(solution)/shard_map/ppermute | solution.py:214
  50.4 10.0 %collective-permute-start.13 = (bf16[256,512]{1,0:T(8,128)(2,1)S(1)}, bf16[256,512]{1,0:T(8,128)(2,1)S(1)}, u32[]{:S(2)}, u32[]{:S(2)}) collective-permute-start(bf16[256,512]{1,0:T(8,128)(2,1)S(1)} %get-tuple-element.77), channel_id=1, source_target_pairs={{0,2},{1,3},{2,0},{3,1},{4,6},{5,7},{6,4},{7,5},{8,10},{9,11},{10,... | collective-permute-start | bytes 786440 | tf_op jit(solution)/shard_map/ppermute | solution.py:214
  51.5 14.4 %copy-start = (bf16[512,512]{1,0:T(8,128)(2,1)S(1)}, bf16[512,512]{1,0:T(8,128)(2,1)}, u32[]{:S(2)}) copy-start(bf16[512,512]{1,0:T(8,128)(2,1)} %refs_7_.1) | copy-start | bytes 1572868
  51.5 14.4 %copy-start.1 = (bf16[512,512]{1,0:T(8,128)(2,1)S(1)}, bf16[512,512]{1,0:T(8,128)(2,1)}, u32[]{:S(2)}) copy-start(bf16[512,512]{1,0:T(8,128)(2,1)} %refs_8_.1) | copy-start | bytes 1572868
  51.5 14.4 %copy-start.8 = (f32[512]{0:T(512)S(1)}, f32[512]{0:T(512)}, u32[]{:S(2)}) copy-start(f32[512]{0:T(512)} %param.30) | copy-start | bytes 6148
  51.5 14.4 %copy-start.9 = (f32[512]{0:T(512)S(1)}, f32[512]{0:T(512)}, u32[]{:S(2)}) copy-start(f32[512]{0:T(512)} %param.23) | copy-start | bytes 6148
  51.6 9.7 %collective-permute-start.15 = (bf16[256,512]{1,0:T(8,128)(2,1)S(1)}, bf16[256,512]{1,0:T(8,128)(2,1)S(1)}, u32[]{:S(2)}, u32[]{:S(2)}) collective-permute-start(bf16[256,512]{1,0:T(8,128)(2,1)S(1)} %get-tuple-element.75), channel_id=1, source_target_pairs={{0,4},{1,5},{2,6},{3,7},{4,0},{5,1},{6,2},{7,3},{8,12},{9,13},{10,... | collective-permute-start | bytes 786440 | tf_op jit(solution)/shard_map/ppermute | solution.py:214
  54.7 11.2 %collective-permute-start.17 = (bf16[128,512]{1,0:T(8,128)(2,1)S(1)}, bf16[128,512]{1,0:T(8,128)(2,1)S(1)}, u32[]{:S(2)}, u32[]{:S(2)}) collective-permute-start(bf16[128,512]{1,0:T(8,128)(2,1)S(1)} %get-tuple-element.89), channel_id=1, source_target_pairs={{0,8},{1,9},{2,10},{3,11},{4,12},{5,13},{6,14},{7,15},{8,0},{9,1},... | collective-permute-start | bytes 393224 | tf_op jit(solution)/shard_map/ppermute | solution.py:214
  60.5 19.3 %copy-start.6 = (bf16[12,128,128]{2,1,0:T(8,128)(2,1)S(1)}, bf16[12,128,128]{2,1,0:T(8,128)(2,1)}, u32[]{:S(2)}) copy-start(bf16[12,128,128]{2,1,0:T(8,128)(2,1)} %values_ref.1) | copy-start | bytes 1179652
  60.5 19.3 %copy-start.11 = (s32[12]{0:T(128)S(1)}, s32[12]{0:T(128)}, u32[]{:S(2)}) copy-start(s32[12]{0:T(128)} %dst_ref.1) | copy-start | bytes 148
  60.5 19.3 %copy-start.12 = (s32[12]{0:T(128)S(1)}, s32[12]{0:T(128)}, u32[]{:S(2)}) copy-start(s32[12]{0:T(128)} %src_ref.1) | copy-start | bytes 148
  61.5 11.6 %collective-permute-start.16 = (bf16[128,512]{1,0:T(8,128)(2,1)S(1)}, bf16[128,512]{1,0:T(8,128)(2,1)S(1)}, u32[]{:S(2)}, u32[]{:S(2)}) collective-permute-start(bf16[128,512]{1,0:T(8,128)(2,1)S(1)} %get-tuple-element.83), channel_id=1, source_target_pairs={{0,8},{1,9},{2,10},{3,11},{4,12},{5,13},{6,14},{7,15},{8,0},{9,1},... | collective-permute-start | bytes 393224 | tf_op jit(solution)/shard_map/ppermute | solution.py:214
  63.4 10.4 %collective-permute-start.14 = (bf16[128,512]{1,0:T(8,128)(2,1)S(1)}, bf16[128,512]{1,0:T(8,128)(2,1)S(1)}, u32[]{:S(2)}, u32[]{:S(2)}) collective-permute-start(bf16[128,512]{1,0:T(8,128)(2,1)S(1)} %get-tuple-element.85), channel_id=1, source_target_pairs={{0,4},{1,5},{2,6},{3,7},{4,0},{5,1},{6,2},{7,3},{8,12},{9,13},{10,... | collective-permute-start | bytes 393224 | tf_op jit(solution)/shard_map/ppermute | solution.py:214
  65.8 8.6 %collective-permute-start.12 = (bf16[128,512]{1,0:T(8,128)(2,1)S(1)}, bf16[128,512]{1,0:T(8,128)(2,1)S(1)}, u32[]{:S(2)}, u32[]{:S(2)}) collective-permute-start(bf16[128,512]{1,0:T(8,128)(2,1)S(1)} %get-tuple-element.87), channel_id=1, source_target_pairs={{0,8},{1,9},{2,10},{3,11},{4,12},{5,13},{6,14},{7,15},{8,0},{9,1},... | collective-permute-start | bytes 393224 | tf_op jit(solution)/shard_map/ppermute | solution.py:214
  65.9 18.6 %copy-start.3 = (bf16[512,512]{1,0:T(8,128)(2,1)S(1)}, bf16[512,512]{1,0:T(8,128)(2,1)}, u32[]{:S(2)}) copy-start(bf16[512,512]{1,0:T(8,128)(2,1)} %refs_4_.1) | copy-start | bytes 1572868
  66.0 18.6 %copy-start.4 = (bf16[512,512]{1,0:T(8,128)(2,1)S(1)}, bf16[512,512]{1,0:T(8,128)(2,1)}, u32[]{:S(2)}) copy-start(bf16[512,512]{1,0:T(8,128)(2,1)} %refs_5_.1) | copy-start | bytes 1572868
  66.0 18.6 %copy-start.10 = (f32[512]{0:T(512)S(1)}, f32[512]{0:T(512)}, u32[]{:S(2)}) copy-start(f32[512]{0:T(512)} %param.37) | copy-start | bytes 6148
  67.2 5.9 %collective-permute-start.18 = (bf16[64,512]{1,0:T(8,128)(2,1)S(1)}, bf16[64,512]{1,0:T(8,128)(2,1)S(1)}, u32[]{:S(2)}, u32[]{:S(2)}) collective-permute-start(bf16[64,512]{1,0:T(8,128)(2,1)S(1)} %get-tuple-element.56), channel_id=1, source_target_pairs={{0,1},{1,0},{2,3},{3,2},{4,5},{5,4},{6,7},{7,6},{8,9},{9,8},{10,11... | collective-permute-start | bytes 196616 | tf_op jit(solution)/shard_map/ppermute | solution.py:417
  67.2 6.6 %collective-permute-start.19 = (bf16[64,512]{1,0:T(8,128)(2,1)S(1)}, bf16[64,512]{1,0:T(8,128)(2,1)S(1)}, u32[]{:S(2)}, u32[]{:S(2)}) collective-permute-start(bf16[64,512]{1,0:T(8,128)(2,1)S(1)} %get-tuple-element.57), channel_id=1, source_target_pairs={{0,15},{1,2},{2,1},{3,4},{4,3},{5,6},{6,5},{7,8},{8,7},{9,10},{10,... | collective-permute-start | bytes 196616 | tf_op jit(solution)/shard_map/ppermute | solution.py:417
  76.7 4.3 %collective-permute-start.20 = (bf16[192,512]{1,0:T(8,128)(2,1)S(1)}, bf16[192,512]{1,0:T(8,128)(2,1)S(1)}, u32[]{:S(2)}, u32[]{:S(2)}) collective-permute-start(bf16[192,512]{1,0:T(8,128)(2,1)S(1)} %get-tuple-element.64), channel_id=1, source_target_pairs={{0,1},{1,0},{2,3},{3,2},{4,5},{5,4},{6,7},{7,6},{8,9},{9,8},{10,11... | collective-permute-start | bytes 589832 | tf_op jit(solution)/shard_map/ppermute | solution.py:427
  76.7 7.9 %collective-permute-start.21 = (bf16[192,512]{1,0:T(8,128)(2,1)S(1)}, bf16[192,512]{1,0:T(8,128)(2,1)S(1)}, u32[]{:S(2)}, u32[]{:S(2)}) collective-permute-start(bf16[192,512]{1,0:T(8,128)(2,1)S(1)} %get-tuple-element.65), channel_id=1, source_target_pairs={{0,15},{1,2},{2,1},{3,4},{4,3},{5,6},{6,5},{7,8},{8,7},{9,10},{10,... | collective-permute-start | bytes 589832 | tf_op jit(solution)/shard_map/ppermute | solution.py:427

commit v6 on v5

--- a/solution.py
+++ b/solution.py
@@ -12,6 +12,9 @@
 SHARES = (2, 2, 2, 2)
 TURNS = (2, 0, 1, 3, 0, 1, 2, 3, 0, 1, 2, 3)
 EARLY = 1
+LISTS_BY = 4
+TILE = 1024
+UNROLL = 2
 VMEM_BYTES = 24 * 1024 * 1024
 GRID_VMEM_BYTES = 43 * 1024 * 1024
 VMEM = pl.BlockSpec(memory_space=pltpu.VMEM)
@@ -59,8 +62,7 @@
     edges,
     table_ref,
     inputs_ref,
-    embed_in_ref,
-    embed_out_ref,
+    weights_ref,
     values_hbm,
     *refs,
 ):
@@ -102,6 +104,7 @@
         crowded[0] = seen + (count == 2).astype(jnp.int32)
 
 
+    channels = latent.shape[1]
     alive = table_ref[table_ref.shape[0] - 1]
     tiles = latent.shape[0] // tile_rows
     sorted_each = edges // tiles
@@ -111,8 +114,8 @@
             sort(tile * sorted_each + index)
         first = pl.multiple_of(tile * tile_rows, tile_rows)
         columns = inputs_ref[:, pl.ds(first, tile_rows)]
-        hidden = silu(transposed_matmul(columns, embed_in_ref[...])).astype(jnp.bfloat16)
-        normal = normalize(matmul(hidden, embed_out_ref[...]))
+        hidden = silu(transposed_matmul(columns, weights_ref[channels:, :])).astype(jnp.bfloat16)
+        normal = normalize(matmul(hidden, weights_ref[:channels, :]))
         row = first + lax.broadcasted_iota(jnp.int32, (tile_rows, 1), 0)
         latent[pl.ds(first, tile_rows), :] = jnp.where(row < alive, normal, 0.0).astype(jnp.bfloat16)
         return carry
@@ -149,7 +152,7 @@
 
         return carry
 
-    lax.fori_loop(0, pairs // 2, multiply, 0)
+    lax.fori_loop(0, pairs // 2, multiply, 0, unroll=UNROLL)
 
     def revisit(index, carry):
         bin_ = crowded_of[index]
@@ -191,8 +194,8 @@
     pairs = partitions // 2
     shapes = [jax.ShapeDtypeStruct((pairs * held * cut, channels), jnp.bfloat16) for cut in cuts]
     return pl.pallas_call(
-        functools.partial(grid_kernel, held, capacity, orders, cuts, min(512, slab_rows), edges),
-        in_specs=[SMEM] + [VMEM] * 3 + [HBM],
+        functools.partial(grid_kernel, held, capacity, orders, cuts, min(TILE, slab_rows), edges),
+        in_specs=[SMEM] + [VMEM] * 2 + [HBM],
         out_specs=[VMEM] * (2 * len(cuts)),
         out_shape=shapes * 2,
         scratch_shapes=[
@@ -206,7 +209,12 @@
         ],
         compiler_params=pltpu.CompilerParams(vmem_limit_bytes=GRID_VMEM_BYTES),
         name="grid_to_mesh",
-    )(jnp.concatenate([g2m_src, g2m_dst, mesh_place, grid_count]), grid_inputs, embed_in, embed_out, g2m_values)
+    )(
+        jnp.concatenate([g2m_src, g2m_dst, mesh_place, grid_count]),
+        grid_inputs,
+        jnp.concatenate([embed_out, embed_in]),
+        g2m_values,
+    )
 
 
 def exchange(cells, bit):
@@ -220,7 +228,7 @@
     made = [0] * len(orders)
     for turn, chunk in enumerate(turns):
         received = arrived[chunk]
-        if turn == len(orders):
+        if turn == LISTS_BY:
             received, _, lists = lax.optimization_barrier((received, previous, lists))
         elif turn > 0:
             received, _ = lax.optimization_barrier((received, previous))

time: 86.6 us -> 83.6 us (0.965)
  local copies, waits for them, and re-layouts: 3.23 us -> 0.07 us
  starting transfers between devices: 25.9 us -> 24.6 us
    unnamed x28 -> x30, local copies, waits for them, and re-layouts: 3.23 us -> 0.07 us
    concatenate x0 -> x1, other arithmetic: none -> 1.22 us  [slab_sums(): jnp.concatenate([embed_out, embed_in])]
    ppermute x1, starting transfers between devices: 6.67 us -> 5.75 us  [shards(): lax.ppermute(recv_blocks, 'space', others)]
  transfers between devices with their start and end apart: 22 -> 22, of which waited for: 11 -> 11; matrix products, arithmetic and copies ran while one was open for 2% -> 3% of each run, Pallas kernels for 3% -> 3%
where the time goes in v6:
time: 83.6 us; the launch traced here: 83.2 us
  waiting for transfers between devices  39.4 us (47%)
  starting transfers between devices  24.6 us (29%)
  Pallas kernels  14.1 us (17%)
  other arithmetic  3.39 us (4%)
  between operations  1.63 us (2%)
    ppermute x16, waiting for transfers between devices, exchange(): lax.ppermute(cells, 'space', [(i, i ^ 1 << bit) for i in range(count)])  35.4 us
    ppermute x16, starting transfers between devices, exchange(): lax.ppermute(cells, 'space', [(i, i ^ 1 << bit) for i in range(count)])  12.6 us
    pallas_call x1, Pallas kernels, slab_sums(): pl.pallas_call(functools.partial(grid_kernel, held, capacity, orders, cut...  7.21 us
    ppermute x2, starting transfers between devices, shards(): lax.ppermute(to_other, 'space', others)  5.91 us
    ppermute x1, starting transfers between devices, shards(): lax.ppermute(recv_blocks, 'space', others)  5.75 us
    ppermute x2, waiting for transfers between devices, shards(): lax.ppermute(to_other, 'space', others)  4.01 us
    pallas_call x2, Pallas kernels, encode(): pl.pallas_call(functools.partial(node_kernel, held, len(summands), len(ea...  3.41 us
    pallas_call x1, Pallas kernels, process(): pl.pallas_call(process_kernel, in_specs=[VMEM] * (5 + len(halos)), out_sp...  2.37 us
  transfers between devices with their start and end apart: 22, of which 11 were waited for; matrix products, arithmetic and copies ran while one was open for 3% of the time, Pallas kernels for 3%

profile of v6, /device:TPU:0, one launch (start us, length us, event | category | flops | bytes accessed | tf_op | source)
XLA Modules:
  0.0 83.2 jit_solution(15270356132035410139)
XLA Ops:
  1.4 1.2 %pad_maximum_fusion.weights_ref = bf16[739,512]{1,0:T(8,128)(2,1)S(1)} fusion(bf16[227,512]{1,0:T(8,128)(2,1)} %param.21, bf16[512,512]{1,0:T(8,128)(2,1)} %param.22), kind=kLoop, calls=%fused_computation.8 | loop fusion | flops 1513472 | bytes 1513472 | tf_op jit(solution)/shard_map/concatenate | solution.py:215
  2.7 0.1 pad_add_fusion.table_ref
  2.7 7.2 %grid_to_mesh.1 = (bf16[1024,512]{1,0:T(8,128)(2,1)S(1)}, bf16[1024,512]{1,0:T(8,128)(2,1)S(1)}, bf16[1024,512]{1,0:T(8,128)(2,1)S(1)}, bf16[1024,512]{1,0:T(8,1...) custom-call(s32[193]{0:T(256)S(1)} %pad_add_fusion.table_ref, ...), custom_call_target="tpu_custom_call" | custom-call | tf_op jit(solution)/shard_map/grid_to_mesh/pallas_call | solution.py:196
  10.0 0.3 collective-permute-start.1
  10.3 0.3 collective-permute-start
  10.5 0.2 collective-permute-start.4
  10.8 0.3 collective-permute-start.3
  11.0 0.2 collective-permute-start.5
  11.3 1.4 %collective-permute-done.1 = bf16[1024,512]{1,0:T(8,128)(2,1)S(1)} collective-permute-done((bf16[1024,512]{1,0:T(8,128)(2,1)S(1)}, bf16[1024,512]{1,0:T(8,128)(2,1)S(1)}, u32[]{:S(2)}, u32[]{:S(2)}) %collective-permute-start.1) | collective-permute-done | bytes 1048608 | tf_op jit(solution)/shard_map/ppermute | solution.py:222
  12.7 5.7 %collective-permute-start.6 = (s32[1,4]{1,0:T(1,128)S(1)}, s32[1,4]{1,0:T(1,128)S(1)}, u32[]{:S(2)}, u32[]{:S(2)}) collective-permute-start(s32[1,4]{1,0:T(1,128)S(1)} %copy-done.14), channel_id=1, source_target_pairs={{0,15},{1,2},{2,1},{3,4},{4,3},{5,6},{6,5},{7,8},{8,7},{9,10},{10,... | collective-permute-start | bytes 56 | tf_op jit(solution)/shard_map/ppermute | solution.py:411
  18.4 0.3 add_convert_fusion.1
  18.8 0.0 collective-permute-done
  18.8 0.1 collective-permute-start.11
  18.8 0.3 add_convert_fusion.3
  19.2 0.0 collective-permute-done.4
  19.2 0.7 collective-permute-start.2
  19.9 0.3 add_convert_fusion.2
  20.2 0.0 collective-permute-done.3
  20.2 1.9 %collective-permute-start.7 = (bf16[512,512]{1,0:T(8,128)(2,1)S(1)}, bf16[512,512]{1,0:T(8,128)(2,1)S(1)}, u32[]{:S(2)}, u32[]{:S(2)}) collective-permute-start(bf16[512,512]{1,0:T(8,128)(2,1)S(1)} %get-tuple-element.73), channel_id=1, source_target_pairs={{0,4},{1,5},{2,6},{3,7},{4,0},{5,1},{6,2},{7,3},{8,12},{9,13},{10,... | collective-permute-start | bytes 1572872 | tf_op jit(solution)/shard_map/ppermute | solution.py:222
  22.1 0.3 add_convert_fusion
  22.4 0.6 collective-permute-start.10
  23.0 0.0 collective-permute-done.6.other_list_ref
  23.0 11.1 %collective-permute-done.2 = bf16[512,512]{1,0:T(8,128)(2,1)S(1)} collective-permute-done((bf16[512,512]{1,0:T(8,128)(2,1)S(1)}, bf16[512,512]{1,0:T(8,128)(2,1)S(1)}, u32[]{:S(2)}, u32[]{:S(2)}) %collective-permute-start.2) | collective-permute-done | bytes 524320 | tf_op jit(solution)/shard_map/ppermute | solution.py:222
  34.1 0.1 add_convert_fusion.11
  34.2 0.9 %collective-permute-start.9 = (bf16[256,512]{1,0:T(8,128)(2,1)S(1)}, bf16[256,512]{1,0:T(8,128)(2,1)S(1)}, u32[]{:S(2)}, u32[]{:S(2)}) collective-permute-start(bf16[256,512]{1,0:T(8,128)(2,1)S(1)} %get-tuple-element.79), channel_id=1, source_target_pairs={{0,4},{1,5},{2,6},{3,7},{4,0},{5,1},{6,2},{7,3},{8,12},{9,13},{10,... | collective-permute-start | bytes 786440 | tf_op jit(solution)/shard_map/ppermute | solution.py:222
  35.2 10.0 %collective-permute-done.7 = bf16[512,512]{1,0:T(8,128)(2,1)S(1)} collective-permute-done((bf16[512,512]{1,0:T(8,128)(2,1)S(1)}, bf16[512,512]{1,0:T(8,128)(2,1)S(1)}, u32[]{:S(2)}, u32[]{:S(2)}) %collective-permute-start.7) | collective-permute-done | bytes 524320 | tf_op jit(solution)/shard_map/ppermute | solution.py:222
  45.2 0.1 add_convert_fusion.14
  45.3 0.5 collective-permute-start.8
  45.8 0.0 collective-permute-done.11
  45.8 0.1 add_convert_fusion.9
  45.9 1.7 %collective-permute-start.13 = (bf16[256,512]{1,0:T(8,128)(2,1)S(1)}, bf16[256,512]{1,0:T(8,128)(2,1)S(1)}, u32[]{:S(2)}, u32[]{:S(2)}) collective-permute-start(bf16[256,512]{1,0:T(8,128)(2,1)S(1)} %get-tuple-element.77), channel_id=1, source_target_pairs={{0,2},{1,3},{2,0},{3,1},{4,6},{5,7},{6,4},{7,5},{8,10},{9,11},{10,... | collective-permute-start | bytes 786440 | tf_op jit(solution)/shard_map/ppermute | solution.py:222
  47.6 0.0 collective-permute-done.10
  47.6 0.1 add_convert_fusion.8
  47.8 0.1 collective-permute-start.15
  47.8 2.9 %collective-permute-done.9 = bf16[256,512]{1,0:T(8,128)(2,1)S(1)} collective-permute-done((bf16[256,512]{1,0:T(8,128)(2,1)S(1)}, bf16[256,512]{1,0:T(8,128)(2,1)S(1)}, u32[]{:S(2)}, u32[]{:S(2)}) %collective-permute-start.9) | collective-permute-done | bytes 262176 | tf_op jit(solution)/shard_map/ppermute | solution.py:222
  50.8 0.1 add_convert_fusion.19
  50.9 1.6 %collective-permute-start.17 = (bf16[128,512]{1,0:T(8,128)(2,1)S(1)}, bf16[128,512]{1,0:T(8,128)(2,1)S(1)}, u32[]{:S(2)}, u32[]{:S(2)}) collective-permute-start(bf16[128,512]{1,0:T(8,128)(2,1)S(1)} %get-tuple-element.89), channel_id=1, source_target_pairs={{0,8},{1,9},{2,10},{3,11},{4,12},{5,13},{6,14},{7,15},{8,0},{9,1},... | collective-permute-start | bytes 393224 | tf_op jit(solution)/shard_map/ppermute | solution.py:222
  52.4 2.2 %collective-permute-done.8 = bf16[256,512]{1,0:T(8,128)(2,1)S(1)} collective-permute-done((bf16[256,512]{1,0:T(8,128)(2,1)S(1)}, bf16[256,512]{1,0:T(8,128)(2,1)S(1)}, u32[]{:S(2)}, u32[]{:S(2)}) %collective-permute-start.8) | collective-permute-done | bytes 262176 | tf_op jit(solution)/shard_map/ppermute | solution.py:222
  54.6 0.1 add_convert_fusion.18
  54.7 3.2 %collective-permute-done.13 = bf16[256,512]{1,0:T(8,128)(2,1)S(1)} collective-permute-done((bf16[256,512]{1,0:T(8,128)(2,1)S(1)}, bf16[256,512]{1,0:T(8,128)(2,1)S(1)}, u32[]{:S(2)}, u32[]{:S(2)}) %collective-permute-start.13) | collective-permute-done | bytes 262176 | tf_op jit(solution)/shard_map/ppermute | solution.py:222
  57.8 0.1 add_convert_fusion.17
  57.9 0.4 collective-permute-done.15
  58.3 0.1 add_convert_fusion.16
  58.4 1.0 %collective-permute-start.16 = (bf16[128,512]{1,0:T(8,128)(2,1)S(1)}, bf16[128,512]{1,0:T(8,128)(2,1)S(1)}, u32[]{:S(2)}, u32[]{:S(2)}) collective-permute-start(bf16[128,512]{1,0:T(8,128)(2,1)S(1)} %get-tuple-element.83), channel_id=1, source_target_pairs={{0,8},{1,9},{2,10},{3,11},{4,12},{5,13},{6,14},{7,15},{8,0},{9,1},... | collective-permute-start | bytes 393224 | tf_op jit(solution)/shard_map/ppermute | solution.py:222
  59.4 2.4 %collective-permute-start.14 = (bf16[128,512]{1,0:T(8,128)(2,1)S(1)}, bf16[128,512]{1,0:T(8,128)(2,1)S(1)}, u32[]{:S(2)}, u32[]{:S(2)}) collective-permute-start(bf16[128,512]{1,0:T(8,128)(2,1)S(1)} %get-tuple-element.85), channel_id=1, source_target_pairs={{0,4},{1,5},{2,6},{3,7},{4,0},{5,1},{6,2},{7,3},{8,12},{9,13},{10,... | collective-permute-start | bytes 393224 | tf_op jit(solution)/shard_map/ppermute | solution.py:222
  61.9 0.1 collective-permute-start.12
  61.9 0.0 collective-permute-done.17.refs_0_
  62.0 0.0 copy-start.5
  62.0 0.0 copy-start.9
  62.0 0.0 copy-start.10
  62.0 1.2 %node_update.2 = (bf16[64,512]{1,0:T(8,128)(2,1)S(1)}, bf16[64,512]{1,0:T(8,128)(2,1)S(1)}, bf16[128,512]{1,0:T(8,128)(2,1)S(1)}) custom-call(s32[1,4]{1,0:T(1,128)S(1)} %collective-permute-done.5.mate_list_ref, s32[1,4]{1,0:T(1,128)S(1)} %collective-permute-done.6.other_list_ref, bf16[128,512]{1,0:T(8,128)(2,1)S(1)} %collective-permute-done.17.refs_0_, ...), custom_call_target="tpu_custom_call" | custom-call | tf_op jit(solution)/shard_map/node_update/pallas_call | solution.py:289
  63.2 0.1 collective-permute-start.18
  63.3 2.4 %collective-permute-start.19 = (bf16[64,512]{1,0:T(8,128)(2,1)S(1)}, bf16[64,512]{1,0:T(8,128)(2,1)S(1)}, u32[]{:S(2)}, u32[]{:S(2)}) collective-permute-start(bf16[64,512]{1,0:T(8,128)(2,1)S(1)} %get-tuple-element.57), channel_id=1, source_target_pairs={{0,15},{1,2},{2,1},{3,4},{4,3},{5,6},{6,5},{7,8},{8,7},{9,10},{10,... | collective-permute-start | bytes 196616 | tf_op jit(solution)/shard_map/ppermute | solution.py:425
  65.6 3.6 %collective-permute-done.16.refs_2_ = bf16[128,512]{1,0:T(8,128)(2,1)S(1)} collective-permute-done((bf16[128,512]{1,0:T(8,128)(2,1)S(1)}, bf16[128,512]{1,0:T(8,128)(2,1)S(1)}, u32[]{:S(2)}, u32[]{:S(2)}) %collective-permute-start.16) | collective-permute-done | bytes 131104 | tf_op jit(solution)/shard_map/ppermute | solution.py:222
  69.3 0.8 collective-permute-done.19.refs_1_
  70.0 0.0 collective-permute-done.14.refs_1_
  70.1 0.6 collective-permute-done.12.refs_0_
  70.7 2.2 %node_update.3 = (bf16[192,512]{1,0:T(8,128)(2,1)S(1)}, bf16[192,512]{1,0:T(8,128)(2,1)S(1)}, bf16[512,512]{1,0:T(8,128)(2,1)}, bf16[512,512]{1,0:T(8,128)(2,1)S(1)}) custom-call(s32[1,4]{1,0:T(1,128)S(1)} %collective-permute-done.5.mate_list_ref, s32[1,4]{1,0:T(1,128)S(1)} %collective-permute-done.6.other_list_ref, ...), custom_call_target="tpu_custom_call" | custom-call | tf_op jit(solution)/shard_map/node_update/pallas_call | solution.py:289
  72.9 0.0 collective-permute-start.20
  72.9 3.5 %collective-permute-start.21 = (bf16[192,512]{1,0:T(8,128)(2,1)S(1)}, bf16[192,512]{1,0:T(8,128)(2,1)S(1)}, u32[]{:S(2)}, u32[]{:S(2)}) collective-permute-start(bf16[192,512]{1,0:T(8,128)(2,1)S(1)} %get-tuple-element.65), channel_id=1, source_target_pairs={{0,15},{1,2},{2,1},{3,4},{4,3},{5,6},{6,5},{7,8},{8,7},{9,10},{10,... | collective-permute-start | bytes 589832 | tf_op jit(solution)/shard_map/ppermute | solution.py:435
  76.5 1.1 %mesh_operator.1.operator_ref = bf16[512,1024]{1,0:T(8,128)(2,1)S(1)} custom-call(s32[12]{0:T(128)S(1)} %copy-done.9, s32[12]{0:T(128)S(1)} %copy-done.10, bf16[12,128,128]{2,1,0:T(8,128)(2,1)S(1)} %copy-done.5), custom_call_target="tpu_custom_call" | custom-call | tf_op jit(solution)/shard_map/mesh_operator/pallas_call | solution.py:320
  77.6 0.0 collective-permute-done.20.refs_2_
  77.6 3.2 %collective-permute-done.21.refs_3_ = bf16[192,512]{1,0:T(8,128)(2,1)S(1)} collective-permute-done((bf16[192,512]{1,0:T(8,128)(2,1)S(1)}, bf16[192,512]{1,0:T(8,128)(2,1)S(1)}, u32[]{:S(2)}, u32[]{:S(2)}) %collective-permute-start.21) | collective-permute-done | bytes 196640 | tf_op jit(solution)/shard_map/ppermute | solution.py:435
  80.8 2.4 %process.1 = bf16[512,512]{1,0:T(8,128)(2,1)} custom-call(bf16[512,1024]{1,0:T(8,128)(2,1)S(1)} %mesh_operator.1.operator_ref, bf16[512,512]{1,0:T(8,128)(2,1)S(1)} %get-tuple-element.61.own_ref, bf16[64,512]{1,0:T(8,128)(2,1)S(1)} %collective-permute-done.18.refs_0_, bf16[64,512]{1,0:T(8,128)(2,1)S(1)} %collective-permute-done.19.refs_1_, ...), custom_call_target="tpu_custom_call" | custom-call | tf_op jit(solution)/shard_map/process/pallas_call | solution.py:341
  (29 shorter events, 0.1 us)
Async XLA Ops:
  0.6 2.0 %copy-start.13 = (s32[64]{0:T(128)S(1)}, s32[64]{0:T(128)}, u32[]{:S(2)}) copy-start(s32[64]{0:T(128)} %param.25) | copy-start | bytes 772
  0.6 2.0 %copy-start.12 = (s32[64]{0:T(128)S(1)}, s32[64]{0:T(128)}, u32[]{:S(2)}) copy-start(s32[64]{0:T(128)} %param.26) | copy-start | bytes 772
  0.7 2.0 %copy-start.11 = (s32[64]{0:T(128)S(1)}, s32[64]{0:T(128)}, u32[]{:S(2)}) copy-start(s32[64]{0:T(128)} %param.27) | copy-start | bytes 772
  0.7 2.1 %copy-start.2 = (bf16[227,2048]{1,0:T(8,128)(2,1)S(1)}, bf16[227,2048]{1,0:T(8,128)(2,1)}, u32[]{:S(2)}) copy-start(bf16[227,2048]{1,0:T(8,128)(2,1)} %inputs_ref.1) | copy-start | bytes 2789380
  2.7 8.3 %copy-start.14 = (s32[1,4]{1,0:T(1,128)S(1)}, s32[1,4]{1,0:T(1,128)}, u32[]{:S(2)}) copy-start(s32[1,4]{1,0:T(1,128)} %param.31) | copy-start | bytes 52
  10.0 2.7 %collective-permute-start.1 = (bf16[1024,512]{1,0:T(8,128)(2,1)S(1)}, bf16[1024,512]{1,0:T(8,128)(2,1)S(1)}, u32[]{:S(2)}, u32[]{:S(2)}) collective-permute-start(bf16[1024,512]{1,0:T(8,128)(2,1)S(1)} %get-tuple-element.35), channel_id=1, source_target_pairs={{0,1},{1,0},{2,3},{3,2},{4,5},{5,4},{6,7},{7,6},{8,9},{9,8},{10,11... | collective-permute-start | bytes 3145736 | tf_op jit(solution)/shard_map/ppermute | solution.py:222
  10.3 8.5 %collective-permute-start = (bf16[1024,512]{1,0:T(8,128)(2,1)S(1)}, bf16[1024,512]{1,0:T(8,128)(2,1)S(1)}, u32[]{:S(2)}, u32[]{:S(2)}) collective-permute-start(bf16[1024,512]{1,0:T(8,128)(2,1)S(1)} %get-tuple-element.34), channel_id=1, source_target_pairs={{0,1},{1,0},{2,3},{3,2},{4,5},{5,4},{6,7},{7,6},{8,9},{9,8},{10,11... | collective-permute-start | bytes 3145736 | tf_op jit(solution)/shard_map/ppermute | solution.py:222
  10.5 8.6 %collective-permute-start.4 = (bf16[1024,512]{1,0:T(8,128)(2,1)S(1)}, bf16[1024,512]{1,0:T(8,128)(2,1)S(1)}, u32[]{:S(2)}, u32[]{:S(2)}) collective-permute-start(bf16[1024,512]{1,0:T(8,128)(2,1)S(1)} %get-tuple-element.40), channel_id=1, source_target_pairs={{0,1},{1,0},{2,3},{3,2},{4,5},{5,4},{6,7},{7,6},{8,9},{9,8},{10,11... | collective-permute-start | bytes 3145736 | tf_op jit(solution)/shard_map/ppermute | solution.py:222
  10.8 9.5 %collective-permute-start.3 = (bf16[1024,512]{1,0:T(8,128)(2,1)S(1)}, bf16[1024,512]{1,0:T(8,128)(2,1)S(1)}, u32[]{:S(2)}, u32[]{:S(2)}) collective-permute-start(bf16[1024,512]{1,0:T(8,128)(2,1)S(1)} %get-tuple-element.39), channel_id=1, source_target_pairs={{0,1},{1,0},{2,3},{3,2},{4,5},{5,4},{6,7},{7,6},{8,9},{9,8},{10,11... | collective-permute-start | bytes 3145736 | tf_op jit(solution)/shard_map/ppermute | solution.py:222
  11.0 11.4 %collective-permute-start.5 = (s32[1,4]{1,0:T(1,128)S(1)}, s32[1,4]{1,0:T(1,128)S(1)}, u32[]{:S(2)}, u32[]{:S(2)}) collective-permute-start(s32[1,4]{1,0:T(1,128)S(1)} %copy-done.14), channel_id=1, source_target_pairs={{0,1},{1,0},{2,3},{3,2},{4,5},{5,4},{6,7},{7,6},{8,9},{9,8},{10,11... | collective-permute-start | bytes 56 | tf_op jit(solution)/shard_map/ppermute | solution.py:411
  12.7 10.3 %collective-permute-start.6 = (s32[1,4]{1,0:T(1,128)S(1)}, s32[1,4]{1,0:T(1,128)S(1)}, u32[]{:S(2)}, u32[]{:S(2)}) collective-permute-start(s32[1,4]{1,0:T(1,128)S(1)} %copy-done.14), channel_id=1, source_target_pairs={{0,15},{1,2},{2,1},{3,4},{4,3},{5,6},{6,5},{7,8},{8,7},{9,10},{10,... | collective-permute-start | bytes 56 | tf_op jit(solution)/shard_map/ppermute | solution.py:411
  18.8 27.0 %collective-permute-start.11 = (bf16[512,512]{1,0:T(8,128)(2,1)S(1)}, bf16[512,512]{1,0:T(8,128)(2,1)S(1)}, u32[]{:S(2)}, u32[]{:S(2)}) collective-permute-start(bf16[512,512]{1,0:T(8,128)(2,1)S(1)} %get-tuple-element.67), channel_id=1, source_target_pairs={{0,8},{1,9},{2,10},{3,11},{4,12},{5,13},{6,14},{7,15},{8,0},{9,1},... | collective-permute-start | bytes 1572872 | tf_op jit(solution)/shard_map/ppermute | solution.py:222
  19.2 14.9 %collective-permute-start.2 = (bf16[512,512]{1,0:T(8,128)(2,1)S(1)}, bf16[512,512]{1,0:T(8,128)(2,1)S(1)}, u32[]{:S(2)}, u32[]{:S(2)}) collective-permute-start(bf16[512,512]{1,0:T(8,128)(2,1)S(1)} %get-tuple-element.71), channel_id=1, source_target_pairs={{0,2},{1,3},{2,0},{3,1},{4,6},{5,7},{6,4},{7,5},{8,10},{9,11},{10,... | collective-permute-start | bytes 1572872 | tf_op jit(solution)/shard_map/ppermute | solution.py:222
  20.2 24.9 %collective-permute-start.7 = (bf16[512,512]{1,0:T(8,128)(2,1)S(1)}, bf16[512,512]{1,0:T(8,128)(2,1)S(1)}, u32[]{:S(2)}, u32[]{:S(2)}) collective-permute-start(bf16[512,512]{1,0:T(8,128)(2,1)S(1)} %get-tuple-element.73), channel_id=1, source_target_pairs={{0,4},{1,5},{2,6},{3,7},{4,0},{5,1},{6,2},{7,3},{8,12},{9,13},{10,... | collective-permute-start | bytes 1572872 | tf_op jit(solution)/shard_map/ppermute | solution.py:222
  22.4 25.2 %collective-permute-start.10 = (bf16[512,512]{1,0:T(8,128)(2,1)S(1)}, bf16[512,512]{1,0:T(8,128)(2,1)S(1)}, u32[]{:S(2)}, u32[]{:S(2)}) collective-permute-start(bf16[512,512]{1,0:T(8,128)(2,1)S(1)} %get-tuple-element.69), channel_id=1, source_target_pairs={{0,2},{1,3},{2,0},{3,1},{4,6},{5,7},{6,4},{7,5},{8,10},{9,11},{10,... | collective-permute-start | bytes 1572872 | tf_op jit(solution)/shard_map/ppermute | solution.py:222
  34.2 16.5 %collective-permute-start.9 = (bf16[256,512]{1,0:T(8,128)(2,1)S(1)}, bf16[256,512]{1,0:T(8,128)(2,1)S(1)}, u32[]{:S(2)}, u32[]{:S(2)}) collective-permute-start(bf16[256,512]{1,0:T(8,128)(2,1)S(1)} %get-tuple-element.79), channel_id=1, source_target_pairs={{0,4},{1,5},{2,6},{3,7},{4,0},{5,1},{6,2},{7,3},{8,12},{9,13},{10,... | collective-permute-start | bytes 786440 | tf_op jit(solution)/shard_map/ppermute | solution.py:222
  45.3 9.3 %collective-permute-start.8 = (bf16[256,512]{1,0:T(8,128)(2,1)S(1)}, bf16[256,512]{1,0:T(8,128)(2,1)S(1)}, u32[]{:S(2)}, u32[]{:S(2)}) collective-permute-start(bf16[256,512]{1,0:T(8,128)(2,1)S(1)} %get-tuple-element.80), channel_id=1, source_target_pairs={{0,2},{1,3},{2,0},{3,1},{4,6},{5,7},{6,4},{7,5},{8,10},{9,11},{10,... | collective-permute-start | bytes 786440 | tf_op jit(solution)/shard_map/ppermute | solution.py:222
  45.9 11.9 %collective-permute-start.13 = (bf16[256,512]{1,0:T(8,128)(2,1)S(1)}, bf16[256,512]{1,0:T(8,128)(2,1)S(1)}, u32[]{:S(2)}, u32[]{:S(2)}) collective-permute-start(bf16[256,512]{1,0:T(8,128)(2,1)S(1)} %get-tuple-element.77), channel_id=1, source_target_pairs={{0,2},{1,3},{2,0},{3,1},{4,6},{5,7},{6,4},{7,5},{8,10},{9,11},{10,... | collective-permute-start | bytes 786440 | tf_op jit(solution)/shard_map/ppermute | solution.py:222
  47.8 10.5 %collective-permute-start.15 = (bf16[256,512]{1,0:T(8,128)(2,1)S(1)}, bf16[256,512]{1,0:T(8,128)(2,1)S(1)}, u32[]{:S(2)}, u32[]{:S(2)}) collective-permute-start(bf16[256,512]{1,0:T(8,128)(2,1)S(1)} %get-tuple-element.75), channel_id=1, source_target_pairs={{0,4},{1,5},{2,6},{3,7},{4,0},{5,1},{6,2},{7,3},{8,12},{9,13},{10,... | collective-permute-start | bytes 786440 | tf_op jit(solution)/shard_map/ppermute | solution.py:222
  50.8 11.2 %copy-start = (bf16[512,512]{1,0:T(8,128)(2,1)S(1)}, bf16[512,512]{1,0:T(8,128)(2,1)}, u32[]{:S(2)}) copy-start(bf16[512,512]{1,0:T(8,128)(2,1)} %refs_7_.1) | copy-start | bytes 1572868
  50.8 11.2 %copy-start.1 = (bf16[512,512]{1,0:T(8,128)(2,1)S(1)}, bf16[512,512]{1,0:T(8,128)(2,1)}, u32[]{:S(2)}) copy-start(bf16[512,512]{1,0:T(8,128)(2,1)} %refs_8_.1) | copy-start | bytes 1572868
  50.8 11.2 %copy-start.6 = (f32[512]{0:T(512)S(1)}, f32[512]{0:T(512)}, u32[]{:S(2)}) copy-start(f32[512]{0:T(512)} %param.30) | copy-start | bytes 6148
  50.8 11.2 %copy-start.7 = (f32[512]{0:T(512)S(1)}, f32[512]{0:T(512)}, u32[]{:S(2)}) copy-start(f32[512]{0:T(512)} %param.23) | copy-start | bytes 6148
  50.9 11.1 %collective-permute-start.17 = (bf16[128,512]{1,0:T(8,128)(2,1)S(1)}, bf16[128,512]{1,0:T(8,128)(2,1)S(1)}, u32[]{:S(2)}, u32[]{:S(2)}) collective-permute-start(bf16[128,512]{1,0:T(8,128)(2,1)S(1)} %get-tuple-element.89), channel_id=1, source_target_pairs={{0,8},{1,9},{2,10},{3,11},{4,12},{5,13},{6,14},{7,15},{8,0},{9,1},... | collective-permute-start | bytes 393224 | tf_op jit(solution)/shard_map/ppermute | solution.py:222
  58.4 10.9 %collective-permute-start.16 = (bf16[128,512]{1,0:T(8,128)(2,1)S(1)}, bf16[128,512]{1,0:T(8,128)(2,1)S(1)}, u32[]{:S(2)}, u32[]{:S(2)}) collective-permute-start(bf16[128,512]{1,0:T(8,128)(2,1)S(1)} %get-tuple-element.83), channel_id=1, source_target_pairs={{0,8},{1,9},{2,10},{3,11},{4,12},{5,13},{6,14},{7,15},{8,0},{9,1},... | collective-permute-start | bytes 393224 | tf_op jit(solution)/shard_map/ppermute | solution.py:222
  59.4 10.6 %collective-permute-start.14 = (bf16[128,512]{1,0:T(8,128)(2,1)S(1)}, bf16[128,512]{1,0:T(8,128)(2,1)S(1)}, u32[]{:S(2)}, u32[]{:S(2)}) collective-permute-start(bf16[128,512]{1,0:T(8,128)(2,1)S(1)} %get-tuple-element.85), channel_id=1, source_target_pairs={{0,4},{1,5},{2,6},{3,7},{4,0},{5,1},{6,2},{7,3},{8,12},{9,13},{10,... | collective-permute-start | bytes 393224 | tf_op jit(solution)/shard_map/ppermute | solution.py:222
  61.9 8.8 %collective-permute-start.12 = (bf16[128,512]{1,0:T(8,128)(2,1)S(1)}, bf16[128,512]{1,0:T(8,128)(2,1)S(1)}, u32[]{:S(2)}, u32[]{:S(2)}) collective-permute-start(bf16[128,512]{1,0:T(8,128)(2,1)S(1)} %get-tuple-element.87), channel_id=1, source_target_pairs={{0,8},{1,9},{2,10},{3,11},{4,12},{5,13},{6,14},{7,15},{8,0},{9,1},... | collective-permute-start | bytes 393224 | tf_op jit(solution)/shard_map/ppermute | solution.py:222
  62.0 14.5 %copy-start.5 = (bf16[12,128,128]{2,1,0:T(8,128)(2,1)S(1)}, bf16[12,128,128]{2,1,0:T(8,128)(2,1)}, u32[]{:S(2)}) copy-start(bf16[12,128,128]{2,1,0:T(8,128)(2,1)} %values_ref.1) | copy-start | bytes 1179652
  62.0 14.5 %copy-start.9 = (s32[12]{0:T(128)S(1)}, s32[12]{0:T(128)}, u32[]{:S(2)}) copy-start(s32[12]{0:T(128)} %dst_ref.1) | copy-start | bytes 148
  62.0 14.5 %copy-start.10 = (s32[12]{0:T(128)S(1)}, s32[12]{0:T(128)}, u32[]{:S(2)}) copy-start(s32[12]{0:T(128)} %src_ref.1) | copy-start | bytes 148
  63.2 6.1 %collective-permute-start.18 = (bf16[64,512]{1,0:T(8,128)(2,1)S(1)}, bf16[64,512]{1,0:T(8,128)(2,1)S(1)}, u32[]{:S(2)}, u32[]{:S(2)}) collective-permute-start(bf16[64,512]{1,0:T(8,128)(2,1)S(1)} %get-tuple-element.56), channel_id=1, source_target_pairs={{0,1},{1,0},{2,3},{3,2},{4,5},{5,4},{6,7},{7,6},{8,9},{9,8},{10,11... | collective-permute-start | bytes 196616 | tf_op jit(solution)/shard_map/ppermute | solution.py:425
  63.3 6.8 %collective-permute-start.19 = (bf16[64,512]{1,0:T(8,128)(2,1)S(1)}, bf16[64,512]{1,0:T(8,128)(2,1)S(1)}, u32[]{:S(2)}, u32[]{:S(2)}) collective-permute-start(bf16[64,512]{1,0:T(8,128)(2,1)S(1)} %get-tuple-element.57), channel_id=1, source_target_pairs={{0,15},{1,2},{2,1},{3,4},{4,3},{5,6},{6,5},{7,8},{8,7},{9,10},{10,... | collective-permute-start | bytes 196616 | tf_op jit(solution)/shard_map/ppermute | solution.py:425
  70.7 10.2 %copy-start.3 = (bf16[512,512]{1,0:T(8,128)(2,1)S(1)}, bf16[512,512]{1,0:T(8,128)(2,1)}, u32[]{:S(2)}) copy-start(bf16[512,512]{1,0:T(8,128)(2,1)} %refs_4_.1) | copy-start | bytes 1572868
  70.7 10.2 %copy-start.4 = (bf16[512,512]{1,0:T(8,128)(2,1)S(1)}, bf16[512,512]{1,0:T(8,128)(2,1)}, u32[]{:S(2)}) copy-start(bf16[512,512]{1,0:T(8,128)(2,1)} %refs_5_.1) | copy-start | bytes 1572868
  70.7 10.2 %copy-start.8 = (f32[512]{0:T(512)S(1)}, f32[512]{0:T(512)}, u32[]{:S(2)}) copy-start(f32[512]{0:T(512)} %param.37) | copy-start | bytes 6148
  72.9 4.7 %collective-permute-start.20 = (bf16[192,512]{1,0:T(8,128)(2,1)S(1)}, bf16[192,512]{1,0:T(8,128)(2,1)S(1)}, u32[]{:S(2)}, u32[]{:S(2)}) collective-permute-start(bf16[192,512]{1,0:T(8,128)(2,1)S(1)} %get-tuple-element.64), channel_id=1, source_target_pairs={{0,1},{1,0},{2,3},{3,2},{4,5},{5,4},{6,7},{7,6},{8,9},{9,8},{10,11... | collective-permute-start | bytes 589832 | tf_op jit(solution)/shard_map/ppermute | solution.py:435
  72.9 7.9 %collective-permute-start.21 = (bf16[192,512]{1,0:T(8,128)(2,1)S(1)}, bf16[192,512]{1,0:T(8,128)(2,1)S(1)}, u32[]{:S(2)}, u32[]{:S(2)}) collective-permute-start(bf16[192,512]{1,0:T(8,128)(2,1)S(1)} %get-tuple-element.65), channel_id=1, source_target_pairs={{0,15},{1,2},{2,1},{3,4},{4,3},{5,6},{6,5},{7,8},{8,7},{9,10},{10,... | collective-permute-start | bytes 589832 | tf_op jit(solution)/shard_map/ppermute | solution.py:435

commit v7 on v6

--- a/solution.py
+++ b/solution.py
@@ -13,7 +13,7 @@
 TURNS = (2, 0, 1, 3, 0, 1, 2, 3, 0, 1, 2, 3)
 EARLY = 1
 LISTS_BY = 4
-TILE = 1024
+TILE = 2048
 UNROLL = 2
 VMEM_BYTES = 24 * 1024 * 1024
 GRID_VMEM_BYTES = 43 * 1024 * 1024

time: 83.6 us -> 83.8 us (level)
    ppermute x16, starting transfers between devices: 12.6 us -> 15.2 us  [exchange(): lax.ppermute(cells, 'space', [(i, i ^ 1 << bit) for i in range(count)])]
    ppermute x1, starting transfers between devices: 5.75 us -> 4.1 us  [shards(): lax.ppermute(recv_blocks, 'space', others)]
  transfers between devices with their start and end apart: 22 -> 22, of which waited for: 11 -> 10; matrix products, arithmetic and copies ran while one was open for 3% -> 2% of each run, Pallas kernels for 3% -> 3%
where the time goes in v7:
time: 83.8 us; the launch traced here: 84 us
  waiting for transfers between devices  39.8 us (47%)
  starting transfers between devices  25.2 us (30%)
  Pallas kernels  13.8 us (16%)
  other arithmetic  3.39 us (4%)
  between operations  1.64 us (2%)
    ppermute x16, waiting for transfers between devices, exchange(): lax.ppermute(cells, 'space', [(i, i ^ 1 << bit) for i in range(count)])  35.7 us
    ppermute x16, starting transfers between devices, exchange(): lax.ppermute(cells, 'space', [(i, i ^ 1 << bit) for i in range(count)])  15.2 us
    pallas_call x1, Pallas kernels, slab_sums(): pl.pallas_call(functools.partial(grid_kernel, held, capacity, orders, cut...  6.92 us
    ppermute x2, starting transfers between devices, shards(): lax.ppermute(to_other, 'space', others)  5.39 us
    ppermute x2, waiting for transfers between devices, shards(): lax.ppermute(to_other, 'space', others)  4.14 us
    ppermute x1, starting transfers between devices, shards(): lax.ppermute(recv_blocks, 'space', others)  4.1 us
    pallas_call x2, Pallas kernels, encode(): pl.pallas_call(functools.partial(node_kernel, held, len(summands), len(ea...  3.44 us
    pallas_call x1, Pallas kernels, process(): pl.pallas_call(process_kernel, in_specs=[VMEM] * (5 + len(halos)), out_sp...  2.37 us
  transfers between devices with their start and end apart: 22, of which 10 were waited for; matrix products, arithmetic and copies ran while one was open for 2% of the time, Pallas kernels for 3%

profile of v7, /device:TPU:0, one launch (start us, length us, event | category | flops | bytes accessed | tf_op | source)
XLA Modules:
  0.0 84.0 jit_solution(1235221181703659399)
XLA Ops:
  1.4 1.2 %pad_maximum_fusion.weights_ref = bf16[739,512]{1,0:T(8,128)(2,1)S(1)} fusion(bf16[227,512]{1,0:T(8,128)(2,1)} %param.21, bf16[512,512]{1,0:T(8,128)(2,1)} %param.22), kind=kLoop, calls=%fused_computation.8 | loop fusion | flops 1513472 | bytes 1513472 | tf_op jit(solution)/shard_map/concatenate | solution.py:215
  2.7 0.1 pad_add_fusion.table_ref
  2.7 6.9 %grid_to_mesh.1 = (bf16[1024,512]{1,0:T(8,128)(2,1)S(1)}, bf16[1024,512]{1,0:T(8,128)(2,1)S(1)}, bf16[1024,512]{1,0:T(8,128)(2,1)S(1)}, bf16[1024,512]{1,0:T(8,1...) custom-call(s32[193]{0:T(256)S(1)} %pad_add_fusion.table_ref, ...), custom_call_target="tpu_custom_call" | custom-call | tf_op jit(solution)/shard_map/grid_to_mesh/pallas_call | solution.py:196
  9.7 2.1 %collective-permute-start.1 = (bf16[1024,512]{1,0:T(8,128)(2,1)S(1)}, bf16[1024,512]{1,0:T(8,128)(2,1)S(1)}, u32[]{:S(2)}, u32[]{:S(2)}) collective-permute-start(bf16[1024,512]{1,0:T(8,128)(2,1)S(1)} %get-tuple-element.35), channel_id=1, source_target_pairs={{0,1},{1,0},{2,3},{3,2},{4,5},{5,4},{6,7},{7,6},{8,9},{9,8},{10,11... | collective-permute-start | bytes 3145736 | tf_op jit(solution)/shard_map/ppermute | solution.py:222
  11.7 0.1 collective-permute-start
  11.8 0.4 collective-permute-start.4
  12.3 0.1 collective-permute-start.3
  12.3 0.4 collective-permute-start.5
  12.8 1.3 %collective-permute-done.1 = bf16[1024,512]{1,0:T(8,128)(2,1)S(1)} collective-permute-done((bf16[1024,512]{1,0:T(8,128)(2,1)S(1)}, bf16[1024,512]{1,0:T(8,128)(2,1)S(1)}, u32[]{:S(2)}, u32[]{:S(2)}) %collective-permute-start.1) | collective-permute-done | bytes 1048608 | tf_op jit(solution)/shard_map/ppermute | solution.py:222
  14.0 4.1 %collective-permute-start.6 = (s32[1,4]{1,0:T(1,128)S(1)}, s32[1,4]{1,0:T(1,128)S(1)}, u32[]{:S(2)}, u32[]{:S(2)}) collective-permute-start(s32[1,4]{1,0:T(1,128)S(1)} %copy-done.14), channel_id=1, source_target_pairs={{0,15},{1,2},{2,1},{3,4},{4,3},{5,6},{6,5},{7,8},{8,7},{9,10},{10,... | collective-permute-start | bytes 56 | tf_op jit(solution)/shard_map/ppermute | solution.py:411
  18.1 0.3 add_convert_fusion.1
  18.5 0.0 collective-permute-done
  18.5 0.1 collective-permute-start.11
  18.5 0.3 add_convert_fusion.3
  18.9 0.0 collective-permute-done.4
  18.9 2.0 %collective-permute-start.2 = (bf16[512,512]{1,0:T(8,128)(2,1)S(1)}, bf16[512,512]{1,0:T(8,128)(2,1)S(1)}, u32[]{:S(2)}, u32[]{:S(2)}) collective-permute-start(bf16[512,512]{1,0:T(8,128)(2,1)S(1)} %get-tuple-element.71), channel_id=1, source_target_pairs={{0,2},{1,3},{2,0},{3,1},{4,6},{5,7},{6,4},{7,5},{8,10},{9,11},{10,... | collective-permute-start | bytes 1572872 | tf_op jit(solution)/shard_map/ppermute | solution.py:222
  20.9 0.3 add_convert_fusion.2
  21.2 0.0 collective-permute-done.3
  21.2 0.8 collective-permute-start.7
  22.0 0.3 add_convert_fusion
  22.3 0.0 collective-permute-done.5.mate_list_ref
  22.3 1.5 %collective-permute-start.10 = (bf16[512,512]{1,0:T(8,128)(2,1)S(1)}, bf16[512,512]{1,0:T(8,128)(2,1)S(1)}, u32[]{:S(2)}, u32[]{:S(2)}) collective-permute-start(bf16[512,512]{1,0:T(8,128)(2,1)S(1)} %get-tuple-element.69), channel_id=1, source_target_pairs={{0,2},{1,3},{2,0},{3,1},{4,6},{5,7},{6,4},{7,5},{8,10},{9,11},{10,... | collective-permute-start | bytes 1572872 | tf_op jit(solution)/shard_map/ppermute | solution.py:222
  23.8 0.0 collective-permute-done.6.other_list_ref
  23.8 9.9 %collective-permute-done.2 = bf16[512,512]{1,0:T(8,128)(2,1)S(1)} collective-permute-done((bf16[512,512]{1,0:T(8,128)(2,1)S(1)}, bf16[512,512]{1,0:T(8,128)(2,1)S(1)}, u32[]{:S(2)}, u32[]{:S(2)}) %collective-permute-start.2) | collective-permute-done | bytes 524320 | tf_op jit(solution)/shard_map/ppermute | solution.py:222
  33.7 0.1 add_convert_fusion.11
  33.9 2.1 %collective-permute-start.9 = (bf16[256,512]{1,0:T(8,128)(2,1)S(1)}, bf16[256,512]{1,0:T(8,128)(2,1)S(1)}, u32[]{:S(2)}, u32[]{:S(2)}) collective-permute-start(bf16[256,512]{1,0:T(8,128)(2,1)S(1)} %get-tuple-element.79), channel_id=1, source_target_pairs={{0,4},{1,5},{2,6},{3,7},{4,0},{5,1},{6,2},{7,3},{8,12},{9,13},{10,... | collective-permute-start | bytes 786440 | tf_op jit(solution)/shard_map/ppermute | solution.py:222
  36.0 10.5 %collective-permute-done.7 = bf16[512,512]{1,0:T(8,128)(2,1)S(1)} collective-permute-done((bf16[512,512]{1,0:T(8,128)(2,1)S(1)}, bf16[512,512]{1,0:T(8,128)(2,1)S(1)}, u32[]{:S(2)}, u32[]{:S(2)}) %collective-permute-start.7) | collective-permute-done | bytes 524320 | tf_op jit(solution)/shard_map/ppermute | solution.py:222
  46.5 0.1 add_convert_fusion.14
  46.7 0.8 collective-permute-start.8
  47.5 0.0 collective-permute-done.11
  47.5 0.1 add_convert_fusion.9
  47.6 1.4 %collective-permute-start.13 = (bf16[256,512]{1,0:T(8,128)(2,1)S(1)}, bf16[256,512]{1,0:T(8,128)(2,1)S(1)}, u32[]{:S(2)}, u32[]{:S(2)}) collective-permute-start(bf16[256,512]{1,0:T(8,128)(2,1)S(1)} %get-tuple-element.77), channel_id=1, source_target_pairs={{0,2},{1,3},{2,0},{3,1},{4,6},{5,7},{6,4},{7,5},{8,10},{9,11},{10,... | collective-permute-start | bytes 786440 | tf_op jit(solution)/shard_map/ppermute | solution.py:222
  49.0 0.0 collective-permute-done.10
  49.0 0.1 add_convert_fusion.8
  49.1 0.1 collective-permute-start.15
  49.2 2.9 %collective-permute-done.9 = bf16[256,512]{1,0:T(8,128)(2,1)S(1)} collective-permute-done((bf16[256,512]{1,0:T(8,128)(2,1)S(1)}, bf16[256,512]{1,0:T(8,128)(2,1)S(1)}, u32[]{:S(2)}, u32[]{:S(2)}) %collective-permute-start.9) | collective-permute-done | bytes 262176 | tf_op jit(solution)/shard_map/ppermute | solution.py:222
  52.2 0.1 add_convert_fusion.19
  52.2 0.2 collective-permute-start.17
  52.5 3.4 %collective-permute-done.8 = bf16[256,512]{1,0:T(8,128)(2,1)S(1)} collective-permute-done((bf16[256,512]{1,0:T(8,128)(2,1)S(1)}, bf16[256,512]{1,0:T(8,128)(2,1)S(1)}, u32[]{:S(2)}, u32[]{:S(2)}) %collective-permute-start.8) | collective-permute-done | bytes 262176 | tf_op jit(solution)/shard_map/ppermute | solution.py:222
  55.9 0.1 add_convert_fusion.18
  56.0 2.7 %collective-permute-done.13 = bf16[256,512]{1,0:T(8,128)(2,1)S(1)} collective-permute-done((bf16[256,512]{1,0:T(8,128)(2,1)S(1)}, bf16[256,512]{1,0:T(8,128)(2,1)S(1)}, u32[]{:S(2)}, u32[]{:S(2)}) %collective-permute-start.13) | collective-permute-done | bytes 262176 | tf_op jit(solution)/shard_map/ppermute | solution.py:222
  58.7 0.1 add_convert_fusion.17
  58.8 0.0 collective-permute-done.15
  58.8 0.1 add_convert_fusion.16
  58.8 0.6 collective-permute-start.16
  59.5 3.0 %collective-permute-start.14 = (bf16[128,512]{1,0:T(8,128)(2,1)S(1)}, bf16[128,512]{1,0:T(8,128)(2,1)S(1)}, u32[]{:S(2)}, u32[]{:S(2)}) collective-permute-start(bf16[128,512]{1,0:T(8,128)(2,1)S(1)} %get-tuple-element.85), channel_id=1, source_target_pairs={{0,4},{1,5},{2,6},{3,7},{4,0},{5,1},{6,2},{7,3},{8,12},{9,13},{10,... | collective-permute-start | bytes 393224 | tf_op jit(solution)/shard_map/ppermute | solution.py:222
  62.4 0.1 collective-permute-start.12
  62.5 0.0 collective-permute-done.17.refs_0_
  62.6 0.0 copy-start.5
  62.6 0.0 copy-start.9
  62.6 0.0 copy-start.10
  62.6 1.2 %node_update.2 = (bf16[64,512]{1,0:T(8,128)(2,1)S(1)}, bf16[64,512]{1,0:T(8,128)(2,1)S(1)}, bf16[128,512]{1,0:T(8,128)(2,1)S(1)}) custom-call(s32[1,4]{1,0:T(1,128)S(1)} %collective-permute-done.5.mate_list_ref, s32[1,4]{1,0:T(1,128)S(1)} %collective-permute-done.6.other_list_ref, bf16[128,512]{1,0:T(8,128)(2,1)S(1)} %collective-permute-done.17.refs_0_, ...), custom_call_target="tpu_custom_call" | custom-call | tf_op jit(solution)/shard_map/node_update/pallas_call | solution.py:289
  63.8 0.1 collective-permute-start.18
  63.8 2.1 %collective-permute-start.19 = (bf16[64,512]{1,0:T(8,128)(2,1)S(1)}, bf16[64,512]{1,0:T(8,128)(2,1)S(1)}, u32[]{:S(2)}, u32[]{:S(2)}) collective-permute-start(bf16[64,512]{1,0:T(8,128)(2,1)S(1)} %get-tuple-element.57), channel_id=1, source_target_pairs={{0,15},{1,2},{2,1},{3,4},{4,3},{5,6},{6,5},{7,8},{8,7},{9,10},{10,... | collective-permute-start | bytes 196616 | tf_op jit(solution)/shard_map/ppermute | solution.py:425
  65.9 4.1 %collective-permute-done.16.refs_2_ = bf16[128,512]{1,0:T(8,128)(2,1)S(1)} collective-permute-done((bf16[128,512]{1,0:T(8,128)(2,1)S(1)}, bf16[128,512]{1,0:T(8,128)(2,1)S(1)}, u32[]{:S(2)}, u32[]{:S(2)}) %collective-permute-start.16) | collective-permute-done | bytes 131104 | tf_op jit(solution)/shard_map/ppermute | solution.py:222
  70.1 0.0 collective-permute-done.18.refs_0_
  70.1 0.7 collective-permute-done.19.refs_1_
  70.7 0.7 collective-permute-done.12.refs_0_
  71.5 2.3 %node_update.3 = (bf16[192,512]{1,0:T(8,128)(2,1)S(1)}, bf16[192,512]{1,0:T(8,128)(2,1)S(1)}, bf16[512,512]{1,0:T(8,128)(2,1)}, bf16[512,512]{1,0:T(8,128)(2,1)S(1)}) custom-call(s32[1,4]{1,0:T(1,128)S(1)} %collective-permute-done.5.mate_list_ref, s32[1,4]{1,0:T(1,128)S(1)} %collective-permute-done.6.other_list_ref, ...), custom_call_target="tpu_custom_call" | custom-call | tf_op jit(solution)/shard_map/node_update/pallas_call | solution.py:289
  73.7 3.3 %collective-permute-start.21 = (bf16[192,512]{1,0:T(8,128)(2,1)S(1)}, bf16[192,512]{1,0:T(8,128)(2,1)S(1)}, u32[]{:S(2)}, u32[]{:S(2)}) collective-permute-start(bf16[192,512]{1,0:T(8,128)(2,1)S(1)} %get-tuple-element.65), channel_id=1, source_target_pairs={{0,15},{1,2},{2,1},{3,4},{4,3},{5,6},{6,5},{7,8},{8,7},{9,10},{10,... | collective-permute-start | bytes 589832 | tf_op jit(solution)/shard_map/ppermute | solution.py:435
  77.0 1.1 %mesh_operator.1.operator_ref = bf16[512,1024]{1,0:T(8,128)(2,1)S(1)} custom-call(s32[12]{0:T(128)S(1)} %copy-done.9, s32[12]{0:T(128)S(1)} %copy-done.10, bf16[12,128,128]{2,1,0:T(8,128)(2,1)S(1)} %copy-done.5), custom_call_target="tpu_custom_call" | custom-call | tf_op jit(solution)/shard_map/mesh_operator/pallas_call | solution.py:320
  78.2 0.0 collective-permute-done.20.refs_2_
  78.2 3.5 %collective-permute-done.21.refs_3_ = bf16[192,512]{1,0:T(8,128)(2,1)S(1)} collective-permute-done((bf16[192,512]{1,0:T(8,128)(2,1)S(1)}, bf16[192,512]{1,0:T(8,128)(2,1)S(1)}, u32[]{:S(2)}, u32[]{:S(2)}) %collective-permute-start.21) | collective-permute-done | bytes 196640 | tf_op jit(solution)/shard_map/ppermute | solution.py:435
  81.6 2.4 %process.1 = bf16[512,512]{1,0:T(8,128)(2,1)} custom-call(bf16[512,1024]{1,0:T(8,128)(2,1)S(1)} %mesh_operator.1.operator_ref, bf16[512,512]{1,0:T(8,128)(2,1)S(1)} %get-tuple-element.61.own_ref, bf16[64,512]{1,0:T(8,128)(2,1)S(1)} %collective-permute-done.18.refs_0_, bf16[64,512]{1,0:T(8,128)(2,1)S(1)} %collective-permute-done.19.refs_1_, ...), custom_call_target="tpu_custom_call" | custom-call | tf_op jit(solution)/shard_map/process/pallas_call | solution.py:341
  (29 shorter events, 0.1 us)
Async XLA Ops:
  0.6 2.0 %copy-start.13 = (s32[64]{0:T(128)S(1)}, s32[64]{0:T(128)}, u32[]{:S(2)}) copy-start(s32[64]{0:T(128)} %param.25) | copy-start | bytes 772
  0.6 2.0 %copy-start.12 = (s32[64]{0:T(128)S(1)}, s32[64]{0:T(128)}, u32[]{:S(2)}) copy-start(s32[64]{0:T(128)} %param.26) | copy-start | bytes 772
  0.7 2.0 %copy-start.11 = (s32[64]{0:T(128)S(1)}, s32[64]{0:T(128)}, u32[]{:S(2)}) copy-start(s32[64]{0:T(128)} %param.27) | copy-start | bytes 772
  0.7 2.1 %copy-start.2 = (bf16[227,2048]{1,0:T(8,128)(2,1)S(1)}, bf16[227,2048]{1,0:T(8,128)(2,1)}, u32[]{:S(2)}) copy-start(bf16[227,2048]{1,0:T(8,128)(2,1)} %inputs_ref.1) | copy-start | bytes 2789380
  2.7 9.6 %copy-start.14 = (s32[1,4]{1,0:T(1,128)S(1)}, s32[1,4]{1,0:T(1,128)}, u32[]{:S(2)}) copy-start(s32[1,4]{1,0:T(1,128)} %param.31) | copy-start | bytes 52
  9.7 4.4 %collective-permute-start.1 = (bf16[1024,512]{1,0:T(8,128)(2,1)S(1)}, bf16[1024,512]{1,0:T(8,128)(2,1)S(1)}, u32[]{:S(2)}, u32[]{:S(2)}) collective-permute-start(bf16[1024,512]{1,0:T(8,128)(2,1)S(1)} %get-tuple-element.35), channel_id=1, source_target_pairs={{0,1},{1,0},{2,3},{3,2},{4,5},{5,4},{6,7},{7,6},{8,9},{9,8},{10,11... | collective-permute-start | bytes 3145736 | tf_op jit(solution)/shard_map/ppermute | solution.py:222
  11.7 6.7 %collective-permute-start = (bf16[1024,512]{1,0:T(8,128)(2,1)S(1)}, bf16[1024,512]{1,0:T(8,128)(2,1)S(1)}, u32[]{:S(2)}, u32[]{:S(2)}) collective-permute-start(bf16[1024,512]{1,0:T(8,128)(2,1)S(1)} %get-tuple-element.34), channel_id=1, source_target_pairs={{0,1},{1,0},{2,3},{3,2},{4,5},{5,4},{6,7},{7,6},{8,9},{9,8},{10,11... | collective-permute-start | bytes 3145736 | tf_op jit(solution)/shard_map/ppermute | solution.py:222
  11.8 7.0 %collective-permute-start.4 = (bf16[1024,512]{1,0:T(8,128)(2,1)S(1)}, bf16[1024,512]{1,0:T(8,128)(2,1)S(1)}, u32[]{:S(2)}, u32[]{:S(2)}) collective-permute-start(bf16[1024,512]{1,0:T(8,128)(2,1)S(1)} %get-tuple-element.40), channel_id=1, source_target_pairs={{0,1},{1,0},{2,3},{3,2},{4,5},{5,4},{6,7},{7,6},{8,9},{9,8},{10,11... | collective-permute-start | bytes 3145736 | tf_op jit(solution)/shard_map/ppermute | solution.py:222
  12.3 8.9 %collective-permute-start.3 = (bf16[1024,512]{1,0:T(8,128)(2,1)S(1)}, bf16[1024,512]{1,0:T(8,128)(2,1)S(1)}, u32[]{:S(2)}, u32[]{:S(2)}) collective-permute-start(bf16[1024,512]{1,0:T(8,128)(2,1)S(1)} %get-tuple-element.39), channel_id=1, source_target_pairs={{0,1},{1,0},{2,3},{3,2},{4,5},{5,4},{6,7},{7,6},{8,9},{9,8},{10,11... | collective-permute-start | bytes 3145736 | tf_op jit(solution)/shard_map/ppermute | solution.py:222
  12.3 10.0 %collective-permute-start.5 = (s32[1,4]{1,0:T(1,128)S(1)}, s32[1,4]{1,0:T(1,128)S(1)}, u32[]{:S(2)}, u32[]{:S(2)}) collective-permute-start(s32[1,4]{1,0:T(1,128)S(1)} %copy-done.14), channel_id=1, source_target_pairs={{0,1},{1,0},{2,3},{3,2},{4,5},{5,4},{6,7},{7,6},{8,9},{9,8},{10,11... | collective-permute-start | bytes 56 | tf_op jit(solution)/shard_map/ppermute | solution.py:411
  14.0 9.8 %collective-permute-start.6 = (s32[1,4]{1,0:T(1,128)S(1)}, s32[1,4]{1,0:T(1,128)S(1)}, u32[]{:S(2)}, u32[]{:S(2)}) collective-permute-start(s32[1,4]{1,0:T(1,128)S(1)} %copy-done.14), channel_id=1, source_target_pairs={{0,15},{1,2},{2,1},{3,4},{4,3},{5,6},{6,5},{7,8},{8,7},{9,10},{10,... | collective-permute-start | bytes 56 | tf_op jit(solution)/shard_map/ppermute | solution.py:411
  18.5 29.0 %collective-permute-start.11 = (bf16[512,512]{1,0:T(8,128)(2,1)S(1)}, bf16[512,512]{1,0:T(8,128)(2,1)S(1)}, u32[]{:S(2)}, u32[]{:S(2)}) collective-permute-start(bf16[512,512]{1,0:T(8,128)(2,1)S(1)} %get-tuple-element.67), channel_id=1, source_target_pairs={{0,8},{1,9},{2,10},{3,11},{4,12},{5,13},{6,14},{7,15},{8,0},{9,1},... | collective-permute-start | bytes 1572872 | tf_op jit(solution)/shard_map/ppermute | solution.py:222
  18.9 14.9 %collective-permute-start.2 = (bf16[512,512]{1,0:T(8,128)(2,1)S(1)}, bf16[512,512]{1,0:T(8,128)(2,1)S(1)}, u32[]{:S(2)}, u32[]{:S(2)}) collective-permute-start(bf16[512,512]{1,0:T(8,128)(2,1)S(1)} %get-tuple-element.71), channel_id=1, source_target_pairs={{0,2},{1,3},{2,0},{3,1},{4,6},{5,7},{6,4},{7,5},{8,10},{9,11},{10,... | collective-permute-start | bytes 1572872 | tf_op jit(solution)/shard_map/ppermute | solution.py:222
  21.2 25.3 %collective-permute-start.7 = (bf16[512,512]{1,0:T(8,128)(2,1)S(1)}, bf16[512,512]{1,0:T(8,128)(2,1)S(1)}, u32[]{:S(2)}, u32[]{:S(2)}) collective-permute-start(bf16[512,512]{1,0:T(8,128)(2,1)S(1)} %get-tuple-element.73), channel_id=1, source_target_pairs={{0,4},{1,5},{2,6},{3,7},{4,0},{5,1},{6,2},{7,3},{8,12},{9,13},{10,... | collective-permute-start | bytes 1572872 | tf_op jit(solution)/shard_map/ppermute | solution.py:222
  22.3 26.7 %collective-permute-start.10 = (bf16[512,512]{1,0:T(8,128)(2,1)S(1)}, bf16[512,512]{1,0:T(8,128)(2,1)S(1)}, u32[]{:S(2)}, u32[]{:S(2)}) collective-permute-start(bf16[512,512]{1,0:T(8,128)(2,1)S(1)} %get-tuple-element.69), channel_id=1, source_target_pairs={{0,2},{1,3},{2,0},{3,1},{4,6},{5,7},{6,4},{7,5},{8,10},{9,11},{10,... | collective-permute-start | bytes 1572872 | tf_op jit(solution)/shard_map/ppermute | solution.py:222
  33.9 18.3 %collective-permute-start.9 = (bf16[256,512]{1,0:T(8,128)(2,1)S(1)}, bf16[256,512]{1,0:T(8,128)(2,1)S(1)}, u32[]{:S(2)}, u32[]{:S(2)}) collective-permute-start(bf16[256,512]{1,0:T(8,128)(2,1)S(1)} %get-tuple-element.79), channel_id=1, source_target_pairs={{0,4},{1,5},{2,6},{3,7},{4,0},{5,1},{6,2},{7,3},{8,12},{9,13},{10,... | collective-permute-start | bytes 786440 | tf_op jit(solution)/shard_map/ppermute | solution.py:222
  46.7 9.2 %collective-permute-start.8 = (bf16[256,512]{1,0:T(8,128)(2,1)S(1)}, bf16[256,512]{1,0:T(8,128)(2,1)S(1)}, u32[]{:S(2)}, u32[]{:S(2)}) collective-permute-start(bf16[256,512]{1,0:T(8,128)(2,1)S(1)} %get-tuple-element.80), channel_id=1, source_target_pairs={{0,2},{1,3},{2,0},{3,1},{4,6},{5,7},{6,4},{7,5},{8,10},{9,11},{10,... | collective-permute-start | bytes 786440 | tf_op jit(solution)/shard_map/ppermute | solution.py:222
  47.6 11.1 %collective-permute-start.13 = (bf16[256,512]{1,0:T(8,128)(2,1)S(1)}, bf16[256,512]{1,0:T(8,128)(2,1)S(1)}, u32[]{:S(2)}, u32[]{:S(2)}) collective-permute-start(bf16[256,512]{1,0:T(8,128)(2,1)S(1)} %get-tuple-element.77), channel_id=1, source_target_pairs={{0,2},{1,3},{2,0},{3,1},{4,6},{5,7},{6,4},{7,5},{8,10},{9,11},{10,... | collective-permute-start | bytes 786440 | tf_op jit(solution)/shard_map/ppermute | solution.py:222
  49.1 9.6 %collective-permute-start.15 = (bf16[256,512]{1,0:T(8,128)(2,1)S(1)}, bf16[256,512]{1,0:T(8,128)(2,1)S(1)}, u32[]{:S(2)}, u32[]{:S(2)}) collective-permute-start(bf16[256,512]{1,0:T(8,128)(2,1)S(1)} %get-tuple-element.75), channel_id=1, source_target_pairs={{0,4},{1,5},{2,6},{3,7},{4,0},{5,1},{6,2},{7,3},{8,12},{9,13},{10,... | collective-permute-start | bytes 786440 | tf_op jit(solution)/shard_map/ppermute | solution.py:222
  52.2 10.4 %copy-start = (bf16[512,512]{1,0:T(8,128)(2,1)S(1)}, bf16[512,512]{1,0:T(8,128)(2,1)}, u32[]{:S(2)}) copy-start(bf16[512,512]{1,0:T(8,128)(2,1)} %refs_7_.1) | copy-start | bytes 1572868
  52.2 10.4 %copy-start.1 = (bf16[512,512]{1,0:T(8,128)(2,1)S(1)}, bf16[512,512]{1,0:T(8,128)(2,1)}, u32[]{:S(2)}) copy-start(bf16[512,512]{1,0:T(8,128)(2,1)} %refs_8_.1) | copy-start | bytes 1572868
  52.2 10.4 %copy-start.6 = (f32[512]{0:T(512)S(1)}, f32[512]{0:T(512)}, u32[]{:S(2)}) copy-start(f32[512]{0:T(512)} %param.30) | copy-start | bytes 6148
  52.2 10.4 %copy-start.7 = (f32[512]{0:T(512)S(1)}, f32[512]{0:T(512)}, u32[]{:S(2)}) copy-start(f32[512]{0:T(512)} %param.23) | copy-start | bytes 6148
  52.2 10.3 %collective-permute-start.17 = (bf16[128,512]{1,0:T(8,128)(2,1)S(1)}, bf16[128,512]{1,0:T(8,128)(2,1)S(1)}, u32[]{:S(2)}, u32[]{:S(2)}) collective-permute-start(bf16[128,512]{1,0:T(8,128)(2,1)S(1)} %get-tuple-element.89), channel_id=1, source_target_pairs={{0,8},{1,9},{2,10},{3,11},{4,12},{5,13},{6,14},{7,15},{8,0},{9,1},... | collective-permute-start | bytes 393224 | tf_op jit(solution)/shard_map/ppermute | solution.py:222
  58.8 11.2 %collective-permute-start.16 = (bf16[128,512]{1,0:T(8,128)(2,1)S(1)}, bf16[128,512]{1,0:T(8,128)(2,1)S(1)}, u32[]{:S(2)}, u32[]{:S(2)}) collective-permute-start(bf16[128,512]{1,0:T(8,128)(2,1)S(1)} %get-tuple-element.83), channel_id=1, source_target_pairs={{0,8},{1,9},{2,10},{3,11},{4,12},{5,13},{6,14},{7,15},{8,0},{9,1},... | collective-permute-start | bytes 393224 | tf_op jit(solution)/shard_map/ppermute | solution.py:222
  59.5 11.3 %collective-permute-start.14 = (bf16[128,512]{1,0:T(8,128)(2,1)S(1)}, bf16[128,512]{1,0:T(8,128)(2,1)S(1)}, u32[]{:S(2)}, u32[]{:S(2)}) collective-permute-start(bf16[128,512]{1,0:T(8,128)(2,1)S(1)} %get-tuple-element.85), channel_id=1, source_target_pairs={{0,4},{1,5},{2,6},{3,7},{4,0},{5,1},{6,2},{7,3},{8,12},{9,13},{10,... | collective-permute-start | bytes 393224 | tf_op jit(solution)/shard_map/ppermute | solution.py:222
  62.4 9.0 %collective-permute-start.12 = (bf16[128,512]{1,0:T(8,128)(2,1)S(1)}, bf16[128,512]{1,0:T(8,128)(2,1)S(1)}, u32[]{:S(2)}, u32[]{:S(2)}) collective-permute-start(bf16[128,512]{1,0:T(8,128)(2,1)S(1)} %get-tuple-element.87), channel_id=1, source_target_pairs={{0,8},{1,9},{2,10},{3,11},{4,12},{5,13},{6,14},{7,15},{8,0},{9,1},... | collective-permute-start | bytes 393224 | tf_op jit(solution)/shard_map/ppermute | solution.py:222
  62.6 14.5 %copy-start.5 = (bf16[12,128,128]{2,1,0:T(8,128)(2,1)S(1)}, bf16[12,128,128]{2,1,0:T(8,128)(2,1)}, u32[]{:S(2)}) copy-start(bf16[12,128,128]{2,1,0:T(8,128)(2,1)} %values_ref.1) | copy-start | bytes 1179652
  62.6 14.5 %copy-start.9 = (s32[12]{0:T(128)S(1)}, s32[12]{0:T(128)}, u32[]{:S(2)}) copy-start(s32[12]{0:T(128)} %dst_ref.1) | copy-start | bytes 148
  62.6 14.5 %copy-start.10 = (s32[12]{0:T(128)S(1)}, s32[12]{0:T(128)}, u32[]{:S(2)}) copy-start(s32[12]{0:T(128)} %src_ref.1) | copy-start | bytes 148
  63.8 6.3 %collective-permute-start.18 = (bf16[64,512]{1,0:T(8,128)(2,1)S(1)}, bf16[64,512]{1,0:T(8,128)(2,1)S(1)}, u32[]{:S(2)}, u32[]{:S(2)}) collective-permute-start(bf16[64,512]{1,0:T(8,128)(2,1)S(1)} %get-tuple-element.56), channel_id=1, source_target_pairs={{0,1},{1,0},{2,3},{3,2},{4,5},{5,4},{6,7},{7,6},{8,9},{9,8},{10,11... | collective-permute-start | bytes 196616 | tf_op jit(solution)/shard_map/ppermute | solution.py:425
  63.8 6.9 %collective-permute-start.19 = (bf16[64,512]{1,0:T(8,128)(2,1)S(1)}, bf16[64,512]{1,0:T(8,128)(2,1)S(1)}, u32[]{:S(2)}, u32[]{:S(2)}) collective-permute-start(bf16[64,512]{1,0:T(8,128)(2,1)S(1)} %get-tuple-element.57), channel_id=1, source_target_pairs={{0,15},{1,2},{2,1},{3,4},{4,3},{5,6},{6,5},{7,8},{8,7},{9,10},{10,... | collective-permute-start | bytes 196616 | tf_op jit(solution)/shard_map/ppermute | solution.py:425
  71.5 10.2 %copy-start.3 = (bf16[512,512]{1,0:T(8,128)(2,1)S(1)}, bf16[512,512]{1,0:T(8,128)(2,1)}, u32[]{:S(2)}) copy-start(bf16[512,512]{1,0:T(8,128)(2,1)} %refs_4_.1) | copy-start | bytes 1572868
  71.5 10.2 %copy-start.4 = (bf16[512,512]{1,0:T(8,128)(2,1)S(1)}, bf16[512,512]{1,0:T(8,128)(2,1)}, u32[]{:S(2)}) copy-start(bf16[512,512]{1,0:T(8,128)(2,1)} %refs_5_.1) | copy-start | bytes 1572868
  71.5 10.2 %copy-start.8 = (f32[512]{0:T(512)S(1)}, f32[512]{0:T(512)}, u32[]{:S(2)}) copy-start(f32[512]{0:T(512)} %param.37) | copy-start | bytes 6148
  73.7 4.4 %collective-permute-start.20 = (bf16[192,512]{1,0:T(8,128)(2,1)S(1)}, bf16[192,512]{1,0:T(8,128)(2,1)S(1)}, u32[]{:S(2)}, u32[]{:S(2)}) collective-permute-start(bf16[192,512]{1,0:T(8,128)(2,1)S(1)} %get-tuple-element.64), channel_id=1, source_target_pairs={{0,1},{1,0},{2,3},{3,2},{4,5},{5,4},{6,7},{7,6},{8,9},{9,8},{10,11... | collective-permute-start | bytes 589832 | tf_op jit(solution)/shard_map/ppermute | solution.py:435
  73.7 7.9 %collective-permute-start.21 = (bf16[192,512]{1,0:T(8,128)(2,1)S(1)}, bf16[192,512]{1,0:T(8,128)(2,1)S(1)}, u32[]{:S(2)}, u32[]{:S(2)}) collective-permute-start(bf16[192,512]{1,0:T(8,128)(2,1)S(1)} %get-tuple-element.65), channel_id=1, source_target_pairs={{0,15},{1,2},{2,1},{3,4},{4,3},{5,6},{6,5},{7,8},{8,7},{9,10},{10,... | collective-permute-start | bytes 589832 | tf_op jit(solution)/shard_map/ppermute | solution.py:435
